TPU v7x, 32 devices: a whole 2x2x4 slice. The times are simulated.
32 devices in a mesh: gx: 4 (over z), gz: 2 (over x), ta: 4 (over y, core).
Axes of the slice: x: 2, y: 2, z: 4, core: 2. Of those that a mesh axis runs over, the one named last changes fastest.
Arguments:
- rhs: float32 [4, 2, 2, 8, 16, 8, 64], P('gx', None, None, 'gz', 'ta'), may hold values from -20 to 20
- self_coupling: bfloat16 [4, 2, 2, 8, 16, 64, 64], P('gx', None, None, 'gz', 'ta'), may hold values from -0.75 to 0.75
- hopping: bfloat16 [4, 4, 2, 2, 8, 16, 64, 64], P(None, 'gx', None, None, 'gz', 'ta'), may hold values from -0.5 to 0.5
Outputs:
- solution: float32 [4, 2, 2, 8, 16, 8, 64], P('gx', None, None, 'gz', 'ta')
- residual: float32 [4, 2, 2, 8, 16, 8, 64], P('gx', None, None, 'gz', 'ta')
All inputs are finite; a program needn't handle non-finite values.
Results may differ from a plain program's by a relative error of at most 0.0087.
Values may be sent and summed in bfloat16 or wider, within the bound.
No kernel may reach another device: no remote copies, remote signals or barrier semaphores. Data moves between devices by JAX's collectives and lax.ppermute only.
A program may use at most 64 MiB of HBM per device.

v0:
```python
import jax
import jax.numpy as jnp
from jax import lax
from jax.sharding import PartitionSpec as P

MR_STEPS = 2


def passed_along(block, axis, distance):
    devices = range(lax.axis_size(axis))
    route = [((i - distance) % len(devices), i) for i in devices]
    return lax.ppermute(block, axis, route)


def site_product(link_block, field_bf):
    return jnp.einsum(
        "xyztab,xyztrb->xyztra", link_block, field_bf, preferred_element_type=jnp.float32
    )


def site_product_back(link_block, field_bf):
    return jnp.einsum(
        "xyztab,xyztra->xyztrb", link_block, field_bf, preferred_element_type=jnp.float32
    )


def rim(values, along, position):
    return lax.slice_in_dim(values, position, position + 1, axis=along)


def plane_move(rim_face, offset):
    return passed_along(rim_face, "gx", offset)


def depth_move(rim_face, offset):
    return passed_along(rim_face, "gz", offset)


def time_move(rim_face, offset):
    return passed_along(rim_face, "ta", offset)


def neighbour_rim(rim_face, direction, toward, row_len):
    if direction == 0:
        return plane_move(rim_face, -toward * row_len)
    if direction == 1:
        return plane_move(rim_face, -toward)
    if direction == 2:
        return depth_move(rim_face, -toward)
    return time_move(rim_face, -toward)


def local_dot(left, right):
    return jnp.sum(left * right, axis=(0, 1, 2, 3, 5))[:, None]


def mesh_total(partials):
    return lax.psum(partials, ("gx", "gz", "ta"))


def on_device(rhs, self_coupling, hopping):
    source = rhs[0]
    self_links = self_coupling[0]
    hop_links = hopping[:, 0]
    channels = source.shape[5]
    chirality = jnp.where(jnp.arange(channels) < channels // 2, 1.0, -1.0).astype(jnp.bfloat16)
    row_len = min(8, max(2, lax.axis_size("gx") // 8))
    link_rims = []
    for direction in range(4):
        last_index = hop_links.shape[direction + 1] - 1
        link_rims.append(
            neighbour_rim(rim(hop_links[direction], direction, last_index), direction, -1, row_len)
        )

    def apply_operator(vector, reach):
        field_bf = vector.astype(jnp.bfloat16)
        result = 4.0 * vector + site_product(self_links, field_bf)
        flipped = chirality * field_bf
        for direction in range(4):
            link_block = hop_links[direction]
            extent = vector.shape[direction]
            back_term = (chirality * site_product_back(link_block, flipped)).astype(jnp.bfloat16)
            if reach == "local":
                upper_rim = jnp.zeros_like(rim(field_bf, direction, 0))
                lower_rim = jnp.zeros_like(rim(back_term, direction, 0))
            else:
                upper_rim = neighbour_rim(rim(field_bf, direction, 0), direction, 1, row_len)
                below_rim = neighbour_rim(
                    rim(field_bf, direction, extent - 1), direction, -1, row_len
                )
                lower_rim = (
                    chirality * site_product_back(link_rims[direction], chirality * below_rim)
                ).astype(jnp.bfloat16)
            ahead_field = jnp.concatenate(
                [lax.slice_in_dim(field_bf, 1, extent, axis=direction), upper_rim], axis=direction
            )
            behind = jnp.concatenate(
                [lower_rim, lax.slice_in_dim(back_term, 0, extent - 1, axis=direction)],
                axis=direction,
            )
            result = result + site_product(link_block, ahead_field) + behind.astype(jnp.float32)
        return result

    def smoothing(start_field):
        remain = start_field
        update = jnp.zeros_like(start_field)
        for repeat_index in range(MR_STEPS):
            mapped = apply_operator(remain, "local")
            weight = local_dot(mapped, remain) / local_dot(mapped, mapped)
            update = update + weight * remain
            remain = remain - weight * mapped
        return update

    direction_zero = smoothing(source)
    mapped_zero = apply_operator(direction_zero, "global")
    first_sums = mesh_total(
        jnp.stack([local_dot(mapped_zero, source), local_dot(mapped_zero, mapped_zero)])
    )
    alpha_first = first_sums[0] / first_sums[1]
    solution_one = alpha_first * direction_zero
    residual_one = source - alpha_first * mapped_zero
    direction_raw = smoothing(residual_one)
    mapped_raw = apply_operator(direction_raw, "global")
    joint_sums = mesh_total(
        jnp.stack(
            [
                local_dot(mapped_zero, mapped_raw),
                local_dot(mapped_raw, mapped_raw),
                local_dot(mapped_raw, residual_one),
                local_dot(mapped_zero, residual_one),
            ]
        )
    )
    beta_value = joint_sums[0] / first_sums[1]
    direction_one = direction_raw - beta_value * direction_zero
    mapped_one = mapped_raw - beta_value * mapped_zero
    numerator = joint_sums[2] - beta_value * joint_sums[3]
    denominator = (
        joint_sums[1] - 2.0 * beta_value * joint_sums[0] + beta_value * beta_value * first_sums[1]
    )
    alpha_second = numerator / denominator
    solution = solution_one + alpha_second * direction_one
    residual = residual_one - alpha_second * mapped_one
    return (solution[None], residual[None])


def solution(mesh):
    in_specs = (
        P("gx", None, None, "gz", "ta", None, None),
        P("gx", None, None, "gz", "ta", None, None),
        P(None, "gx", None, None, "gz", "ta", None, None),
    )
    out_specs = (
        P("gx", None, None, "gz", "ta", None, None),
        P("gx", None, None, "gz", "ta", None, None),
    )
    return jax.shard_map(
        on_device, mesh=mesh, in_specs=in_specs, out_specs=out_specs, check_vma=False
    )
```

profile of v0, /device:TPU:0, one launch (start us, length us, event | category | flops | bytes accessed | tf_op | source)
XLA Modules:
  0.0 185.4 jit_solution(2299578962263160762)
XLA Ops:
  0.7 2.7 %slice_bitcast_fusion = (bf16[2,2,4,4,64,64]{5,4,3,2,1,0:T(8,128)(2,1)S(1)}, bf16[2,2,4,4,64,64]{5,4,3,2,1,0:T(8,128)(2,1)S(1)}, bf16[2,2,4,4,64,64]{5,4,3,2,1,0:T(8,128)(2,1)S(1)}) fusion(bf16[4,1,2,2,4,4,64,64]{7,6,5,4,3,2,1,0:T(8,128)(2,1)} %param.5), kind=kLoop, calls=%fused_computation.102 | loop fusion | bytes 3145728 | tf_op jit(solution)/shard_map/squeeze | solution.py:80
  3.4 0.5 collective-permute-start.11
  4.4 0.4 fusion.61
  4.8 0.4 fusion.182
  5.1 0.4 fusion.180
  5.5 0.6 convolution_add_fusion.23
  6.3 0.6 fusion.15
  6.9 0.7 fusion.14
  7.6 0.7 fusion.13
  8.3 0.8 multiply_reduce_fusion.11
  10.8 0.6 convolution_add_fusion.22
  11.5 0.6 fusion.11
  12.2 0.7 fusion.10
  12.9 0.7 fusion.9
  13.5 0.8 multiply_reduce_fusion.9
  14.5 2.7 %collective-permute-start.10 = (bf16[2,2,4,1,8,64]{5,4,3,2,1,0:T(8,128)(2,1)S(1)}, bf16[2,2,4,1,8,64]{5,4,3,2,1,0:T(8,128)(2,1)S(1)}, u32[]{:S(2)}, u32[]{:S(2)}) collective-permute-start(bf16[2,2,4,1,8,64]{5,4,3,2,1,0:T(8,128)(2,1)S(1)} %get-tuple-element.39), channel_id=1, source_target_pairs={{3,0},{0,1},{1,2},{2,3},{7,4},{4,5},{5,6},{6,7},{11,8},{8,9},{9,10... | collective-permute-start | bytes 49160 | tf_op jit(solution)/shard_map/ppermute | solution.py:12
  17.2 2.1 %collective-permute-start.8 = (bf16[2,2,1,4,64,64]{5,4,3,2,1,0:T(8,128)(2,1)S(1)}, bf16[2,2,1,4,64,64]{5,4,3,2,1,0:T(8,128)(2,1)S(1)}, u32[]{:S(2)}, u32[]{:S(2)}) collective-permute-start(bf16[2,2,1,4,64,64]{5,4,3,2,1,0:T(8,128)(2,1)S(1)} %slice.362), channel_id=1, source_target_pairs={{4,0},{0,4},{5,1},{1,5},{6,2},{2,6},{7,3},{3,7},{12,8},{8,12},{13,... | collective-permute-start | bytes 393224 | tf_op jit(solution)/shard_map/ppermute | solution.py:12
  21.1 0.6 convolution_add_fusion.21
  21.9 2.1 %collective-permute-start.5 = (bf16[2,1,4,4,64,64]{5,4,3,2,1,0:T(8,128)(2,1)S(1)}, bf16[2,1,4,4,64,64]{5,4,3,2,1,0:T(8,128)(2,1)S(1)}, u32[]{:S(2)}, u32[]{:S(2)}) collective-permute-start(bf16[2,1,4,4,64,64]{5,4,3,2,1,0:T(8,128)(2,1)S(1)} %slice.357), channel_id=1, source_target_pairs={{24,0},{0,8},{8,16},{16,24},{25,1},{1,9},{9,17},{17,25},{26,2},{2,... | collective-permute-start | bytes 786440 | tf_op jit(solution)/shard_map/ppermute | solution.py:12
  23.9 0.6 fusion.116
  24.6 2.1 %collective-permute-done.6 = bf16[2,2,1,4,8,64]{5,4,3,2,1,0:T(8,128)(2,1)S(1)} collective-permute-done((bf16[2,2,1,4,8,64]{5,4,3,2,1,0:T(8,128)(2,1)S(1)}, bf16[2,2,1,4,8,64]{5,4,3,2,1,0:T(8,128)(2,1)S(1)}, u32[]{:S(2)}, u32[]{:S(2)}) %collective-permute-start.6) | collective-permute-done | bytes 16416 | tf_op jit(solution)/shard_map/ppermute | solution.py:12
  26.7 3.6 %collective-permute-start.3 = (bf16[2,1,4,4,8,64]{5,4,3,2,1,0:T(8,128)(2,1)S(1)}, bf16[2,1,4,4,8,64]{5,4,3,2,1,0:T(8,128)(2,1)S(1)}, u32[]{:S(2)}, u32[]{:S(2)}) collective-permute-start(bf16[2,1,4,4,8,64]{5,4,3,2,1,0:T(8,128)(2,1)S(1)} %get-tuple-element.46), channel_id=1, source_target_pairs={{8,0},{16,8},{24,16},{0,24},{9,1},{17,9},{25,17},{1,25},{10,2},{18... | collective-permute-start | bytes 98312 | tf_op jit(solution)/shard_map/ppermute | solution.py:12
  30.3 0.6 fusion.112
  30.9 7.9 %collective-permute-done.3 = bf16[2,1,4,4,8,64]{5,4,3,2,1,0:T(8,128)(2,1)S(1)} collective-permute-done((bf16[2,1,4,4,8,64]{5,4,3,2,1,0:T(8,128)(2,1)S(1)}, bf16[2,1,4,4,8,64]{5,4,3,2,1,0:T(8,128)(2,1)S(1)}, u32[]{:S(2)}, u32[]{:S(2)}) %collective-permute-start.3) | collective-permute-done | bytes 32800 | tf_op jit(solution)/shard_map/ppermute | solution.py:12
  38.9 0.6 collective-permute-start.4
  39.4 0.6 fusion.108
  40.1 1.5 collective-permute-start.7
  41.6 1.7 collective-permute-start.2
  43.4 0.6 collective-permute-done.7
  44.0 1.7 collective-permute-start.1
  45.7 1.3 collective-permute-start
  47.4 24.4 %collective-permute-done.1 = bf16[1,2,4,4,8,64]{5,4,3,2,1,0:T(8,128)(2,1)S(1)} collective-permute-done((bf16[1,2,4,4,8,64]{5,4,3,2,1,0:T(8,128)(2,1)S(1)}, bf16[1,2,4,4,8,64]{5,4,3,2,1,0:T(8,128)(2,1)S(1)}, u32[]{:S(2)}, u32[]{:S(2)}) %collective-permute-start.1) | collective-permute-done | bytes 32800 | tf_op jit(solution)/shard_map/ppermute | solution.py:12
  72.1 1.0 collective-permute-done
  73.0 0.8 fusion.80
  73.9 37.1 %psum.14 = f32[2,8,1]{1,2,0:T(1,128)S(1)} all-reduce(f32[2,8,1]{1,2,0:T(1,128)S(1)} %pad_maximum_fusion.1), channel_id=1, replica_groups=mesh['gx'=4,'gz'=2,'ta'=4] {'gx','gz','ta'}, use_global_device_ids=true, to_apply=%region_6.7 | all-reduce | flops 16 | bytes 128 | tf_op jit(solution)/shard_map/psum | solution.py:58
  111.1 1.7 fusion.157
  112.8 1.6 fusion.52
  114.4 1.6 fusion.161
  116.0 0.4 fusion.159
  116.5 0.6 convolution_add_fusion.19
  117.2 0.6 fusion.7
  117.8 0.7 fusion.6
  118.5 0.7 fusion.5
  119.2 0.8 multiply_reduce_fusion.6
  121.7 0.6 convolution_add_fusion.18
  122.4 0.6 fusion.3
  123.1 0.7 fusion.2
  123.7 0.7 fusion.1
  124.4 0.8 multiply_reduce_fusion.4
  127.1 1.7 collective-permute-start.18
  128.8 2.3 %collective-permute-start.17 = (bf16[2,2,1,4,8,64]{5,4,3,2,1,0:T(8,128)(2,1)S(1)}, bf16[2,2,1,4,8,64]{5,4,3,2,1,0:T(8,128)(2,1)S(1)}, u32[]{:S(2)}, u32[]{:S(2)}) collective-permute-start(bf16[2,2,1,4,8,64]{5,4,3,2,1,0:T(8,128)(2,1)S(1)} %get-tuple-element.33), channel_id=1, source_target_pairs={{4,0},{0,4},{5,1},{1,5},{6,2},{2,6},{7,3},{3,7},{12,8},{8,12},{13,... | collective-permute-start | bytes 49160 | tf_op jit(solution)/shard_map/ppermute | solution.py:12
  131.3 2.9 %collective-permute-start.15 = (bf16[2,1,4,4,8,64]{5,4,3,2,1,0:T(8,128)(2,1)S(1)}, bf16[2,1,4,4,8,64]{5,4,3,2,1,0:T(8,128)(2,1)S(1)}, u32[]{:S(2)}, u32[]{:S(2)}) collective-permute-start(bf16[2,1,4,4,8,64]{5,4,3,2,1,0:T(8,128)(2,1)S(1)} %get-tuple-element.37), channel_id=1, source_target_pairs={{24,0},{0,8},{8,16},{16,24},{25,1},{1,9},{9,17},{17,25},{26,2},{2,... | collective-permute-start | bytes 98312 | tf_op jit(solution)/shard_map/ppermute | solution.py:12
  134.2 0.6 convolution_add_fusion.17
  134.9 1.0 collective-permute-start.14
  135.9 0.6 fusion.131
  136.5 1.5 collective-permute-start.13
  138.0 0.6 fusion.127
  138.7 1.5 collective-permute-start.12
  140.5 0.6 fusion.123
  141.4 0.4 collective-permute-done.13
  142.1 3.1 %collective-permute-done.12 = bf16[1,2,4,4,8,64]{5,4,3,2,1,0:T(8,128)(2,1)S(1)} collective-permute-done((bf16[1,2,4,4,8,64]{5,4,3,2,1,0:T(8,128)(2,1)S(1)}, bf16[1,2,4,4,8,64]{5,4,3,2,1,0:T(8,128)(2,1)S(1)}, u32[]{:S(2)}, u32[]{:S(2)}) %collective-permute-start.12) | collective-permute-done | bytes 32800 | tf_op jit(solution)/shard_map/ppermute | solution.py:12
  145.2 0.8 multiply_reduce_fusion.3
  146.1 38.3 %psum.15 = f32[4,8,1]{1,2,0:T(1,128)S(1)} all-reduce(f32[4,8,1]{1,2,0:T(1,128)S(1)} %pad_maximum_fusion), channel_id=1, replica_groups=mesh['gx'=4,'gz'=2,'ta'=4] {'gx','gz','ta'}, use_global_device_ids=true, to_apply=%region_15.16 | all-reduce | flops 32 | bytes 256 | tf_op jit(solution)/shard_map/psum | solution.py:58
  184.4 1.0 subtract_bitcast_fusion
  (109 shorter events, 10.0 us)
Async XLA Ops:
  0.6 4.9 %copy-start = (bf16[1,2,2,4,4,64,64]{6,5,4,3,2,1,0:T(8,128)(2,1)S(1)}, bf16[1,2,2,4,4,64,64]{6,5,4,3,2,1,0:T(8,128)(2,1)}, u32[]{:S(2)}) copy-start(bf16[1,2,2,4,4,64,64]{6,5,4,3,2,1,0:T(8,128)(2,1)} %param.4) | copy-start | bytes 1572868
  0.6 3.3 %copy-start.1 = (bf16[4,1,2,2,4,4,64,64]{7,6,5,4,3,2,1,0:T(8,128)(2,1)S(1)}, bf16[4,1,2,2,4,4,64,64]{7,6,5,4,3,2,1,0:T(8,128)(2,1)}, u32[]{:S(2)}) copy-start(bf16[4,1,2,2,4,4,64,64]{7,6,5,4,3,2,1,0:T(8,128)(2,1)} %param.5) | copy-start | bytes 6291460
  0.7 3.3 %copy-start.3 = (f32[1,2,2,4,4,8,64]{6,5,4,3,2,1,0:T(8,128)S(1)}, f32[1,2,2,4,4,8,64]{6,5,4,3,2,1,0:T(8,128)}, u32[]{:S(2)}) copy-start(f32[1,2,2,4,4,8,64]{6,5,4,3,2,1,0:T(8,128)} %param.3) | copy-start | bytes 393220
  3.4 38.2 %collective-permute-start.11 = (bf16[2,2,4,1,64,64]{5,4,3,2,1,0:T(8,128)(2,1)S(1)}, bf16[2,2,4,1,64,64]{5,4,3,2,1,0:T(8,128)(2,1)S(1)}, u32[]{:S(2)}, u32[]{:S(2)}) collective-permute-start(bf16[2,2,4,1,64,64]{5,4,3,2,1,0:T(8,128)(2,1)S(1)} %slice.367), channel_id=1, source_target_pairs={{3,0},{0,1},{1,2},{2,3},{7,4},{4,5},{5,6},{6,7},{11,8},{8,9},{9,10... | collective-permute-start | bytes 393224 | tf_op jit(solution)/shard_map/ppermute | solution.py:12
  14.5 25.6 %collective-permute-start.10 = (bf16[2,2,4,1,8,64]{5,4,3,2,1,0:T(8,128)(2,1)S(1)}, bf16[2,2,4,1,8,64]{5,4,3,2,1,0:T(8,128)(2,1)S(1)}, u32[]{:S(2)}, u32[]{:S(2)}) collective-permute-start(bf16[2,2,4,1,8,64]{5,4,3,2,1,0:T(8,128)(2,1)S(1)} %get-tuple-element.39), channel_id=1, source_target_pairs={{3,0},{0,1},{1,2},{2,3},{7,4},{4,5},{5,6},{6,7},{11,8},{8,9},{9,10... | collective-permute-start | bytes 49160 | tf_op jit(solution)/shard_map/ppermute | solution.py:12
  17.2 4.7 %collective-permute-start.9 = (bf16[2,2,4,1,8,64]{5,4,3,2,1,0:T(8,128)(2,1)S(1)}, bf16[2,2,4,1,8,64]{5,4,3,2,1,0:T(8,128)(2,1)S(1)}, u32[]{:S(2)}, u32[]{:S(2)}) collective-permute-start(bf16[2,2,4,1,8,64]{5,4,3,2,1,0:T(8,128)(2,1)S(1)} %get-tuple-element.40), channel_id=1, source_target_pairs={{1,0},{2,1},{3,2},{0,3},{5,4},{6,5},{7,6},{4,7},{9,8},{10,9},{11,1... | collective-permute-start | bytes 49160 | tf_op jit(solution)/shard_map/ppermute | solution.py:12
  17.2 28.5 %collective-permute-start.8 = (bf16[2,2,1,4,64,64]{5,4,3,2,1,0:T(8,128)(2,1)S(1)}, bf16[2,2,1,4,64,64]{5,4,3,2,1,0:T(8,128)(2,1)S(1)}, u32[]{:S(2)}, u32[]{:S(2)}) collective-permute-start(bf16[2,2,1,4,64,64]{5,4,3,2,1,0:T(8,128)(2,1)S(1)} %slice.362), channel_id=1, source_target_pairs={{4,0},{0,4},{5,1},{1,5},{6,2},{2,6},{7,3},{3,7},{12,8},{8,12},{13,... | collective-permute-start | bytes 393224 | tf_op jit(solution)/shard_map/ppermute | solution.py:12
  19.3 7.4 %collective-permute-start.6 = (bf16[2,2,1,4,8,64]{5,4,3,2,1,0:T(8,128)(2,1)S(1)}, bf16[2,2,1,4,8,64]{5,4,3,2,1,0:T(8,128)(2,1)S(1)}, u32[]{:S(2)}, u32[]{:S(2)}) collective-permute-start(bf16[2,2,1,4,8,64]{5,4,3,2,1,0:T(8,128)(2,1)S(1)} %get-tuple-element.42), channel_id=1, source_target_pairs={{4,0},{0,4},{5,1},{1,5},{6,2},{2,6},{7,3},{3,7},{12,8},{8,12},{13,... | collective-permute-start | bytes 49160 | tf_op jit(solution)/shard_map/ppermute | solution.py:12
  21.9 25.3 %collective-permute-start.5 = (bf16[2,1,4,4,64,64]{5,4,3,2,1,0:T(8,128)(2,1)S(1)}, bf16[2,1,4,4,64,64]{5,4,3,2,1,0:T(8,128)(2,1)S(1)}, u32[]{:S(2)}, u32[]{:S(2)}) collective-permute-start(bf16[2,1,4,4,64,64]{5,4,3,2,1,0:T(8,128)(2,1)S(1)} %slice.357), channel_id=1, source_target_pairs={{24,0},{0,8},{8,16},{16,24},{25,1},{1,9},{9,17},{17,25},{26,2},{2,... | collective-permute-start | bytes 786440 | tf_op jit(solution)/shard_map/ppermute | solution.py:12
  26.7 12.2 %collective-permute-start.3 = (bf16[2,1,4,4,8,64]{5,4,3,2,1,0:T(8,128)(2,1)S(1)}, bf16[2,1,4,4,8,64]{5,4,3,2,1,0:T(8,128)(2,1)S(1)}, u32[]{:S(2)}, u32[]{:S(2)}) collective-permute-start(bf16[2,1,4,4,8,64]{5,4,3,2,1,0:T(8,128)(2,1)S(1)} %get-tuple-element.46), channel_id=1, source_target_pairs={{8,0},{16,8},{24,16},{0,24},{9,1},{17,9},{25,17},{1,25},{10,2},{18... | collective-permute-start | bytes 98312 | tf_op jit(solution)/shard_map/ppermute | solution.py:12
  38.9 8.3 %collective-permute-start.4 = (bf16[2,1,4,4,8,64]{5,4,3,2,1,0:T(8,128)(2,1)S(1)}, bf16[2,1,4,4,8,64]{5,4,3,2,1,0:T(8,128)(2,1)S(1)}, u32[]{:S(2)}, u32[]{:S(2)}) collective-permute-start(bf16[2,1,4,4,8,64]{5,4,3,2,1,0:T(8,128)(2,1)S(1)} %get-tuple-element.45), channel_id=1, source_target_pairs={{24,0},{0,8},{8,16},{16,24},{25,1},{1,9},{9,17},{17,25},{26,2},{2,... | collective-permute-start | bytes 98312 | tf_op jit(solution)/shard_map/ppermute | solution.py:12
  40.1 3.9 %collective-permute-start.7 = (bf16[2,2,1,4,8,64]{5,4,3,2,1,0:T(8,128)(2,1)S(1)}, bf16[2,2,1,4,8,64]{5,4,3,2,1,0:T(8,128)(2,1)S(1)}, u32[]{:S(2)}, u32[]{:S(2)}) collective-permute-start(bf16[2,2,1,4,8,64]{5,4,3,2,1,0:T(8,128)(2,1)S(1)} %get-tuple-element.41), channel_id=1, source_target_pairs={{4,0},{0,4},{5,1},{1,5},{6,2},{2,6},{7,3},{3,7},{12,8},{8,12},{13,... | collective-permute-start | bytes 49160 | tf_op jit(solution)/shard_map/ppermute | solution.py:12
  41.6 30.2 %collective-permute-start.2 = (bf16[1,2,4,4,64,64]{5,4,3,2,1,0:T(8,128)(2,1)S(1)}, bf16[1,2,4,4,64,64]{5,4,3,2,1,0:T(8,128)(2,1)S(1)}, u32[]{:S(2)}, u32[]{:S(2)}) collective-permute-start(bf16[1,2,4,4,64,64]{5,4,3,2,1,0:T(8,128)(2,1)S(1)} %slice_bitcast_fusion.3), channel_id=1, source_target_pairs={{16,0},{24,8},{0,16},{8,24},{17,1},{25,9},{1,17},{9,25},{18,2},{26... | collective-permute-start | bytes 786440 | tf_op jit(solution)/shard_map/ppermute | solution.py:12
  44.0 27.8 %collective-permute-start.1 = (bf16[1,2,4,4,8,64]{5,4,3,2,1,0:T(8,128)(2,1)S(1)}, bf16[1,2,4,4,8,64]{5,4,3,2,1,0:T(8,128)(2,1)S(1)}, u32[]{:S(2)}, u32[]{:S(2)}) collective-permute-start(bf16[1,2,4,4,8,64]{5,4,3,2,1,0:T(8,128)(2,1)S(1)} %get-tuple-element.43), channel_id=1, source_target_pairs={{16,0},{24,8},{0,16},{8,24},{17,1},{25,9},{1,17},{9,25},{18,2},{26... | collective-permute-start | bytes 98312 | tf_op jit(solution)/shard_map/ppermute | solution.py:12
  45.7 65.2 %copy-start.4 = (bf16[2,2,1,4,64,64]{5,4,3,2,1,0:T(8,128)(2,1)}, bf16[2,2,1,4,64,64]{5,4,3,2,1,0:T(8,128)(2,1)S(1)}, u32[]{:S(2)}) copy-start(bf16[2,2,1,4,64,64]{5,4,3,2,1,0:T(8,128)(2,1)S(1)} %collective-permute-done.8) | copy-start | bytes 393220
  45.7 27.3 %collective-permute-start = (bf16[1,2,4,4,8,64]{5,4,3,2,1,0:T(8,128)(2,1)S(1)}, bf16[1,2,4,4,8,64]{5,4,3,2,1,0:T(8,128)(2,1)S(1)}, u32[]{:S(2)}, u32[]{:S(2)}) collective-permute-start(bf16[1,2,4,4,8,64]{5,4,3,2,1,0:T(8,128)(2,1)S(1)} %get-tuple-element.44), channel_id=1, source_target_pairs={{16,0},{24,8},{0,16},{8,24},{17,1},{25,9},{1,17},{9,25},{18,2},{26... | collective-permute-start | bytes 98312 | tf_op jit(solution)/shard_map/ppermute | solution.py:12
  110.9 5.1 %copy-start.2 = (bf16[4,1,2,2,4,4,64,64]{7,6,5,4,3,2,1,0:T(8,128)(2,1)S(1)}, bf16[4,1,2,2,4,4,64,64]{7,6,5,4,3,2,1,0:T(8,128)(2,1)}, u32[]{:S(2)}) copy-start(bf16[4,1,2,2,4,4,64,64]{7,6,5,4,3,2,1,0:T(8,128)(2,1)} %param.5) | copy-start | bytes 6291460
  126.6 13.8 %copy-start.5 = (bf16[2,2,1,4,64,64]{5,4,3,2,1,0:T(8,128)(2,1)S(1)}, bf16[2,2,1,4,64,64]{5,4,3,2,1,0:T(8,128)(2,1)}, u32[]{:S(2)}) copy-start(bf16[2,2,1,4,64,64]{5,4,3,2,1,0:T(8,128)(2,1)} %copy-done.4) | copy-start | bytes 393220
  127.0 11.7 %collective-permute-start.19 = (bf16[2,2,4,1,8,64]{5,4,3,2,1,0:T(8,128)(2,1)S(1)}, bf16[2,2,4,1,8,64]{5,4,3,2,1,0:T(8,128)(2,1)S(1)}, u32[]{:S(2)}, u32[]{:S(2)}) collective-permute-start(bf16[2,2,4,1,8,64]{5,4,3,2,1,0:T(8,128)(2,1)S(1)} %get-tuple-element.31), channel_id=1, source_target_pairs={{3,0},{0,1},{1,2},{2,3},{7,4},{4,5},{5,6},{6,7},{11,8},{8,9},{9,10... | collective-permute-start | bytes 49160 | tf_op jit(solution)/shard_map/ppermute | solution.py:12
  127.1 7.8 %collective-permute-start.18 = (bf16[2,2,4,1,8,64]{5,4,3,2,1,0:T(8,128)(2,1)S(1)}, bf16[2,2,4,1,8,64]{5,4,3,2,1,0:T(8,128)(2,1)S(1)}, u32[]{:S(2)}, u32[]{:S(2)}) collective-permute-start(bf16[2,2,4,1,8,64]{5,4,3,2,1,0:T(8,128)(2,1)S(1)} %get-tuple-element.32), channel_id=1, source_target_pairs={{1,0},{2,1},{3,2},{0,3},{5,4},{6,5},{7,6},{4,7},{9,8},{10,9},{11,1... | collective-permute-start | bytes 49160 | tf_op jit(solution)/shard_map/ppermute | solution.py:12
  128.8 11.5 %collective-permute-start.17 = (bf16[2,2,1,4,8,64]{5,4,3,2,1,0:T(8,128)(2,1)S(1)}, bf16[2,2,1,4,8,64]{5,4,3,2,1,0:T(8,128)(2,1)S(1)}, u32[]{:S(2)}, u32[]{:S(2)}) collective-permute-start(bf16[2,2,1,4,8,64]{5,4,3,2,1,0:T(8,128)(2,1)S(1)} %get-tuple-element.33), channel_id=1, source_target_pairs={{4,0},{0,4},{5,1},{1,5},{6,2},{2,6},{7,3},{3,7},{12,8},{8,12},{13,... | collective-permute-start | bytes 49160 | tf_op jit(solution)/shard_map/ppermute | solution.py:12
  131.2 5.4 %collective-permute-start.16 = (bf16[2,2,1,4,8,64]{5,4,3,2,1,0:T(8,128)(2,1)S(1)}, bf16[2,2,1,4,8,64]{5,4,3,2,1,0:T(8,128)(2,1)S(1)}, u32[]{:S(2)}, u32[]{:S(2)}) collective-permute-start(bf16[2,2,1,4,8,64]{5,4,3,2,1,0:T(8,128)(2,1)S(1)} %get-tuple-element.34), channel_id=1, source_target_pairs={{4,0},{0,4},{5,1},{1,5},{6,2},{2,6},{7,3},{3,7},{12,8},{8,12},{13,... | collective-permute-start | bytes 49160 | tf_op jit(solution)/shard_map/ppermute | solution.py:12
  131.3 9.9 %collective-permute-start.15 = (bf16[2,1,4,4,8,64]{5,4,3,2,1,0:T(8,128)(2,1)S(1)}, bf16[2,1,4,4,8,64]{5,4,3,2,1,0:T(8,128)(2,1)S(1)}, u32[]{:S(2)}, u32[]{:S(2)}) collective-permute-start(bf16[2,1,4,4,8,64]{5,4,3,2,1,0:T(8,128)(2,1)S(1)} %get-tuple-element.37), channel_id=1, source_target_pairs={{24,0},{0,8},{8,16},{16,24},{25,1},{1,9},{9,17},{17,25},{26,2},{2,... | collective-permute-start | bytes 98312 | tf_op jit(solution)/shard_map/ppermute | solution.py:12
  134.9 5.6 %collective-permute-start.14 = (bf16[2,1,4,4,8,64]{5,4,3,2,1,0:T(8,128)(2,1)S(1)}, bf16[2,1,4,4,8,64]{5,4,3,2,1,0:T(8,128)(2,1)S(1)}, u32[]{:S(2)}, u32[]{:S(2)}) collective-permute-start(bf16[2,1,4,4,8,64]{5,4,3,2,1,0:T(8,128)(2,1)S(1)} %get-tuple-element.38), channel_id=1, source_target_pairs={{8,0},{16,8},{24,16},{0,24},{9,1},{17,9},{25,17},{1,25},{10,2},{18... | collective-permute-start | bytes 98312 | tf_op jit(solution)/shard_map/ppermute | solution.py:12
  136.5 5.3 %collective-permute-start.13 = (bf16[1,2,4,4,8,64]{5,4,3,2,1,0:T(8,128)(2,1)S(1)}, bf16[1,2,4,4,8,64]{5,4,3,2,1,0:T(8,128)(2,1)S(1)}, u32[]{:S(2)}, u32[]{:S(2)}) collective-permute-start(bf16[1,2,4,4,8,64]{5,4,3,2,1,0:T(8,128)(2,1)S(1)} %get-tuple-element.35), channel_id=1, source_target_pairs={{16,0},{24,8},{0,16},{8,24},{17,1},{25,9},{1,17},{9,25},{18,2},{26... | collective-permute-start | bytes 98312 | tf_op jit(solution)/shard_map/ppermute | solution.py:12
  138.7 6.6 %collective-permute-start.12 = (bf16[1,2,4,4,8,64]{5,4,3,2,1,0:T(8,128)(2,1)S(1)}, bf16[1,2,4,4,8,64]{5,4,3,2,1,0:T(8,128)(2,1)S(1)}, u32[]{:S(2)}, u32[]{:S(2)}) collective-permute-start(bf16[1,2,4,4,8,64]{5,4,3,2,1,0:T(8,128)(2,1)S(1)} %get-tuple-element.36), channel_id=1, source_target_pairs={{16,0},{24,8},{0,16},{8,24},{17,1},{25,9},{1,17},{9,25},{18,2},{26... | collective-permute-start | bytes 98312 | tf_op jit(solution)/shard_map/ppermute | solution.py:12
where the time goes:
time: 186 us; the launch traced here: 185 us
  blocking collectives  75.4 us (41%)
  waiting for transfers between devices  39.6 us (21%)
  matrix products  35.3 us (19%)
  starting transfers between devices  28.8 us (15%)
  local copies, waits for them, and re-layouts  3.02 us (2%)
  other arithmetic  2.15 us (1%)
    psum x2, blocking collectives, mesh_total(): return lax.psum(partials, ('gx', 'gz', 'ta'))  75.4 us
    ppermute x20, waiting for transfers between devices, passed_along(): return lax.ppermute(block, axis, route)  39.6 us
    ppermute x20, starting transfers between devices, passed_along(): return lax.ppermute(block, axis, route)  28.8 us
    dot_general x30, matrix products, site_product(): jnp.einsum('xyztab,xyztrb->xyztra', link_block, field_bf, preferred_eleme...  20.5 us
    dot_general x32, matrix products, site_product_back(): jnp.einsum('xyztab,xyztra->xyztrb', link_block, field_bf, preferred_eleme...  14.8 us
  transfers between devices with their start and end apart: 20, of which 7 were waited for; matrix products, arithmetic and copies ran while one was open for 10% of the time, Pallas kernels for 0%

commit v1 on v0

v1 whole, which is shorter than its diff:
```python
import functools

import jax
import jax.numpy as jnp
from jax import lax
from jax.experimental import pallas as pl
from jax.experimental.pallas import tpu as pltpu
from jax.sharding import PartitionSpec as P

F32 = jnp.float32
BF16 = jnp.bfloat16
NT = (((1,), (1,)), ((), ()))
NN = (((1,), (0,)), ((), ()))
VMEM_BYTES = 24 * 2**20
AXES = ("gx", "gx", "gz", "ta")


class Box:
    def __init__(self, extents):
        self.extents = tuple(extents)
        self.strides = []
        count = 1
        for extent in reversed(self.extents):
            self.strides.insert(0, count)
            count *= extent
        self.count = count

    def coord(self, site, direction):
        return site // self.strides[direction] % self.extents[direction]

    def ahead(self, site, direction):
        last = self.extents[direction] - 1
        return None if self.coord(site, direction) == last else site + self.strides[direction]

    def behind(self, site, direction):
        return None if self.coord(site, direction) == 0 else site - self.strides[direction]

    def rim(self, direction, upper):
        wanted = self.extents[direction] - 1 if upper else 0
        return [s for s in range(self.count) if self.coord(s, direction) == wanted]


def lane_tools(rows, lanes):
    lane = lax.broadcasted_iota(jnp.int32, (rows, lanes), 1)
    low = lane < lanes // 2
    chirality = jnp.where(lane % (lanes // 2) < lanes // 4, 1.0, -1.0).astype(F32)
    return low, chirality


def twice(value):
    return jnp.concatenate([value, value], axis=1)


def local_products(box, field, links, own, back, mapped, low, chirality):
    rows, lanes = field.shape[1:]
    half = lanes // 2
    zero = jnp.zeros((rows, lanes), F32)
    for s in range(box.count):
        ahead = [box.ahead(s, d) for d in range(4)]
        part = [zero if a is None else field[a] for a in ahead]
        here = field[s]
        spread = jnp.concatenate(
            [jnp.where(low, part[0], part[1]), jnp.where(low, part[2], part[3])], axis=1
        ).astype(BF16)
        total = lax.dot_general(here[:, :half].astype(BF16), own[s], NT, preferred_element_type=F32)
        if any(a is not None for a in ahead):
            total = total + lax.dot_general(spread, links[s], NT, preferred_element_type=F32)
        mapped[s] = jnp.concatenate([total, jnp.zeros((rows, half), F32)], axis=1)
        back[s] = lax.dot_general(
            (chirality * here)[:, :half].astype(BF16), links[s], NN, preferred_element_type=F32
        )
    top = zero
    bottom = zero
    for s in range(box.count):
        behind = [box.behind(s, d) for d in range(4)]
        piece = []
        for d in range(4):
            start = d // 2 * lanes
            piece.append(zero if behind[d] is None else back[behind[d], :, start : start + lanes])
        gathered = jnp.where(low, piece[0], piece[1]) + jnp.where(low, piece[2], piece[3])
        gathered = chirality * gathered + mapped[s]
        here = field[s]
        value = 4.0 * here + gathered + pltpu.roll(gathered, half, 1)
        mapped[s] = value
        top = top + value * here
        bottom = bottom + value * value
    return jnp.sum(top, axis=1, keepdims=True) / jnp.sum(bottom, axis=1, keepdims=True)


def smooth(box, flips, field, links, own, outs, scratch):
    update, image, sends = outs
    back_a, back_b, map_a, map_b, second = scratch
    rows, lanes = field.shape[1:]
    half = lanes // 2
    low, chirality = lane_tools(rows, lanes)
    weight_a = local_products(box, field, links, own, back_a, map_a, low, chirality)
    for s in range(box.count):
        second[s] = field[s] - weight_a * map_a[s]
    weight_b = local_products(box, second, links, own, back_b, map_b, low, chirality)
    for s in range(box.count):
        update[s] = weight_a * field[s] + weight_b * second[s]
        image[s] = weight_a * map_a[s] + weight_b * map_b[s]
    for d in range(4):
        flip = flips[d]
        lower = box.rim(d, False)
        upper = box.rim(d, True)
        start = d // 2 * lanes
        for j in range(len(lower) // 4):
            block = []
            for k in (4 * j, 4 * j + 2):
                block.append(jnp.where(low, update[lower[k]], update[lower[k + 1]]))
            sends[d][flip, j] = jnp.concatenate(block, axis=0).astype(BF16)
            block = []
            for k in (4 * j, 4 * j + 2):
                pair = []
                for u in (upper[k], upper[k + 1]):
                    pair.append(
                        weight_a * back_a[u, :, start : start + lanes]
                        + weight_b * back_b[u, :, start : start + lanes]
                    )
                if d % 2 == 0:
                    joined = jnp.where(low, pair[0], pltpu.roll(pair[1], half, 1))
                else:
                    joined = jnp.where(low, pltpu.roll(pair[0], half, 1), pair[1])
                block.append(chirality * joined)
            sends[d][1 - flip, j] = jnp.concatenate(block, axis=0).astype(BF16)


def first_kernel(box, flips, rhs, own, hop, update, image, send0, send1, send2, send3, links, field, *scratch):
    for s in range(box.count):
        links[s] = jnp.concatenate([hop[d, s] for d in range(4)], axis=1)
        field[s] = twice(rhs[s])
    smooth(box, flips, field, links, own, (update, image, (send0, send1, send2, send3)), scratch)


def second_kernel(box, flips, rhs, mapped, sums, links, own, update, image, send0, send1, send2, send3, field, *scratch):
    alpha = sums[:, 0:1] / sums[:, 1:2]
    for s in range(box.count):
        field[s] = twice(rhs[s]) - alpha * mapped[s]
    smooth(box, flips, field, links, own, (update, image, (send0, send1, send2, send3)), scratch)


def joined_halo(box, flips, image, links, came, mapped, low):
    rows, lanes = image.shape[1:]
    half = lanes // 2

    places = [{s: k for k, s in enumerate(box.rim(d, True))} for d in range(4)]
    lows = [{s: k for k, s in enumerate(box.rim(d, False))} for d in range(4)]

    def read(d, which, k):
        slot = flips[d] if which == 0 else 1 - flips[d]
        tile = came[d][slot, k // 4].astype(F32)
        tile = tile[(k // 2 % 2) * rows : (k // 2 % 2 + 1) * rows]
        if which == 0 and k % 2 != d % 2:
            tile = pltpu.roll(tile, half, 1)
        return tile

    zero = jnp.zeros((rows, lanes), F32)
    for s in range(box.count):
        part = [read(d, 0, places[d][s]) if s in places[d] else None for d in range(4)]
        extra = zero
        if any(p is not None for p in part):
            part = [zero if p is None else p for p in part]
            spread = jnp.concatenate(
                [jnp.where(low, part[0], part[1]), jnp.where(low, part[2], part[3])], axis=1
            ).astype(BF16)
            total = lax.dot_general(spread, links[s], NT, preferred_element_type=F32)
            extra = jnp.concatenate([total, jnp.zeros((rows, half), F32)], axis=1)
        for d in range(4):
            if s in lows[d]:
                k = lows[d][s]
                tile = read(d, 1, k)
                extra = extra + (jnp.where(low, tile, 0.0) if k % 2 == 0 else jnp.where(low, 0.0, tile))
        mapped[s] = image[s] + extra + pltpu.roll(extra, half, 1)


def packed_sums(values, rows, lanes):
    lane = lax.broadcasted_iota(jnp.int32, (rows, lanes), 1)
    out = jnp.zeros((rows, lanes), F32)
    for k, value in enumerate(values):
        out = jnp.where(lane == k, jnp.sum(value, axis=1, keepdims=True), out)
    return out


def third_kernel(box, flips, rhs, image, links, came0, came1, came2, came3, mapped, sums):
    rows, lanes = image.shape[1:]
    low, _ = lane_tools(rows, lanes)
    joined_halo(box, flips, image, links, (came0, came1, came2, came3), mapped, low)
    zero = jnp.zeros((rows, lanes), F32)
    top = zero
    bottom = zero
    for s in range(box.count):
        value = mapped[s]
        top = top + value * twice(rhs[s])
        bottom = bottom + value * value
    sums[...] = packed_sums((top, bottom), rows, lanes)


def fourth_kernel(box, flips, rhs, first, before, image, links, came0, came1, came2, came3, mapped, sums):
    rows, lanes = image.shape[1:]
    low, _ = lane_tools(rows, lanes)
    joined_halo(box, flips, image, links, (came0, came1, came2, came3), mapped, low)
    alpha = before[:, 0:1] / before[:, 1:2]
    total = [jnp.zeros((rows, lanes), F32) for _ in range(4)]
    for s in range(box.count):
        old = first[s]
        value = mapped[s]
        remain = twice(rhs[s]) - alpha * old
        for k, product in enumerate((old * value, value * value, value * remain, old * remain)):
            total[k] = total[k] + product
    sums[...] = packed_sums(total, rows, lanes)


def last_kernel(box, rhs, update_a, map_a, update_b, map_b, sums_a, sums_b, solution_out, residual_out):
    half = update_a.shape[2] // 2
    square = sums_a[:, 1:2]
    alpha = sums_a[:, 0:1] / square
    beta = sums_b[:, 0:1] / square
    top = sums_b[:, 2:3] - beta * sums_b[:, 3:4]
    bottom = sums_b[:, 1:2] - 2.0 * beta * sums_b[:, 0:1] + beta * beta * square
    step = top / bottom
    for s in range(box.count):
        old = update_a[s][:, :half]
        solution_out[s] = alpha * old + step * (update_b[s][:, :half] - beta * old)
        old = map_a[s][:, :half]
        residual_out[s] = rhs[s] - alpha * old - step * (map_b[s][:, :half] - beta * old)


def call(body, outs, scratch, ins, flips=None):
    vmem = pl.BlockSpec(memory_space=pltpu.VMEM)
    smem = pl.BlockSpec(memory_space=pltpu.SMEM)
    specs = [vmem] * len(ins)
    if flips is not None:
        specs.insert(0, smem)
        ins = (flips, *ins)
    return pl.pallas_call(
        body,
        out_shape=outs,
        in_specs=specs,
        out_specs=[vmem] * len(outs),
        scratch_shapes=scratch,
        compiler_params=pltpu.CompilerParams(vmem_limit_bytes=VMEM_BYTES),
    )(*ins)


def plan(direction):
    axis = AXES[direction]
    size = lax.axis_size(axis)
    step = min(8, max(2, lax.axis_size("gx") // 8)) if direction == 0 else 1
    if 2 * step % size == 0:
        return axis, size, step, "both"
    if step == 1 and size % 2 == 0:
        return axis, size, step, "pairs"
    return axis, size, step, "shift"


def exchange(sends):
    came = [None] * 4
    for d in range(4):
        axis, size, step, kind = plan(d)
        ring = range(size)
        if kind == "both":
            came[d] = lax.ppermute(sends[d], axis, [(i, (i + step) % size) for i in ring])
        elif kind == "pairs":
            even = lax.ppermute(sends[d][0], axis, [(i, i ^ 1) for i in ring])
            odd = lax.ppermute(sends[d][1], axis, [(i, (i + 1 if i % 2 else i - 1) % size) for i in ring])
            came[d] = jnp.stack([even, odd])
        else:
            field = lax.ppermute(sends[d][0], axis, [(i, (i - step) % size) for i in ring])
            back = lax.ppermute(sends[d][1], axis, [(i, (i + step) % size) for i in ring])
            came[d] = jnp.stack([field, back])
    return came


def mesh_sum(value):
    for axis in ("ta", "gz", "gx"):
        size = lax.axis_size(axis)
        if size & (size - 1):
            value = lax.psum(value, axis)
            continue
        hop = 1
        while hop < size:
            value = value + lax.ppermute(value, axis, [(i, i ^ hop) for i in range(size)])
            hop *= 2
    return value


def on_device(rhs, self_coupling, hopping):
    extents = rhs.shape[1:5]
    rows, channels = rhs.shape[5:]
    lanes = 2 * channels
    box = Box(extents)
    count = box.count
    source = rhs.reshape(count, rows, channels)
    own = self_coupling.reshape(count, channels, channels)
    hop = hopping.reshape(4, count, channels, channels)

    flips_out = []
    flips_in = []
    for d in range(4):
        axis, _, _, kind = plan(d)
        if kind == "pairs":
            odd = lax.axis_index(axis) % 2
            flips_out.append(1 - odd)
            flips_in.append(odd)
        else:
            flips_out.append(jnp.int32(0))
            flips_in.append(jnp.int32(0))
    flips_out = jnp.stack(flips_out).astype(jnp.int32)
    flips_in = jnp.stack(flips_in).astype(jnp.int32)

    full = jax.ShapeDtypeStruct((count, rows, lanes), F32)
    small = jax.ShapeDtypeStruct((rows, lanes), F32)
    narrow = jax.ShapeDtypeStruct((count, rows, channels), F32)
    links_shape = jax.ShapeDtypeStruct((count, channels, 4 * channels), BF16)
    send_shapes = [
        jax.ShapeDtypeStruct((2, len(box.rim(d, True)) // 4, 2 * rows, lanes), BF16) for d in range(4)
    ]
    field_scratch = pltpu.VMEM((count, rows, lanes), F32)
    back_scratch = pltpu.VMEM((count, rows, 4 * channels), F32)
    scratch = [field_scratch, back_scratch, back_scratch, field_scratch, field_scratch, field_scratch]

    update_a, image_a, *sends, links = call(
        functools.partial(first_kernel, box),
        [full, full, *send_shapes, links_shape],
        scratch,
        (source, own, hop),
        flips_out,
    )
    came = exchange(sends)
    map_a, sums_a = call(
        functools.partial(third_kernel, box), [full, small], [], (source, image_a, links, *came), flips_in
    )
    sums_a = mesh_sum(sums_a)
    update_b, image_b, *sends = call(
        functools.partial(second_kernel, box),
        [full, full, *send_shapes],
        scratch,
        (source, map_a, sums_a, links, own),
        flips_out,
    )
    came = exchange(sends)
    map_b, sums_b = call(
        functools.partial(fourth_kernel, box),
        [full, small],
        [],
        (source, map_a, sums_a, image_b, links, *came),
        flips_in,
    )
    sums_b = mesh_sum(sums_b)
    found, left = call(
        functools.partial(last_kernel, box),
        [narrow, narrow],
        [],
        (source, update_a, map_a, update_b, map_b, sums_a, sums_b),
    )
    return found.reshape(rhs.shape), left.reshape(rhs.shape)


def solution(mesh):
    in_specs = (
        P("gx", None, None, "gz", "ta", None, None),
        P("gx", None, None, "gz", "ta", None, None),
        P(None, "gx", None, None, "gz", "ta", None, None),
    )
    out_specs = (
        P("gx", None, None, "gz", "ta", None, None),
        P("gx", None, None, "gz", "ta", None, None),
    )
    return jax.shard_map(
        on_device, mesh=mesh, in_specs=in_specs, out_specs=out_specs, check_vma=False
    )
```

time: 186 us -> 75.2 us (0.40)
  blocking collectives: 75.4 us -> 0 us
  matrix products: 35.3 us -> 0 us
  Pallas kernels: 0 us -> 12.4 us
  starting transfers between devices: 28.8 us -> 18.5 us
  other arithmetic: 2.15 us -> 0.21 us
    psum x2 -> x0, blocking collectives: 75.4 us -> none  [mesh_total(): return lax.psum(partials, ('gx', 'gz', 'ta'))]
    dot_general x62 -> x0, matrix products: 35.3 us -> none  [the longest x30 20.5 us: site_product(): jnp.einsum('xyztab,xyztrb->xyztra', link_block, field_bf, preferred_eleme...]
    pallas_call x0 -> x5, Pallas kernels: none -> 12.4 us  [call(): pl.pallas_call(body, out_shape=outs, in_specs=specs, out_specs=[vmem] * l...]
    ppermute x20 -> x22, starting transfers between devices: 28.8 us -> 18.5 us  [the longest x4 7.54 us: exchange(): lax.ppermute(sends[d][1], axis, [(i, (i + 1 if i % 2 else i - 1) % size)...]
    unnamed x12 -> x10, local copies, waits for them, and re-layouts: 0.03 us -> 4.37 us
    squeeze x1 -> x4, local copies, waits for them, and re-layouts: 2.74 us -> 0.02 us  [exchange(): even = lax.ppermute(sends[d][0], axis, [(i, i ^ 1) for i in ring])]
    ppermute x20 -> x22, waiting for transfers between devices: 39.6 us -> 38.6 us  [the longest x10 28 us: mesh_sum(): lax.ppermute(value, axis, [(i, i ^ hop) for i in range(size)])]
  transfers between devices with their start and end apart: 20 -> 22, of which waited for: 7 -> 15; matrix products, arithmetic and copies ran while one was open for 10% -> 0% of each run, Pallas kernels for 0% -> 0%
where the time goes in v1:
time: 75.2 us; the launch traced here: 74.9 us
  waiting for transfers between devices  38.6 us (51%)
  starting transfers between devices  18.5 us (25%)
  Pallas kernels  12.4 us (16%)
  local copies, waits for them, and re-layouts  4.39 us (6%)
  between operations  0.77 us (1%)
    ppermute x10, waiting for transfers between devices, mesh_sum(): lax.ppermute(value, axis, [(i, i ^ hop) for i in range(size)])  28 us
    pallas_call x5, Pallas kernels, call(): pl.pallas_call(body, out_shape=outs, in_specs=specs, out_specs=[vmem] * l...  12.4 us
    ppermute x4, starting transfers between devices, exchange(): lax.ppermute(sends[d][1], axis, [(i, (i + 1 if i % 2 else i - 1) % size)...  7.54 us
    ppermute x4, waiting for transfers between devices, exchange(): lax.ppermute(sends[d][1], axis, [(i, (i + 1 if i % 2 else i - 1) % size)...  5.65 us
    ppermute x10, starting transfers between devices, mesh_sum(): lax.ppermute(value, axis, [(i, i ^ hop) for i in range(size)])  4.97 us
    ppermute x4, waiting for transfers between devices, exchange(): lax.ppermute(sends[d], axis, [(i, (i + step) % size) for i in ring])  4.52 us
    unnamed x10, local copies, waits for them, and re-layouts  4.37 us
    ppermute x4, starting transfers between devices, exchange(): lax.ppermute(sends[d], axis, [(i, (i + step) % size) for i in ring])  3.78 us
  transfers between devices with their start and end apart: 22, of which 15 were waited for; matrix products, arithmetic and copies ran while one was open for 0% of the time, Pallas kernels for 0%

profile of v1, /device:TPU:0, one launch (start us, length us, event | category | flops | bytes accessed | tf_op | source)
XLA Modules:
  0.0 74.9 jit_solution(13408000466054327043)
XLA Ops:
  0.6 0.1 fusion.flips
  0.7 0.0 copy-start
  0.7 0.9 %copy-done = f32[1,2,2,4,4,8,64]{6,5,4,3,2,1,0:T(8,128)S(1)} copy-done((f32[1,2,2,4,4,8,64]{6,5,4,3,2,1,0:T(8,128)S(1)}, f32[1,2,2,4,4,8,64]{6,5,4,3,2,1,0:T(8,128)}, u32[]{:S(2)}) %copy-start) | copy-done | bytes 131096
  1.7 0.0 copy-start.2
  1.7 2.2 %copy-done.2 = bf16[4,1,2,2,4,4,64,64]{7,6,5,4,3,2,1,0:T(8,128)(2,1)S(1)} copy-done((bf16[4,1,2,2,4,4,64,64]{7,6,5,4,3,2,1,0:T(8,128)(2,1)S(1)}, bf16[4,1,2,2,4,4,64,64]{7,6,5,4,3,2,1,0:T(8,128)(2,1)}, u32[]{:S(2)}) %copy-start.2) | copy-done | bytes 2097176
  3.9 0.0 copy-start.3
  3.9 1.2 %copy-done.3 = bf16[1,2,2,4,4,64,64]{6,5,4,3,2,1,0:T(8,128)(2,1)S(1)} copy-done((bf16[1,2,2,4,4,64,64]{6,5,4,3,2,1,0:T(8,128)(2,1)S(1)}, bf16[1,2,2,4,4,64,64]{6,5,4,3,2,1,0:T(8,128)(2,1)}, u32[]{:S(2)}) %copy-start.3) | copy-done | bytes 524312
  5.1 0.0 copy-start.1
  5.1 0.0 copy-start.4
  5.1 4.3 %shard_map.50 = (f32[64,8,128]{2,1,0:T(8,128)S(1)}, f32[64,8,128]{2,1,0:T(8,128)S(1)}, bf16[2,8,16,128]{3,2,1,0:T(8,128)(2,1)S(1)}, bf16[2,8,16,128]{3,2,1,0:T(8...) custom-call(s32[4]{0:T(128)S(1)} %fusion.flips, ...), custom_call_target="tpu_custom_call" | custom-call | tf_op jit(solution)/shard_map/pallas_call | solution.py:236
  9.4 0.5 collective-permute-start.4
  9.9 2.6 %collective-permute-start.5 = (bf16[4,16,128]{2,1,0:T(8,128)(2,1)S(1)}, bf16[4,16,128]{2,1,0:T(8,128)(2,1)S(1)}, u32[]{:S(2)}, u32[]{:S(2)}) collective-permute-start(bf16[4,16,128]{2,1,0:T(8,128)(2,1)S(1)} %get-tuple-element.47), channel_id=1, source_target_pairs={{0,3},{1,2},{2,1},{3,0},{4,7},{5,6},{6,5},{7,4},{8,11},{9,10},{10,... | collective-permute-start | bytes 49160 | tf_op jit(solution)/shard_map/ppermute | solution.py:266
  12.6 1.5 %collective-permute-start.3 = (bf16[2,4,16,128]{3,2,1,0:T(8,128)(2,1)S(1)}, bf16[2,4,16,128]{3,2,1,0:T(8,128)(2,1)S(1)}, u32[]{:S(2)}, u32[]{:S(2)}) collective-permute-start(bf16[2,4,16,128]{3,2,1,0:T(8,128)(2,1)S(1)} %get-tuple-element.26), channel_id=1, source_target_pairs={{0,4},{4,0},{1,5},{5,1},{2,6},{6,2},{3,7},{7,3},{8,12},{12,8},{9,1... | collective-permute-start | bytes 98312 | tf_op jit(solution)/shard_map/ppermute | solution.py:263
  14.1 1.6 %collective-permute-start.1 = (bf16[8,16,128]{2,1,0:T(8,128)(2,1)S(1)}, bf16[8,16,128]{2,1,0:T(8,128)(2,1)S(1)}, u32[]{:S(2)}, u32[]{:S(2)}) collective-permute-start(bf16[8,16,128]{2,1,0:T(8,128)(2,1)S(1)} %get-tuple-element.42), channel_id=1, source_target_pairs={{0,8},{8,0},{16,24},{24,16},{1,9},{9,1},{17,25},{25,17},{2,10},{10... | collective-permute-start | bytes 98312 | tf_op jit(solution)/shard_map/ppermute | solution.py:265
  15.7 2.5 %collective-permute-start.2 = (bf16[8,16,128]{2,1,0:T(8,128)(2,1)S(1)}, bf16[8,16,128]{2,1,0:T(8,128)(2,1)S(1)}, u32[]{:S(2)}, u32[]{:S(2)}) collective-permute-start(bf16[8,16,128]{2,1,0:T(8,128)(2,1)S(1)} %get-tuple-element.43), channel_id=1, source_target_pairs={{0,24},{8,16},{16,8},{24,0},{1,25},{9,17},{17,9},{25,1},{2,26},{10... | collective-permute-start | bytes 98312 | tf_op jit(solution)/shard_map/ppermute | solution.py:266
  18.1 0.1 fusion.1.flips
  18.2 0.0 collective-permute-done.4
  18.2 0.1 collective-permute-start
  18.3 0.0 collective-permute-done.5
  18.3 0.0 collective-permute-done.1
  18.4 3.4 %collective-permute-done.2 = bf16[8,16,128]{2,1,0:T(8,128)(2,1)S(1)} collective-permute-done((bf16[8,16,128]{2,1,0:T(8,128)(2,1)S(1)}, bf16[8,16,128]{2,1,0:T(8,128)(2,1)S(1)}, u32[]{:S(2)}, u32[]{:S(2)}) %collective-permute-start.2) | collective-permute-done | bytes 32800 | tf_op jit(solution)/shard_map/ppermute | solution.py:266
  21.8 0.0 collective-permute-done.3.came2
  21.8 2.3 %collective-permute-done.came0 = bf16[2,8,16,128]{3,2,1,0:T(8,128)(2,1)S(1)} collective-permute-done((bf16[2,8,16,128]{3,2,1,0:T(8,128)(2,1)S(1)}, bf16[2,8,16,128]{3,2,1,0:T(8,128)(2,1)S(1)}, u32[]{:S(2)}, u32[]{:S(2)}) %collective-permute-start) | collective-permute-done | bytes 65568 | tf_op jit(solution)/shard_map/ppermute | solution.py:263
  24.1 0.0 copy-done.1
  24.1 1.3 %shard_map.51 = (f32[64,8,128]{2,1,0:T(8,128)S(1)}, f32[8,128]{1,0:T(8,128)S(1)}) custom-call(s32[4]{0:T(128)S(1)} %fusion.1.flips, f32[64,8,64]{2,1,0:T(8,128)S(1)} %bitcast.34, f32[64,8,128]{2,1,0:T(8,128)S(1)} %get-tuple-element.22.image, bf16[64,64,256]{2,1,0:T(8,128)(2,1)S(1)} %get-tuple-element.23.links, ...), custom_call_target="tpu_custom_call" | custom-call | tf_op jit(solution)/shard_map/pallas_call | solution.py:236
  25.4 0.0 collective-permute-start.6
  25.4 1.2 %collective-permute-done.6 = f32[8,128]{1,0:T(8,128)S(1)} collective-permute-done((f32[8,128]{1,0:T(8,128)S(1)}, f32[8,128]{1,0:T(8,128)S(1)}, u32[]{:S(2)}, u32[]{:S(2)}) %collective-permute-start.6) | collective-permute-done | bytes 4128 | tf_op jit(solution)/shard_map/ppermute | solution.py:283
  26.6 0.5 collective-permute-start.7
  27.1 3.1 %collective-permute-done.7 = f32[8,128]{1,0:T(8,128)S(1)} collective-permute-done((f32[8,128]{1,0:T(8,128)S(1)}, f32[8,128]{1,0:T(8,128)S(1)}, u32[]{:S(2)}, u32[]{:S(2)}) %collective-permute-start.7) | collective-permute-done | bytes 4128 | tf_op jit(solution)/shard_map/ppermute | solution.py:283
  30.2 0.5 collective-permute-start.8
  30.8 3.1 %collective-permute-done.8 = f32[8,128]{1,0:T(8,128)S(1)} collective-permute-done((f32[8,128]{1,0:T(8,128)S(1)}, f32[8,128]{1,0:T(8,128)S(1)}, u32[]{:S(2)}, u32[]{:S(2)}) %collective-permute-start.8) | collective-permute-done | bytes 4128 | tf_op jit(solution)/shard_map/ppermute | solution.py:283
  33.8 0.1 collective-permute-start.9
  33.9 3.5 %collective-permute-done.9 = f32[8,128]{1,0:T(8,128)S(1)} collective-permute-done((f32[8,128]{1,0:T(8,128)S(1)}, f32[8,128]{1,0:T(8,128)S(1)}, u32[]{:S(2)}, u32[]{:S(2)}) %collective-permute-start.9) | collective-permute-done | bytes 4128 | tf_op jit(solution)/shard_map/ppermute | solution.py:283
  37.4 0.3 collective-permute-start.10
  37.8 4.2 %collective-permute-done.10 = f32[8,128]{1,0:T(8,128)S(1)} collective-permute-done((f32[8,128]{1,0:T(8,128)S(1)}, f32[8,128]{1,0:T(8,128)S(1)}, u32[]{:S(2)}, u32[]{:S(2)}) %collective-permute-start.10) | collective-permute-done | bytes 4128 | tf_op jit(solution)/shard_map/ppermute | solution.py:283
  42.0 0.0 copy-done.4
  42.0 4.3 %shard_map.52 = (f32[64,8,128]{2,1,0:T(8,128)S(1)}, f32[64,8,128]{2,1,0:T(8,128)S(1)}, bf16[2,8,16,128]{3,2,1,0:T(8,128)(2,1)S(1)}, bf16[2,8,16,128]{3,2,1,0:T(8...) custom-call(s32[4]{0:T(128)S(1)} %fusion.flips, f32[64,8,64]{2,1,0:T(8,128)S(1)} %bitcast.35, ...), custom_call_target="tpu_custom_call" | custom-call | tf_op jit(solution)/shard_map/pallas_call | solution.py:236
  46.3 0.1 collective-permute-start.15
  46.4 0.6 collective-permute-start.16
  47.0 0.5 collective-permute-start.14
  47.5 0.1 collective-permute-start.12
  47.6 1.8 %collective-permute-start.13 = (bf16[8,16,128]{2,1,0:T(8,128)(2,1)S(1)}, bf16[8,16,128]{2,1,0:T(8,128)(2,1)S(1)}, u32[]{:S(2)}, u32[]{:S(2)}) collective-permute-start(bf16[8,16,128]{2,1,0:T(8,128)(2,1)S(1)} %get-tuple-element.41), channel_id=1, source_target_pairs={{0,24},{8,16},{16,8},{24,0},{1,25},{9,17},{17,9},{25,1},{2,26},{10... | collective-permute-start | bytes 98312 | tf_op jit(solution)/shard_map/ppermute | solution.py:266
  49.4 0.0 collective-permute-done.15
  49.4 1.6 %collective-permute-start.11 = (bf16[2,8,16,128]{3,2,1,0:T(8,128)(2,1)S(1)}, bf16[2,8,16,128]{3,2,1,0:T(8,128)(2,1)S(1)}, u32[]{:S(2)}, u32[]{:S(2)}) collective-permute-start(bf16[2,8,16,128]{3,2,1,0:T(8,128)(2,1)S(1)} %get-tuple-element.32), channel_id=1, source_target_pairs={{0,16},{8,24},{16,0},{24,8},{1,17},{9,25},{17,1},{25,9},{2,18},{10... | collective-permute-start | bytes 196616 | tf_op jit(solution)/shard_map/ppermute | solution.py:263
  51.0 0.0 collective-permute-done.16
  51.0 0.4 collective-permute-done.12
  51.5 2.2 %collective-permute-done.13 = bf16[8,16,128]{2,1,0:T(8,128)(2,1)S(1)} collective-permute-done((bf16[8,16,128]{2,1,0:T(8,128)(2,1)S(1)}, bf16[8,16,128]{2,1,0:T(8,128)(2,1)S(1)}, u32[]{:S(2)}, u32[]{:S(2)}) %collective-permute-start.13) | collective-permute-done | bytes 32800 | tf_op jit(solution)/shard_map/ppermute | solution.py:266
  53.7 0.0 collective-permute-done.14.came2
  53.7 2.2 %collective-permute-done.11.came0 = bf16[2,8,16,128]{3,2,1,0:T(8,128)(2,1)S(1)} collective-permute-done((bf16[2,8,16,128]{3,2,1,0:T(8,128)(2,1)S(1)}, bf16[2,8,16,128]{3,2,1,0:T(8,128)(2,1)S(1)}, u32[]{:S(2)}, u32[]{:S(2)}) %collective-permute-start.11) | collective-permute-done | bytes 65568 | tf_op jit(solution)/shard_map/ppermute | solution.py:263
  55.9 1.4 %shard_map.53 = (f32[64,8,128]{2,1,0:T(8,128)S(1)}, f32[8,128]{1,0:T(8,128)S(1)}) custom-call(s32[4]{0:T(128)S(1)} %fusion.1.flips, f32[64,8,64]{2,1,0:T(8,128)S(1)} %bitcast.36, f32[64,8,128]{2,1,0:T(8,128)S(1)} %get-tuple-element.28.mapped.first.map_a, f32[8,128]{1,0:T(8,128)S(1)} %add.43.sums.before.sums_a, f32[64,8,128]{2,1,0:T(8,128)S(1)} %get-tuple-element.31.image, ...), custom_call_target="tpu_custom_call" | custom-call | tf_op jit(solution)/shard_map/pallas_call | solution.py:236
  57.3 0.0 collective-permute-start.17
  57.3 1.2 %collective-permute-done.17 = f32[8,128]{1,0:T(8,128)S(1)} collective-permute-done((f32[8,128]{1,0:T(8,128)S(1)}, f32[8,128]{1,0:T(8,128)S(1)}, u32[]{:S(2)}, u32[]{:S(2)}) %collective-permute-start.17) | collective-permute-done | bytes 4128 | tf_op jit(solution)/shard_map/ppermute | solution.py:283
  58.4 1.5 %collective-permute-start.18 = (f32[8,128]{1,0:T(8,128)S(1)}, f32[8,128]{1,0:T(8,128)S(1)}, u32[]{:S(2)}, u32[]{:S(2)}) collective-permute-start(f32[8,128]{1,0:T(8,128)S(1)} %add.44), channel_id=1, source_target_pairs={{0,2},{1,3},{2,0},{3,1},{4,6},{5,7},{6,4},{7,5},{8,10},{9,11},{10,... | collective-permute-start | bytes 12296 | tf_op jit(solution)/shard_map/ppermute | solution.py:283
  60.0 2.1 %collective-permute-done.18 = f32[8,128]{1,0:T(8,128)S(1)} collective-permute-done((f32[8,128]{1,0:T(8,128)S(1)}, f32[8,128]{1,0:T(8,128)S(1)}, u32[]{:S(2)}, u32[]{:S(2)}) %collective-permute-start.18) | collective-permute-done | bytes 4128 | tf_op jit(solution)/shard_map/ppermute | solution.py:283
  62.1 1.5 %collective-permute-start.19 = (f32[8,128]{1,0:T(8,128)S(1)}, f32[8,128]{1,0:T(8,128)S(1)}, u32[]{:S(2)}, u32[]{:S(2)}) collective-permute-start(f32[8,128]{1,0:T(8,128)S(1)} %add.45), channel_id=1, source_target_pairs={{0,4},{4,0},{1,5},{5,1},{2,6},{6,2},{3,7},{7,3},{8,12},{12,8},{9,1... | collective-permute-start | bytes 12296 | tf_op jit(solution)/shard_map/ppermute | solution.py:283
  63.5 2.1 %collective-permute-done.19 = f32[8,128]{1,0:T(8,128)S(1)} collective-permute-done((f32[8,128]{1,0:T(8,128)S(1)}, f32[8,128]{1,0:T(8,128)S(1)}, u32[]{:S(2)}, u32[]{:S(2)}) %collective-permute-start.19) | collective-permute-done | bytes 4128 | tf_op jit(solution)/shard_map/ppermute | solution.py:283
  65.7 0.0 collective-permute-start.20
  65.7 3.6 %collective-permute-done.20 = f32[8,128]{1,0:T(8,128)S(1)} collective-permute-done((f32[8,128]{1,0:T(8,128)S(1)}, f32[8,128]{1,0:T(8,128)S(1)}, u32[]{:S(2)}, u32[]{:S(2)}) %collective-permute-start.20) | collective-permute-done | bytes 4128 | tf_op jit(solution)/shard_map/ppermute | solution.py:283
  69.3 0.5 collective-permute-start.21
  69.8 4.0 %collective-permute-done.21 = f32[8,128]{1,0:T(8,128)S(1)} collective-permute-done((f32[8,128]{1,0:T(8,128)S(1)}, f32[8,128]{1,0:T(8,128)S(1)}, u32[]{:S(2)}, u32[]{:S(2)}) %collective-permute-start.21) | collective-permute-done | bytes 4128 | tf_op jit(solution)/shard_map/ppermute | solution.py:283
  73.8 1.2 %shard_map.54 = (f32[64,8,64]{2,1,0:T(8,128)}, f32[64,8,64]{2,1,0:T(8,128)}) custom-call(f32[64,8,64]{2,1,0:T(8,128)S(1)} %bitcast.37, f32[64,8,128]{2,1,0:T(8,128)S(1)} %get-tuple-element.21.update_a, f32[64,8,128]{2,1,0:T(8,128)S(1)} %get-tuple-element.28.mapped.first.map_a, f32[64,8,128]{2,1,0:T(8,128)S(1)} %get-tuple-element.30.update_b, ...), custom_call_target="tpu_custom_call" | custom-call | tf_op jit(solution)/shard_map/pallas_call | solution.py:236
  (18 shorter events, 0.1 us)
Async XLA Ops:
  0.7 1.0 %copy-start = (f32[1,2,2,4,4,8,64]{6,5,4,3,2,1,0:T(8,128)S(1)}, f32[1,2,2,4,4,8,64]{6,5,4,3,2,1,0:T(8,128)}, u32[]{:S(2)}) copy-start(f32[1,2,2,4,4,8,64]{6,5,4,3,2,1,0:T(8,128)} %param.3) | copy-start | bytes 393220
  1.7 2.2 %copy-start.2 = (bf16[4,1,2,2,4,4,64,64]{7,6,5,4,3,2,1,0:T(8,128)(2,1)S(1)}, bf16[4,1,2,2,4,4,64,64]{7,6,5,4,3,2,1,0:T(8,128)(2,1)}, u32[]{:S(2)}) copy-start(bf16[4,1,2,2,4,4,64,64]{7,6,5,4,3,2,1,0:T(8,128)(2,1)} %param.5) | copy-start | bytes 6291460
  3.9 1.2 %copy-start.3 = (bf16[1,2,2,4,4,64,64]{6,5,4,3,2,1,0:T(8,128)(2,1)S(1)}, bf16[1,2,2,4,4,64,64]{6,5,4,3,2,1,0:T(8,128)(2,1)}, u32[]{:S(2)}) copy-start(bf16[1,2,2,4,4,64,64]{6,5,4,3,2,1,0:T(8,128)(2,1)} %param.4) | copy-start | bytes 1572868
  5.1 19.0 %copy-start.1 = (f32[1,2,2,4,4,8,64]{6,5,4,3,2,1,0:T(8,128)S(1)}, f32[1,2,2,4,4,8,64]{6,5,4,3,2,1,0:T(8,128)}, u32[]{:S(2)}) copy-start(f32[1,2,2,4,4,8,64]{6,5,4,3,2,1,0:T(8,128)} %param.3) | copy-start | bytes 393220
  5.1 36.9 %copy-start.4 = (bf16[1,2,2,4,4,64,64]{6,5,4,3,2,1,0:T(8,128)(2,1)S(1)}, bf16[1,2,2,4,4,64,64]{6,5,4,3,2,1,0:T(8,128)(2,1)}, u32[]{:S(2)}) copy-start(bf16[1,2,2,4,4,64,64]{6,5,4,3,2,1,0:T(8,128)(2,1)} %param.4) | copy-start | bytes 1572868
  9.4 8.8 %collective-permute-start.4 = (bf16[4,16,128]{2,1,0:T(8,128)(2,1)S(1)}, bf16[4,16,128]{2,1,0:T(8,128)(2,1)S(1)}, u32[]{:S(2)}, u32[]{:S(2)}) collective-permute-start(bf16[4,16,128]{2,1,0:T(8,128)(2,1)S(1)} %get-tuple-element.46), channel_id=1, source_target_pairs={{0,1},{1,0},{2,3},{3,2},{4,5},{5,4},{6,7},{7,6},{8,9},{9,8},{10,11... | collective-permute-start | bytes 49160 | tf_op jit(solution)/shard_map/ppermute | solution.py:265
  9.9 8.4 %collective-permute-start.5 = (bf16[4,16,128]{2,1,0:T(8,128)(2,1)S(1)}, bf16[4,16,128]{2,1,0:T(8,128)(2,1)S(1)}, u32[]{:S(2)}, u32[]{:S(2)}) collective-permute-start(bf16[4,16,128]{2,1,0:T(8,128)(2,1)S(1)} %get-tuple-element.47), channel_id=1, source_target_pairs={{0,3},{1,2},{2,1},{3,0},{4,7},{5,6},{6,5},{7,4},{8,11},{9,10},{10,... | collective-permute-start | bytes 49160 | tf_op jit(solution)/shard_map/ppermute | solution.py:266
  12.6 9.2 %collective-permute-start.3 = (bf16[2,4,16,128]{3,2,1,0:T(8,128)(2,1)S(1)}, bf16[2,4,16,128]{3,2,1,0:T(8,128)(2,1)S(1)}, u32[]{:S(2)}, u32[]{:S(2)}) collective-permute-start(bf16[2,4,16,128]{3,2,1,0:T(8,128)(2,1)S(1)} %get-tuple-element.26), channel_id=1, source_target_pairs={{0,4},{4,0},{1,5},{5,1},{2,6},{6,2},{3,7},{7,3},{8,12},{12,8},{9,1... | collective-permute-start | bytes 98312 | tf_op jit(solution)/shard_map/ppermute | solution.py:263
  14.1 4.3 %collective-permute-start.1 = (bf16[8,16,128]{2,1,0:T(8,128)(2,1)S(1)}, bf16[8,16,128]{2,1,0:T(8,128)(2,1)S(1)}, u32[]{:S(2)}, u32[]{:S(2)}) collective-permute-start(bf16[8,16,128]{2,1,0:T(8,128)(2,1)S(1)} %get-tuple-element.42), channel_id=1, source_target_pairs={{0,8},{8,0},{16,24},{24,16},{1,9},{9,1},{17,25},{25,17},{2,10},{10... | collective-permute-start | bytes 98312 | tf_op jit(solution)/shard_map/ppermute | solution.py:265
  15.7 6.1 %collective-permute-start.2 = (bf16[8,16,128]{2,1,0:T(8,128)(2,1)S(1)}, bf16[8,16,128]{2,1,0:T(8,128)(2,1)S(1)}, u32[]{:S(2)}, u32[]{:S(2)}) collective-permute-start(bf16[8,16,128]{2,1,0:T(8,128)(2,1)S(1)} %get-tuple-element.43), channel_id=1, source_target_pairs={{0,24},{8,16},{16,8},{24,0},{1,25},{9,17},{17,9},{25,1},{2,26},{10... | collective-permute-start | bytes 98312 | tf_op jit(solution)/shard_map/ppermute | solution.py:266
  18.2 5.9 %collective-permute-start = (bf16[2,8,16,128]{3,2,1,0:T(8,128)(2,1)S(1)}, bf16[2,8,16,128]{3,2,1,0:T(8,128)(2,1)S(1)}, u32[]{:S(2)}, u32[]{:S(2)}) collective-permute-start(bf16[2,8,16,128]{3,2,1,0:T(8,128)(2,1)S(1)} %get-tuple-element.24), channel_id=1, source_target_pairs={{0,16},{8,24},{16,0},{24,8},{1,17},{9,25},{17,1},{25,9},{2,18},{10... | collective-permute-start | bytes 196616 | tf_op jit(solution)/shard_map/ppermute | solution.py:263
  25.4 1.2 %collective-permute-start.6 = (f32[8,128]{1,0:T(8,128)S(1)}, f32[8,128]{1,0:T(8,128)S(1)}, u32[]{:S(2)}, u32[]{:S(2)}) collective-permute-start(f32[8,128]{1,0:T(8,128)S(1)} %get-tuple-element.29), channel_id=1, source_target_pairs={{0,1},{1,0},{2,3},{3,2},{4,5},{5,4},{6,7},{7,6},{8,9},{9,8},{10,11... | collective-permute-start | bytes 12296 | tf_op jit(solution)/shard_map/ppermute | solution.py:283
  26.6 3.6 %collective-permute-start.7 = (f32[8,128]{1,0:T(8,128)S(1)}, f32[8,128]{1,0:T(8,128)S(1)}, u32[]{:S(2)}, u32[]{:S(2)}) collective-permute-start(f32[8,128]{1,0:T(8,128)S(1)} %add.39), channel_id=1, source_target_pairs={{0,2},{1,3},{2,0},{3,1},{4,6},{5,7},{6,4},{7,5},{8,10},{9,11},{10,... | collective-permute-start | bytes 12296 | tf_op jit(solution)/shard_map/ppermute | solution.py:283
  30.2 3.6 %collective-permute-start.8 = (f32[8,128]{1,0:T(8,128)S(1)}, f32[8,128]{1,0:T(8,128)S(1)}, u32[]{:S(2)}, u32[]{:S(2)}) collective-permute-start(f32[8,128]{1,0:T(8,128)S(1)} %add.40), channel_id=1, source_target_pairs={{0,4},{4,0},{1,5},{5,1},{2,6},{6,2},{3,7},{7,3},{8,12},{12,8},{9,1... | collective-permute-start | bytes 12296 | tf_op jit(solution)/shard_map/ppermute | solution.py:283
  33.8 3.6 %collective-permute-start.9 = (f32[8,128]{1,0:T(8,128)S(1)}, f32[8,128]{1,0:T(8,128)S(1)}, u32[]{:S(2)}, u32[]{:S(2)}) collective-permute-start(f32[8,128]{1,0:T(8,128)S(1)} %add.41), channel_id=1, source_target_pairs={{0,8},{8,0},{16,24},{24,16},{1,9},{9,1},{17,25},{25,17},{2,10},{10... | collective-permute-start | bytes 12296 | tf_op jit(solution)/shard_map/ppermute | solution.py:283
  37.4 4.5 %collective-permute-start.10 = (f32[8,128]{1,0:T(8,128)S(1)}, f32[8,128]{1,0:T(8,128)S(1)}, u32[]{:S(2)}, u32[]{:S(2)}) collective-permute-start(f32[8,128]{1,0:T(8,128)S(1)} %add.42), channel_id=1, source_target_pairs={{0,16},{8,24},{16,0},{24,8},{1,17},{9,25},{17,1},{25,9},{2,18},{10... | collective-permute-start | bytes 12296 | tf_op jit(solution)/shard_map/ppermute | solution.py:283
  46.3 3.1 %collective-permute-start.15 = (bf16[4,16,128]{2,1,0:T(8,128)(2,1)S(1)}, bf16[4,16,128]{2,1,0:T(8,128)(2,1)S(1)}, u32[]{:S(2)}, u32[]{:S(2)}) collective-permute-start(bf16[4,16,128]{2,1,0:T(8,128)(2,1)S(1)} %get-tuple-element.44), channel_id=1, source_target_pairs={{0,1},{1,0},{2,3},{3,2},{4,5},{5,4},{6,7},{7,6},{8,9},{9,8},{10,11... | collective-permute-start | bytes 49160 | tf_op jit(solution)/shard_map/ppermute | solution.py:265
  46.4 4.7 %collective-permute-start.16 = (bf16[4,16,128]{2,1,0:T(8,128)(2,1)S(1)}, bf16[4,16,128]{2,1,0:T(8,128)(2,1)S(1)}, u32[]{:S(2)}, u32[]{:S(2)}) collective-permute-start(bf16[4,16,128]{2,1,0:T(8,128)(2,1)S(1)} %get-tuple-element.45), channel_id=1, source_target_pairs={{0,3},{1,2},{2,1},{3,0},{4,7},{5,6},{6,5},{7,4},{8,11},{9,10},{10,... | collective-permute-start | bytes 49160 | tf_op jit(solution)/shard_map/ppermute | solution.py:266
  47.0 6.7 %collective-permute-start.14 = (bf16[2,4,16,128]{3,2,1,0:T(8,128)(2,1)S(1)}, bf16[2,4,16,128]{3,2,1,0:T(8,128)(2,1)S(1)}, u32[]{:S(2)}, u32[]{:S(2)}) collective-permute-start(bf16[2,4,16,128]{3,2,1,0:T(8,128)(2,1)S(1)} %get-tuple-element.34), channel_id=1, source_target_pairs={{0,4},{4,0},{1,5},{5,1},{2,6},{6,2},{3,7},{7,3},{8,12},{12,8},{9,1... | collective-permute-start | bytes 98312 | tf_op jit(solution)/shard_map/ppermute | solution.py:263
  47.5 3.9 %collective-permute-start.12 = (bf16[8,16,128]{2,1,0:T(8,128)(2,1)S(1)}, bf16[8,16,128]{2,1,0:T(8,128)(2,1)S(1)}, u32[]{:S(2)}, u32[]{:S(2)}) collective-permute-start(bf16[8,16,128]{2,1,0:T(8,128)(2,1)S(1)} %get-tuple-element.40), channel_id=1, source_target_pairs={{0,8},{8,0},{16,24},{24,16},{1,9},{9,1},{17,25},{25,17},{2,10},{10... | collective-permute-start | bytes 98312 | tf_op jit(solution)/shard_map/ppermute | solution.py:265
  47.6 6.1 %collective-permute-start.13 = (bf16[8,16,128]{2,1,0:T(8,128)(2,1)S(1)}, bf16[8,16,128]{2,1,0:T(8,128)(2,1)S(1)}, u32[]{:S(2)}, u32[]{:S(2)}) collective-permute-start(bf16[8,16,128]{2,1,0:T(8,128)(2,1)S(1)} %get-tuple-element.41), channel_id=1, source_target_pairs={{0,24},{8,16},{16,8},{24,0},{1,25},{9,17},{17,9},{25,1},{2,26},{10... | collective-permute-start | bytes 98312 | tf_op jit(solution)/shard_map/ppermute | solution.py:266
  49.4 6.5 %collective-permute-start.11 = (bf16[2,8,16,128]{3,2,1,0:T(8,128)(2,1)S(1)}, bf16[2,8,16,128]{3,2,1,0:T(8,128)(2,1)S(1)}, u32[]{:S(2)}, u32[]{:S(2)}) collective-permute-start(bf16[2,8,16,128]{3,2,1,0:T(8,128)(2,1)S(1)} %get-tuple-element.32), channel_id=1, source_target_pairs={{0,16},{8,24},{16,0},{24,8},{1,17},{9,25},{17,1},{25,9},{2,18},{10... | collective-permute-start | bytes 196616 | tf_op jit(solution)/shard_map/ppermute | solution.py:263
  57.3 1.2 %collective-permute-start.17 = (f32[8,128]{1,0:T(8,128)S(1)}, f32[8,128]{1,0:T(8,128)S(1)}, u32[]{:S(2)}, u32[]{:S(2)}) collective-permute-start(f32[8,128]{1,0:T(8,128)S(1)} %get-tuple-element.37), channel_id=1, source_target_pairs={{0,1},{1,0},{2,3},{3,2},{4,5},{5,4},{6,7},{7,6},{8,9},{9,8},{10,11... | collective-permute-start | bytes 12296 | tf_op jit(solution)/shard_map/ppermute | solution.py:283
  58.4 3.6 %collective-permute-start.18 = (f32[8,128]{1,0:T(8,128)S(1)}, f32[8,128]{1,0:T(8,128)S(1)}, u32[]{:S(2)}, u32[]{:S(2)}) collective-permute-start(f32[8,128]{1,0:T(8,128)S(1)} %add.44), channel_id=1, source_target_pairs={{0,2},{1,3},{2,0},{3,1},{4,6},{5,7},{6,4},{7,5},{8,10},{9,11},{10,... | collective-permute-start | bytes 12296 | tf_op jit(solution)/shard_map/ppermute | solution.py:283
  62.1 3.6 %collective-permute-start.19 = (f32[8,128]{1,0:T(8,128)S(1)}, f32[8,128]{1,0:T(8,128)S(1)}, u32[]{:S(2)}, u32[]{:S(2)}) collective-permute-start(f32[8,128]{1,0:T(8,128)S(1)} %add.45), channel_id=1, source_target_pairs={{0,4},{4,0},{1,5},{5,1},{2,6},{6,2},{3,7},{7,3},{8,12},{12,8},{9,1... | collective-permute-start | bytes 12296 | tf_op jit(solution)/shard_map/ppermute | solution.py:283
  65.7 3.6 %collective-permute-start.20 = (f32[8,128]{1,0:T(8,128)S(1)}, f32[8,128]{1,0:T(8,128)S(1)}, u32[]{:S(2)}, u32[]{:S(2)}) collective-permute-start(f32[8,128]{1,0:T(8,128)S(1)} %add.46), channel_id=1, source_target_pairs={{0,8},{8,0},{16,24},{24,16},{1,9},{9,1},{17,25},{25,17},{2,10},{10... | collective-permute-start | bytes 12296 | tf_op jit(solution)/shard_map/ppermute | solution.py:283
  69.3 4.5 %collective-permute-start.21 = (f32[8,128]{1,0:T(8,128)S(1)}, f32[8,128]{1,0:T(8,128)S(1)}, u32[]{:S(2)}, u32[]{:S(2)}) collective-permute-start(f32[8,128]{1,0:T(8,128)S(1)} %add.47), channel_id=1, source_target_pairs={{0,16},{8,24},{16,0},{24,8},{1,17},{9,25},{17,1},{25,9},{2,18},{10... | collective-permute-start | bytes 12296 | tf_op jit(solution)/shard_map/ppermute | solution.py:283

commit v2 on v1

--- a/solution.py
+++ b/solution.py
@@ -12,6 +12,7 @@
 NT = (((1,), (1,)), ((), ()))
 NN = (((1,), (0,)), ((), ()))
 VMEM_BYTES = 24 * 2**20
+GROUP = 4
 AXES = ("gx", "gx", "gz", "ta")
 
 
@@ -51,24 +52,43 @@
     return jnp.concatenate([value, value], axis=1)
 
 
-def local_products(box, field, links, own, back, mapped, low, chirality):
+def own_products(group, here, own, low):
+    rows, lanes = here[0].shape
+    zero = jnp.zeros((rows, lanes), F32)
+    left = [jnp.where(low, here[0], 0.0), jnp.where(low, 0.0, here[1]), zero, zero]
+    right = [zero, zero, jnp.where(low, here[2], 0.0), jnp.where(low, 0.0, here[3])]
+    blocks = jnp.concatenate(
+        [jnp.concatenate(left, axis=0), jnp.concatenate(right, axis=0)], axis=1
+    ).astype(BF16)
+    return lax.dot_general(blocks, own[group], NT, preferred_element_type=F32)
+
+
+def local_products(box, field, links, own, back, mapped, low, chirality, arrive=None):
     rows, lanes = field.shape[1:]
     half = lanes // 2
     zero = jnp.zeros((rows, lanes), F32)
-    for s in range(box.count):
-        ahead = [box.ahead(s, d) for d in range(4)]
-        part = [zero if a is None else field[a] for a in ahead]
-        here = field[s]
-        spread = jnp.concatenate(
-            [jnp.where(low, part[0], part[1]), jnp.where(low, part[2], part[3])], axis=1
-        ).astype(BF16)
-        total = lax.dot_general(here[:, :half].astype(BF16), own[s], NT, preferred_element_type=F32)
-        if any(a is not None for a in ahead):
-            total = total + lax.dot_general(spread, links[s], NT, preferred_element_type=F32)
-        mapped[s] = jnp.concatenate([total, jnp.zeros((rows, half), F32)], axis=1)
-        back[s] = lax.dot_general(
-            (chirality * here)[:, :half].astype(BF16), links[s], NN, preferred_element_type=F32
-        )
+    for g in range(box.count // GROUP):
+        if arrive is not None:
+            arrive(g)
+        sites = range(GROUP * g, GROUP * g + GROUP)
+        here = [field[s] for s in sites]
+        diagonal = own_products(g, here, own, low)
+        for i, s in enumerate(sites):
+            ahead = [box.ahead(s, d) for d in range(4)]
+            total = diagonal[i * rows : (i + 1) * rows]
+            if any(a is not None for a in ahead):
+                part = [zero if a is None else field[a] for a in ahead]
+                spread = jnp.concatenate(
+                    [jnp.where(low, part[0], part[1]), jnp.where(low, part[2], part[3])], axis=1
+                ).astype(BF16)
+                total = total + lax.dot_general(spread, links[s], NT, preferred_element_type=F32)
+            mapped[s] = jnp.concatenate([total, jnp.zeros((rows, half), F32)], axis=1)
+            back[s] = lax.dot_general(
+                (chirality * here[i])[:, :half].astype(BF16),
+                links[s],
+                NN,
+                preferred_element_type=F32,
+            )
     top = zero
     bottom = zero
     for s in range(box.count):
@@ -87,13 +107,13 @@
     return jnp.sum(top, axis=1, keepdims=True) / jnp.sum(bottom, axis=1, keepdims=True)
 
 
-def smooth(box, flips, field, links, own, outs, scratch):
+def smooth(box, flips, field, links, own, outs, scratch, arrive=None):
     update, image, sends = outs
     back_a, back_b, map_a, map_b, second = scratch
     rows, lanes = field.shape[1:]
     half = lanes // 2
     low, chirality = lane_tools(rows, lanes)
-    weight_a = local_products(box, field, links, own, back_a, map_a, low, chirality)
+    weight_a = local_products(box, field, links, own, back_a, map_a, low, chirality, arrive)
     for s in range(box.count):
         second[s] = field[s] - weight_a * map_a[s]
     weight_b = local_products(box, second, links, own, back_b, map_b, low, chirality)
@@ -126,15 +146,40 @@
             sends[d][1 - flip, j] = jnp.concatenate(block, axis=0).astype(BF16)
 
 
-def first_kernel(box, flips, rhs, own, hop, update, image, send0, send1, send2, send3, links, field, *scratch):
-    for s in range(box.count):
-        links[s] = jnp.concatenate([hop[d, s] for d in range(4)], axis=1)
+def first_kernel(
+    box, parts, flips, rhs_in, own_in, hop_in, *refs
+):
+    update, image, send0, send1, send2, send3, links, own = refs[:8]
+    field, back_a, back_b, map_a, map_b, second, rhs, own_raw, hop, sems = refs[8:]
+    each = box.count // parts
+    copies = [pltpu.make_async_copy(rhs_in, rhs, sems.at[2 * parts])]
+    for c in range(parts):
+        run = pl.ds(c * each, each)
+        copies.append(pltpu.make_async_copy(hop_in.at[:, run], hop.at[:, run], sems.at[2 * c]))
+        copies.append(pltpu.make_async_copy(own_in.at[run], own_raw.at[run], sems.at[2 * c + 1]))
+    for copy in copies:
+        copy.start()
+    copies[0].wait()
+    for s in range(box.count):
         field[s] = twice(rhs[s])
-    smooth(box, flips, field, links, own, (update, image, (send0, send1, send2, send3)), scratch)
+
+    def arrive(g):
+        if g * GROUP % each == 0:
+            c = g * GROUP // each
+            copies[2 * c + 1].wait()
+            copies[2 * c + 2].wait()
+        sites = range(GROUP * g, GROUP * g + GROUP)
+        own[g] = jnp.concatenate([own_raw[s] for s in sites], axis=1)
+        for s in sites:
+            links[s] = jnp.concatenate([hop[d, s] for d in range(4)], axis=1)
+
+    scratch = (back_a, back_b, map_a, map_b, second)
+    smooth(box, flips, field, links, own, (update, image, (send0, send1, send2, send3)), scratch, arrive)
 
 
 def second_kernel(box, flips, rhs, mapped, sums, links, own, update, image, send0, send1, send2, send3, field, *scratch):
-    alpha = sums[:, 0:1] / sums[:, 1:2]
+    top, square = unpacked_sums(sums, 2, mapped.shape[1])
+    alpha = top / square
     for s in range(box.count):
         field[s] = twice(rhs[s]) - alpha * mapped[s]
     smooth(box, flips, field, links, own, (update, image, (send0, send1, send2, send3)), scratch)
@@ -174,15 +219,31 @@
         mapped[s] = image[s] + extra + pltpu.roll(extra, half, 1)
 
 
-def packed_sums(values, rows, lanes):
+def sum_places(rows, lanes):
+    row = lax.broadcasted_iota(jnp.int32, (rows, lanes), 0)
     lane = lax.broadcasted_iota(jnp.int32, (rows, lanes), 1)
-    out = jnp.zeros((rows, lanes), F32)
+    return lane - row
+
+
+def packed_sums(values, out):
+    rows, lanes = values[0].shape
+    places = sum_places(rows, lanes)
+    spread = jnp.zeros((rows, lanes), F32)
     for k, value in enumerate(values):
-        out = jnp.where(lane == k, jnp.sum(value, axis=1, keepdims=True), out)
-    return out
-
-
-def third_kernel(box, flips, rhs, image, links, came0, came1, came2, came3, mapped, sums):
+        spread = jnp.where(places == k * rows, jnp.sum(value, axis=1, keepdims=True), spread)
+    out[...] = jnp.broadcast_to(jnp.sum(spread, axis=0, keepdims=True), out.shape)
+
+
+def unpacked_sums(sums, count, rows):
+    lanes = sums.shape[1]
+    total = jnp.broadcast_to(jnp.sum(sums[...], axis=0, keepdims=True), (rows, lanes))
+    places = sum_places(rows, lanes)
+    return [
+        jnp.sum(jnp.where(places == k * rows, total, 0.0), axis=1, keepdims=True) for k in range(count)
+    ]
+
+
+def third_kernel(box, flips, rhs, image, links, came3, came2, came1, came0, mapped, sums):
     rows, lanes = image.shape[1:]
     low, _ = lane_tools(rows, lanes)
     joined_halo(box, flips, image, links, (came0, came1, came2, came3), mapped, low)
@@ -193,14 +254,15 @@
         value = mapped[s]
         top = top + value * twice(rhs[s])
         bottom = bottom + value * value
-    sums[...] = packed_sums((top, bottom), rows, lanes)
-
-
-def fourth_kernel(box, flips, rhs, first, before, image, links, came0, came1, came2, came3, mapped, sums):
+    packed_sums((top, bottom), sums)
+
+
+def fourth_kernel(box, flips, rhs, first, before, image, links, came3, came2, came1, came0, mapped, sums):
     rows, lanes = image.shape[1:]
     low, _ = lane_tools(rows, lanes)
     joined_halo(box, flips, image, links, (came0, came1, came2, came3), mapped, low)
-    alpha = before[:, 0:1] / before[:, 1:2]
+    top, square = unpacked_sums(before, 2, rows)
+    alpha = top / square
     total = [jnp.zeros((rows, lanes), F32) for _ in range(4)]
     for s in range(box.count):
         old = first[s]
@@ -208,17 +270,17 @@
         remain = twice(rhs[s]) - alpha * old
         for k, product in enumerate((old * value, value * value, value * remain, old * remain)):
             total[k] = total[k] + product
-    sums[...] = packed_sums(total, rows, lanes)
+    packed_sums(total, sums)
 
 
 def last_kernel(box, rhs, update_a, map_a, update_b, map_b, sums_a, sums_b, solution_out, residual_out):
-    half = update_a.shape[2] // 2
-    square = sums_a[:, 1:2]
-    alpha = sums_a[:, 0:1] / square
-    beta = sums_b[:, 0:1] / square
-    top = sums_b[:, 2:3] - beta * sums_b[:, 3:4]
-    bottom = sums_b[:, 1:2] - 2.0 * beta * sums_b[:, 0:1] + beta * beta * square
-    step = top / bottom
+    rows, lanes = update_a.shape[1:]
+    half = lanes // 2
+    top, square = unpacked_sums(sums_a, 2, rows)
+    alpha = top / square
+    cross, norm, raw, old = unpacked_sums(sums_b, 4, rows)
+    beta = cross / square
+    step = (raw - beta * old) / (norm - 2.0 * beta * cross + beta * beta * square)
     for s in range(box.count):
         old = update_a[s][:, :half]
         solution_out[s] = alpha * old + step * (update_b[s][:, :half] - beta * old)
@@ -226,12 +288,11 @@
         residual_out[s] = rhs[s] - alpha * old - step * (map_b[s][:, :half] - beta * old)
 
 
-def call(body, outs, scratch, ins, flips=None):
+def call(body, outs, scratch, ins, flips=None, space=pltpu.VMEM):
     vmem = pl.BlockSpec(memory_space=pltpu.VMEM)
-    smem = pl.BlockSpec(memory_space=pltpu.SMEM)
-    specs = [vmem] * len(ins)
+    specs = [pl.BlockSpec(memory_space=space)] * len(ins)
     if flips is not None:
-        specs.insert(0, smem)
+        specs.insert(0, pl.BlockSpec(memory_space=pltpu.SMEM))
         ins = (flips, *ins)
     return pl.pallas_call(
         body,
@@ -256,7 +317,7 @@
 
 def exchange(sends):
     came = [None] * 4
-    for d in range(4):
+    for d in reversed(range(4)):
         axis, size, step, kind = plan(d)
         ring = range(size)
         if kind == "both":
@@ -272,8 +333,18 @@
     return came
 
 
+def device_count():
+    return lax.axis_size("gx") * lax.axis_size("gz") * lax.axis_size("ta")
+
+
+def sum_rows():
+    return device_count() if device_count() <= 64 else 1
+
+
 def mesh_sum(value):
-    for axis in ("ta", "gz", "gx"):
+    if sum_rows() > 1:
+        return lax.all_to_all(value, ("gx", "gz", "ta"), 0, 0, tiled=True)
+    for axis in ("gx", "gz", "ta"):
         size = lax.axis_size(axis)
         if size & (size - 1):
             value = lax.psum(value, axis)
@@ -310,9 +381,17 @@
     flips_in = jnp.stack(flips_in).astype(jnp.int32)
 
     full = jax.ShapeDtypeStruct((count, rows, lanes), F32)
-    small = jax.ShapeDtypeStruct((rows, lanes), F32)
+    small = jax.ShapeDtypeStruct((sum_rows(), lanes), F32)
     narrow = jax.ShapeDtypeStruct((count, rows, channels), F32)
     links_shape = jax.ShapeDtypeStruct((count, channels, 4 * channels), BF16)
+    own_shape = jax.ShapeDtypeStruct((count // GROUP, channels, GROUP * channels), BF16)
+    parts = extents[0] * extents[1]
+    raw = [
+        pltpu.VMEM(source.shape, F32),
+        pltpu.VMEM(own.shape, BF16),
+        pltpu.VMEM(hop.shape, BF16),
+        pltpu.SemaphoreType.DMA((2 * parts + 1,)),
+    ]
     send_shapes = [
         jax.ShapeDtypeStruct((2, len(box.rim(d, True)) // 4, 2 * rows, lanes), BF16) for d in range(4)
     ]
@@ -320,16 +399,17 @@
     back_scratch = pltpu.VMEM((count, rows, 4 * channels), F32)
     scratch = [field_scratch, back_scratch, back_scratch, field_scratch, field_scratch, field_scratch]
 
-    update_a, image_a, *sends, links = call(
-        functools.partial(first_kernel, box),
-        [full, full, *send_shapes, links_shape],
-        scratch,
-        (source, own, hop),
+    update_a, image_a, *sends, links, own = call(
+        functools.partial(first_kernel, box, parts),
+        [full, full, *send_shapes, links_shape, own_shape],
+        scratch + raw,
+        [pltpu.with_memory_space_constraint(a, pltpu.HBM) for a in (source, own, hop)],
         flips_out,
+        pltpu.HBM,
     )
     came = exchange(sends)
     map_a, sums_a = call(
-        functools.partial(third_kernel, box), [full, small], [], (source, image_a, links, *came), flips_in
+        functools.partial(third_kernel, box), [full, small], [], (source, image_a, links, *came[::-1]), flips_in
     )
     sums_a = mesh_sum(sums_a)
     update_b, image_b, *sends = call(
@@ -344,7 +424,7 @@
         functools.partial(fourth_kernel, box),
         [full, small],
         [],
-        (source, map_a, sums_a, image_b, links, *came),
+        (source, map_a, sums_a, image_b, links, *came[::-1]),
         flips_in,
     )
     sums_b = mesh_sum(sums_b)

time: 75.2 us -> 58.1 us (0.77)
  waiting for transfers between devices: 38.6 us -> 10.6 us
  blocking collectives: 0 us -> 20.1 us
  starting transfers between devices: 18.5 us -> 13.7 us
  local copies, waits for them, and re-layouts: 4.39 us -> 0.03 us
    ppermute x10 -> x0, waiting for transfers between devices: 28 us -> none  [mesh_sum(): lax.ppermute(value, axis, [(i, i ^ hop) for i in range(size)])]
    all_to_all x0 -> x2, blocking collectives: none -> 20.1 us  [mesh_sum(): return lax.all_to_all(value, ('gx', 'gz', 'ta'), 0, 0, tiled=True)]
    ppermute x10 -> x0, starting transfers between devices: 4.97 us -> none  [mesh_sum(): lax.ppermute(value, axis, [(i, i ^ hop) for i in range(size)])]
    unnamed x10 -> x2, local copies, waits for them, and re-layouts: 4.37 us -> 0.01 us
  transfers between devices with their start and end apart: 22 -> 12, of which waited for: 15 -> 5; matrix products, arithmetic and copies ran while one was open for 0% -> 0% of each run, Pallas kernels for 0% -> 0%
where the time goes in v2:
time: 58.1 us; the launch traced here: 57.9 us
  blocking collectives  20.1 us (35%)
  starting transfers between devices  13.7 us (24%)
  Pallas kernels  12.6 us (22%)
  waiting for transfers between devices  10.6 us (18%)
  between operations  0.75 us (1%)
    all_to_all x2, blocking collectives, mesh_sum(): return lax.all_to_all(value, ('gx', 'gz', 'ta'), 0, 0, tiled=True)  20.1 us
    pallas_call x5, Pallas kernels, call(): pl.pallas_call(body, out_shape=outs, in_specs=specs, out_specs=[vmem] * l...  12.6 us
    ppermute x4, starting transfers between devices, exchange(): lax.ppermute(sends[d][1], axis, [(i, (i + 1 if i % 2 else i - 1) % size)...  7.18 us
    ppermute x4, waiting for transfers between devices, exchange(): lax.ppermute(sends[d][1], axis, [(i, (i + 1 if i % 2 else i - 1) % size)...  5.81 us
    ppermute x4, waiting for transfers between devices, exchange(): lax.ppermute(sends[d], axis, [(i, (i + step) % size) for i in ring])  4.32 us
    ppermute x4, starting transfers between devices, exchange(): lax.ppermute(sends[d], axis, [(i, (i + step) % size) for i in ring])  3.74 us
    ppermute x4, starting transfers between devices, exchange(): even = lax.ppermute(sends[d][0], axis, [(i, i ^ 1) for i in ring])  2.75 us
  transfers between devices with their start and end apart: 12, of which 5 were waited for; matrix products, arithmetic and copies ran while one was open for 0% of the time, Pallas kernels for 0%

profile of v2, /device:TPU:0, one launch (start us, length us, event | category | flops | bytes accessed | tf_op | source)
XLA Modules:
  0.0 57.9 jit_solution(1028104891473796742)
XLA Ops:
  0.6 0.0 copy-start
  0.7 0.1 fusion.flips
  0.7 5.4 %shard_map.50 = (f32[64,8,128]{2,1,0:T(8,128)S(1)}, f32[64,8,128]{2,1,0:T(8,128)S(1)}, bf16[2,8,16,128]{3,2,1,0:T(8,128)(2,1)S(1)}, bf16[2,8,16,128]{3,2,1,0:T(8...) custom-call(s32[4]{0:T(128)S(1)} %fusion.flips, ...), custom_call_target="tpu_custom_call" | custom-call | tf_op jit(solution)/shard_map/pallas_call | solution.py:297
  6.2 0.5 collective-permute-start
  6.7 2.6 %collective-permute-start.1 = (bf16[4,16,128]{2,1,0:T(8,128)(2,1)S(1)}, bf16[4,16,128]{2,1,0:T(8,128)(2,1)S(1)}, u32[]{:S(2)}, u32[]{:S(2)}) collective-permute-start(bf16[4,16,128]{2,1,0:T(8,128)(2,1)S(1)} %get-tuple-element.49), channel_id=1, source_target_pairs={{0,3},{1,2},{2,1},{3,0},{4,7},{5,6},{6,5},{7,4},{8,11},{9,10},{10,... | collective-permute-start | bytes 49160 | tf_op jit(solution)/shard_map/ppermute | solution.py:327
  9.4 1.5 %collective-permute-start.2 = (bf16[2,4,16,128]{3,2,1,0:T(8,128)(2,1)S(1)}, bf16[2,4,16,128]{3,2,1,0:T(8,128)(2,1)S(1)}, u32[]{:S(2)}, u32[]{:S(2)}) collective-permute-start(bf16[2,4,16,128]{3,2,1,0:T(8,128)(2,1)S(1)} %get-tuple-element.26), channel_id=1, source_target_pairs={{0,4},{4,0},{1,5},{5,1},{2,6},{6,2},{3,7},{7,3},{8,12},{12,8},{9,1... | collective-permute-start | bytes 98312 | tf_op jit(solution)/shard_map/ppermute | solution.py:324
  10.9 1.6 %collective-permute-start.3 = (bf16[8,16,128]{2,1,0:T(8,128)(2,1)S(1)}, bf16[8,16,128]{2,1,0:T(8,128)(2,1)S(1)}, u32[]{:S(2)}, u32[]{:S(2)}) collective-permute-start(bf16[8,16,128]{2,1,0:T(8,128)(2,1)S(1)} %get-tuple-element.44), channel_id=1, source_target_pairs={{0,8},{8,0},{16,24},{24,16},{1,9},{9,1},{17,25},{25,17},{2,10},{10... | collective-permute-start | bytes 98312 | tf_op jit(solution)/shard_map/ppermute | solution.py:326
  12.4 2.5 %collective-permute-start.4 = (bf16[8,16,128]{2,1,0:T(8,128)(2,1)S(1)}, bf16[8,16,128]{2,1,0:T(8,128)(2,1)S(1)}, u32[]{:S(2)}, u32[]{:S(2)}) collective-permute-start(bf16[8,16,128]{2,1,0:T(8,128)(2,1)S(1)} %get-tuple-element.45), channel_id=1, source_target_pairs={{0,24},{8,16},{16,8},{24,0},{1,25},{9,17},{17,9},{25,1},{2,26},{10... | collective-permute-start | bytes 98312 | tf_op jit(solution)/shard_map/ppermute | solution.py:327
  14.9 0.1 fusion.1.flips
  15.0 0.0 collective-permute-done
  15.0 0.1 collective-permute-start.5
  15.1 0.0 collective-permute-done.1
  15.1 0.0 collective-permute-done.3
  15.1 3.4 %collective-permute-done.4 = bf16[8,16,128]{2,1,0:T(8,128)(2,1)S(1)} collective-permute-done((bf16[8,16,128]{2,1,0:T(8,128)(2,1)S(1)}, bf16[8,16,128]{2,1,0:T(8,128)(2,1)S(1)}, u32[]{:S(2)}, u32[]{:S(2)}) %collective-permute-start.4) | collective-permute-done | bytes 32800 | tf_op jit(solution)/shard_map/ppermute | solution.py:327
  18.6 0.0 collective-permute-done.2.came2
  18.6 2.3 %collective-permute-done.5.came0 = bf16[2,8,16,128]{3,2,1,0:T(8,128)(2,1)S(1)} collective-permute-done((bf16[2,8,16,128]{3,2,1,0:T(8,128)(2,1)S(1)}, bf16[2,8,16,128]{3,2,1,0:T(8,128)(2,1)S(1)}, u32[]{:S(2)}, u32[]{:S(2)}) %collective-permute-start.5) | collective-permute-done | bytes 65568 | tf_op jit(solution)/shard_map/ppermute | solution.py:324
  20.9 0.0 copy-done
  20.9 1.3 %shard_map.51 = (f32[64,8,128]{2,1,0:T(8,128)S(1)}, f32[32,128]{1,0:T(8,128)S(1)}) custom-call(s32[4]{0:T(128)S(1)} %fusion.1.flips, f32[64,8,64]{2,1,0:T(8,128)S(1)} %bitcast.42, f32[64,8,128]{2,1,0:T(8,128)S(1)} %get-tuple-element.23.image, bf16[64,64,256]{2,1,0:T(8,128)(2,1)S(1)} %get-tuple-element.24.links, ...), custom_call_target="tpu_custom_call" | custom-call | tf_op jit(solution)/shard_map/pallas_call | solution.py:297
  22.2 9.1 %all_to_all.22 = f32[32,1,128]{2,1,0:T(1,128)S(1)} all-to-all(f32[32,1,128]{2,1,0:T(1,128)S(1)} %bitcast.51), channel_id=1, replica_groups=mesh['gx'=4,'gz'=2,'ta'=4] {'gx','gz','ta'}, dimensions={0} | all-to-all | bytes 32768 | tf_op jit(solution)/shard_map/all_to_all | solution.py:346
  31.3 3.5 %shard_map.52 = (f32[64,8,128]{2,1,0:T(8,128)S(1)}, f32[64,8,128]{2,1,0:T(8,128)S(1)}, bf16[2,8,16,128]{3,2,1,0:T(8,128)(2,1)S(1)}, bf16[2,8,16,128]{3,2,1,0:T(8...) custom-call(s32[4]{0:T(128)S(1)} %fusion.flips, f32[64,8,64]{2,1,0:T(8,128)S(1)} %bitcast.43, ...), custom_call_target="tpu_custom_call" | custom-call | tf_op jit(solution)/shard_map/pallas_call | solution.py:297
  34.8 0.1 collective-permute-start.6
  34.9 0.6 %collective-permute-start.7 = (bf16[4,16,128]{2,1,0:T(8,128)(2,1)S(1)}, bf16[4,16,128]{2,1,0:T(8,128)(2,1)S(1)}, u32[]{:S(2)}, u32[]{:S(2)}) collective-permute-start(bf16[4,16,128]{2,1,0:T(8,128)(2,1)S(1)} %get-tuple-element.47), channel_id=1, source_target_pairs={{0,3},{1,2},{2,1},{3,0},{4,7},{5,6},{6,5},{7,4},{8,11},{9,10},{10,... | collective-permute-start | bytes 49160 | tf_op jit(solution)/shard_map/ppermute | solution.py:327
  35.6 0.6 %collective-permute-start.8 = (bf16[2,4,16,128]{3,2,1,0:T(8,128)(2,1)S(1)}, bf16[2,4,16,128]{3,2,1,0:T(8,128)(2,1)S(1)}, u32[]{:S(2)}, u32[]{:S(2)}) collective-permute-start(bf16[2,4,16,128]{3,2,1,0:T(8,128)(2,1)S(1)} %get-tuple-element.35), channel_id=1, source_target_pairs={{0,4},{4,0},{1,5},{5,1},{2,6},{6,2},{3,7},{7,3},{8,12},{12,8},{9,1... | collective-permute-start | bytes 98312 | tf_op jit(solution)/shard_map/ppermute | solution.py:324
  36.2 0.6 %collective-permute-start.9 = (bf16[8,16,128]{2,1,0:T(8,128)(2,1)S(1)}, bf16[8,16,128]{2,1,0:T(8,128)(2,1)S(1)}, u32[]{:S(2)}, u32[]{:S(2)}) collective-permute-start(bf16[8,16,128]{2,1,0:T(8,128)(2,1)S(1)} %get-tuple-element.42), channel_id=1, source_target_pairs={{0,8},{8,0},{16,24},{24,16},{1,9},{9,1},{17,25},{25,17},{2,10},{10... | collective-permute-start | bytes 98312 | tf_op jit(solution)/shard_map/ppermute | solution.py:326
  36.8 1.4 %collective-permute-start.10 = (bf16[8,16,128]{2,1,0:T(8,128)(2,1)S(1)}, bf16[8,16,128]{2,1,0:T(8,128)(2,1)S(1)}, u32[]{:S(2)}, u32[]{:S(2)}) collective-permute-start(bf16[8,16,128]{2,1,0:T(8,128)(2,1)S(1)} %get-tuple-element.43), channel_id=1, source_target_pairs={{0,24},{8,16},{16,8},{24,0},{1,25},{9,17},{17,9},{25,1},{2,26},{10... | collective-permute-start | bytes 98312 | tf_op jit(solution)/shard_map/ppermute | solution.py:327
  38.2 0.0 collective-permute-done.6
  38.2 1.5 %collective-permute-start.11 = (bf16[2,8,16,128]{3,2,1,0:T(8,128)(2,1)S(1)}, bf16[2,8,16,128]{3,2,1,0:T(8,128)(2,1)S(1)}, u32[]{:S(2)}, u32[]{:S(2)}) collective-permute-start(bf16[2,8,16,128]{3,2,1,0:T(8,128)(2,1)S(1)} %get-tuple-element.37), channel_id=1, source_target_pairs={{0,16},{8,24},{16,0},{24,8},{1,17},{9,25},{17,1},{25,9},{2,18},{10... | collective-permute-start | bytes 196616 | tf_op jit(solution)/shard_map/ppermute | solution.py:324
  39.7 0.0 collective-permute-done.7
  39.7 0.4 collective-permute-done.9
  40.1 2.4 %collective-permute-done.10 = bf16[8,16,128]{2,1,0:T(8,128)(2,1)S(1)} collective-permute-done((bf16[8,16,128]{2,1,0:T(8,128)(2,1)S(1)}, bf16[8,16,128]{2,1,0:T(8,128)(2,1)S(1)}, u32[]{:S(2)}, u32[]{:S(2)}) %collective-permute-start.10) | collective-permute-done | bytes 32800 | tf_op jit(solution)/shard_map/ppermute | solution.py:327
  42.5 0.0 collective-permute-done.8.came2
  42.5 2.0 %collective-permute-done.11.came0 = bf16[2,8,16,128]{3,2,1,0:T(8,128)(2,1)S(1)} collective-permute-done((bf16[2,8,16,128]{3,2,1,0:T(8,128)(2,1)S(1)}, bf16[2,8,16,128]{3,2,1,0:T(8,128)(2,1)S(1)}, u32[]{:S(2)}, u32[]{:S(2)}) %collective-permute-start.11) | collective-permute-done | bytes 65568 | tf_op jit(solution)/shard_map/ppermute | solution.py:324
  44.5 1.4 %shard_map.53 = (f32[64,8,128]{2,1,0:T(8,128)S(1)}, f32[32,128]{1,0:T(8,128)S(1)}) custom-call(s32[4]{0:T(128)S(1)} %fusion.1.flips, f32[64,8,64]{2,1,0:T(8,128)S(1)} %bitcast.44, f32[64,8,128]{2,1,0:T(8,128)S(1)} %get-tuple-element.29.mapped.first.map_a, f32[32,128]{1,0:T(8,128)S(1)} %bitcast.47, f32[64,8,128]{2,1,0:T(8,128)S(1)} %get-tuple-element.33.image, ...), custom_call_target="tpu_custom_call" | custom-call | tf_op jit(solution)/shard_map/pallas_call | solution.py:297
  45.9 11.0 %all_to_all.23 = f32[32,1,128]{2,1,0:T(1,128)S(1)} all-to-all(f32[32,1,128]{2,1,0:T(1,128)S(1)} %bitcast.50), channel_id=1, replica_groups=mesh['gx'=4,'gz'=2,'ta'=4] {'gx','gz','ta'}, dimensions={0} | all-to-all | bytes 32768 | tf_op jit(solution)/shard_map/all_to_all | solution.py:346
  56.9 1.0 %shard_map.54 = (f32[64,8,64]{2,1,0:T(8,128)}, f32[64,8,64]{2,1,0:T(8,128)}) custom-call(f32[64,8,64]{2,1,0:T(8,128)S(1)} %bitcast.45, f32[64,8,128]{2,1,0:T(8,128)S(1)} %get-tuple-element.22.update_a, f32[64,8,128]{2,1,0:T(8,128)S(1)} %get-tuple-element.29.mapped.first.map_a, f32[64,8,128]{2,1,0:T(8,128)S(1)} %get-tuple-element.32.update_b, ...), custom_call_target="tpu_custom_call" | custom-call | tf_op jit(solution)/shard_map/pallas_call | solution.py:297
  (8 shorter events, 0.0 us)
Async XLA Ops:
  0.6 20.3 %copy-start = (f32[1,2,2,4,4,8,64]{6,5,4,3,2,1,0:T(8,128)S(1)}, f32[1,2,2,4,4,8,64]{6,5,4,3,2,1,0:T(8,128)}, u32[]{:S(2)}) copy-start(f32[1,2,2,4,4,8,64]{6,5,4,3,2,1,0:T(8,128)} %param.3) | copy-start | bytes 393220
  6.2 8.8 %collective-permute-start = (bf16[4,16,128]{2,1,0:T(8,128)(2,1)S(1)}, bf16[4,16,128]{2,1,0:T(8,128)(2,1)S(1)}, u32[]{:S(2)}, u32[]{:S(2)}) collective-permute-start(bf16[4,16,128]{2,1,0:T(8,128)(2,1)S(1)} %get-tuple-element.48), channel_id=1, source_target_pairs={{0,1},{1,0},{2,3},{3,2},{4,5},{5,4},{6,7},{7,6},{8,9},{9,8},{10,11... | collective-permute-start | bytes 49160 | tf_op jit(solution)/shard_map/ppermute | solution.py:326
  6.7 8.4 %collective-permute-start.1 = (bf16[4,16,128]{2,1,0:T(8,128)(2,1)S(1)}, bf16[4,16,128]{2,1,0:T(8,128)(2,1)S(1)}, u32[]{:S(2)}, u32[]{:S(2)}) collective-permute-start(bf16[4,16,128]{2,1,0:T(8,128)(2,1)S(1)} %get-tuple-element.49), channel_id=1, source_target_pairs={{0,3},{1,2},{2,1},{3,0},{4,7},{5,6},{6,5},{7,4},{8,11},{9,10},{10,... | collective-permute-start | bytes 49160 | tf_op jit(solution)/shard_map/ppermute | solution.py:327
  9.4 9.2 %collective-permute-start.2 = (bf16[2,4,16,128]{3,2,1,0:T(8,128)(2,1)S(1)}, bf16[2,4,16,128]{3,2,1,0:T(8,128)(2,1)S(1)}, u32[]{:S(2)}, u32[]{:S(2)}) collective-permute-start(bf16[2,4,16,128]{3,2,1,0:T(8,128)(2,1)S(1)} %get-tuple-element.26), channel_id=1, source_target_pairs={{0,4},{4,0},{1,5},{5,1},{2,6},{6,2},{3,7},{7,3},{8,12},{12,8},{9,1... | collective-permute-start | bytes 98312 | tf_op jit(solution)/shard_map/ppermute | solution.py:324
  10.9 4.3 %collective-permute-start.3 = (bf16[8,16,128]{2,1,0:T(8,128)(2,1)S(1)}, bf16[8,16,128]{2,1,0:T(8,128)(2,1)S(1)}, u32[]{:S(2)}, u32[]{:S(2)}) collective-permute-start(bf16[8,16,128]{2,1,0:T(8,128)(2,1)S(1)} %get-tuple-element.44), channel_id=1, source_target_pairs={{0,8},{8,0},{16,24},{24,16},{1,9},{9,1},{17,25},{25,17},{2,10},{10... | collective-permute-start | bytes 98312 | tf_op jit(solution)/shard_map/ppermute | solution.py:326
  12.4 6.1 %collective-permute-start.4 = (bf16[8,16,128]{2,1,0:T(8,128)(2,1)S(1)}, bf16[8,16,128]{2,1,0:T(8,128)(2,1)S(1)}, u32[]{:S(2)}, u32[]{:S(2)}) collective-permute-start(bf16[8,16,128]{2,1,0:T(8,128)(2,1)S(1)} %get-tuple-element.45), channel_id=1, source_target_pairs={{0,24},{8,16},{16,8},{24,0},{1,25},{9,17},{17,9},{25,1},{2,26},{10... | collective-permute-start | bytes 98312 | tf_op jit(solution)/shard_map/ppermute | solution.py:327
  15.0 5.9 %collective-permute-start.5 = (bf16[2,8,16,128]{3,2,1,0:T(8,128)(2,1)S(1)}, bf16[2,8,16,128]{3,2,1,0:T(8,128)(2,1)S(1)}, u32[]{:S(2)}, u32[]{:S(2)}) collective-permute-start(bf16[2,8,16,128]{3,2,1,0:T(8,128)(2,1)S(1)} %get-tuple-element.28), channel_id=1, source_target_pairs={{0,16},{8,24},{16,0},{24,8},{1,17},{9,25},{17,1},{25,9},{2,18},{10... | collective-permute-start | bytes 196616 | tf_op jit(solution)/shard_map/ppermute | solution.py:324
  34.8 3.4 %collective-permute-start.6 = (bf16[4,16,128]{2,1,0:T(8,128)(2,1)S(1)}, bf16[4,16,128]{2,1,0:T(8,128)(2,1)S(1)}, u32[]{:S(2)}, u32[]{:S(2)}) collective-permute-start(bf16[4,16,128]{2,1,0:T(8,128)(2,1)S(1)} %get-tuple-element.46), channel_id=1, source_target_pairs={{0,1},{1,0},{2,3},{3,2},{4,5},{5,4},{6,7},{7,6},{8,9},{9,8},{10,11... | collective-permute-start | bytes 49160 | tf_op jit(solution)/shard_map/ppermute | solution.py:326
  34.9 4.8 %collective-permute-start.7 = (bf16[4,16,128]{2,1,0:T(8,128)(2,1)S(1)}, bf16[4,16,128]{2,1,0:T(8,128)(2,1)S(1)}, u32[]{:S(2)}, u32[]{:S(2)}) collective-permute-start(bf16[4,16,128]{2,1,0:T(8,128)(2,1)S(1)} %get-tuple-element.47), channel_id=1, source_target_pairs={{0,3},{1,2},{2,1},{3,0},{4,7},{5,6},{6,5},{7,4},{8,11},{9,10},{10,... | collective-permute-start | bytes 49160 | tf_op jit(solution)/shard_map/ppermute | solution.py:327
  35.6 7.0 %collective-permute-start.8 = (bf16[2,4,16,128]{3,2,1,0:T(8,128)(2,1)S(1)}, bf16[2,4,16,128]{3,2,1,0:T(8,128)(2,1)S(1)}, u32[]{:S(2)}, u32[]{:S(2)}) collective-permute-start(bf16[2,4,16,128]{3,2,1,0:T(8,128)(2,1)S(1)} %get-tuple-element.35), channel_id=1, source_target_pairs={{0,4},{4,0},{1,5},{5,1},{2,6},{6,2},{3,7},{7,3},{8,12},{12,8},{9,1... | collective-permute-start | bytes 98312 | tf_op jit(solution)/shard_map/ppermute | solution.py:324
  36.2 3.9 %collective-permute-start.9 = (bf16[8,16,128]{2,1,0:T(8,128)(2,1)S(1)}, bf16[8,16,128]{2,1,0:T(8,128)(2,1)S(1)}, u32[]{:S(2)}, u32[]{:S(2)}) collective-permute-start(bf16[8,16,128]{2,1,0:T(8,128)(2,1)S(1)} %get-tuple-element.42), channel_id=1, source_target_pairs={{0,8},{8,0},{16,24},{24,16},{1,9},{9,1},{17,25},{25,17},{2,10},{10... | collective-permute-start | bytes 98312 | tf_op jit(solution)/shard_map/ppermute | solution.py:326
  36.8 5.7 %collective-permute-start.10 = (bf16[8,16,128]{2,1,0:T(8,128)(2,1)S(1)}, bf16[8,16,128]{2,1,0:T(8,128)(2,1)S(1)}, u32[]{:S(2)}, u32[]{:S(2)}) collective-permute-start(bf16[8,16,128]{2,1,0:T(8,128)(2,1)S(1)} %get-tuple-element.43), channel_id=1, source_target_pairs={{0,24},{8,16},{16,8},{24,0},{1,25},{9,17},{17,9},{25,1},{2,26},{10... | collective-permute-start | bytes 98312 | tf_op jit(solution)/shard_map/ppermute | solution.py:327
  38.2 6.3 %collective-permute-start.11 = (bf16[2,8,16,128]{3,2,1,0:T(8,128)(2,1)S(1)}, bf16[2,8,16,128]{3,2,1,0:T(8,128)(2,1)S(1)}, u32[]{:S(2)}, u32[]{:S(2)}) collective-permute-start(bf16[2,8,16,128]{3,2,1,0:T(8,128)(2,1)S(1)} %get-tuple-element.37), channel_id=1, source_target_pairs={{0,16},{8,24},{16,0},{24,8},{1,17},{9,25},{17,1},{25,9},{2,18},{10... | collective-permute-start | bytes 196616 | tf_op jit(solution)/shard_map/ppermute | solution.py:324

commit v3 on v2

--- a/solution.py
+++ b/solution.py
@@ -315,6 +315,12 @@
     return axis, size, step, "shift"
 
 
+def message_tiles(box):
+    tiles = [len(box.rim(d, True)) // 4 for d in range(4)]
+    longest = 2 * max(tiles[:2])
+    return tiles[:2] + [longest // 2 + 1, longest + 1]
+
+
 def exchange(sends):
     came = [None] * 4
     for d in reversed(range(4)):
@@ -393,7 +399,7 @@
         pltpu.SemaphoreType.DMA((2 * parts + 1,)),
     ]
     send_shapes = [
-        jax.ShapeDtypeStruct((2, len(box.rim(d, True)) // 4, 2 * rows, lanes), BF16) for d in range(4)
+        jax.ShapeDtypeStruct((2, tiles, 2 * rows, lanes), BF16) for tiles in message_tiles(box)
     ]
     field_scratch = pltpu.VMEM((count, rows, lanes), F32)
     back_scratch = pltpu.VMEM((count, rows, 4 * channels), F32)

time: 58.1 us -> 54.1 us (0.931)
  waiting for transfers between devices: 10.6 us -> 5.87 us
  blocking collectives: 20.1 us -> 20.7 us
    ppermute x4, waiting for transfers between devices: 4.32 us -> 0.39 us  [exchange(): lax.ppermute(sends[d], axis, [(i, (i + step) % size) for i in ring])]
    ppermute x4, starting transfers between devices: 2.75 us -> 3.87 us  [exchange(): even = lax.ppermute(sends[d][0], axis, [(i, i ^ 1) for i in ring])]
    ppermute x4, starting transfers between devices: 7.18 us -> 6.3 us  [exchange(): lax.ppermute(sends[d][1], axis, [(i, (i + 1 if i % 2 else i - 1) % size)...]
    all_to_all x2, blocking collectives: 20.1 us -> 20.7 us  [mesh_sum(): return lax.all_to_all(value, ('gx', 'gz', 'ta'), 0, 0, tiled=True)]
  transfers between devices with their start and end apart: 12 -> 12, of which waited for: 5 -> 6; matrix products, arithmetic and copies ran while one was open for 0% -> 0% of each run, Pallas kernels for 0% -> 0%
where the time goes in v3:
time: 54.1 us; the launch traced here: 54 us
  blocking collectives  20.7 us (38%)
  starting transfers between devices  13.8 us (26%)
  Pallas kernels  12.6 us (23%)
  waiting for transfers between devices  5.87 us (11%)
  between operations  0.76 us (1%)
    all_to_all x2, blocking collectives, mesh_sum(): return lax.all_to_all(value, ('gx', 'gz', 'ta'), 0, 0, tiled=True)  20.7 us
    pallas_call x5, Pallas kernels, call(): pl.pallas_call(body, out_shape=outs, in_specs=specs, out_specs=[vmem] * l...  12.6 us
    ppermute x4, starting transfers between devices, exchange(): lax.ppermute(sends[d][1], axis, [(i, (i + 1 if i % 2 else i - 1) % size)...  6.3 us
    ppermute x4, waiting for transfers between devices, exchange(): lax.ppermute(sends[d][1], axis, [(i, (i + 1 if i % 2 else i - 1) % size)...  5.47 us
    ppermute x4, starting transfers between devices, exchange(): even = lax.ppermute(sends[d][0], axis, [(i, i ^ 1) for i in ring])  3.87 us
    ppermute x4, starting transfers between devices, exchange(): lax.ppermute(sends[d], axis, [(i, (i + step) % size) for i in ring])  3.6 us
  transfers between devices with their start and end apart: 12, of which 6 were waited for; matrix products, arithmetic and copies ran while one was open for 0% of the time, Pallas kernels for 0%

profile of v3, /device:TPU:0, one launch (start us, length us, event | category | flops | bytes accessed | tf_op | source)
XLA Modules:
  0.0 54.0 jit_solution(4725386869047740037)
XLA Ops:
  0.6 0.0 copy-start
  0.7 0.1 fusion.flips
  0.7 5.4 %shard_map.50 = (f32[64,8,128]{2,1,0:T(8,128)S(1)}, f32[64,8,128]{2,1,0:T(8,128)S(1)}, bf16[2,8,16,128]{3,2,1,0:T(8,128)(2,1)S(1)}, bf16[2,8,16,128]{3,2,1,0:T(8...) custom-call(s32[4]{0:T(128)S(1)} %fusion.flips, ...), custom_call_target="tpu_custom_call" | custom-call | tf_op jit(solution)/shard_map/pallas_call | solution.py:297
  6.2 3.1 %collective-permute-start.3 = (bf16[8,16,128]{2,1,0:T(8,128)(2,1)S(1)}, bf16[8,16,128]{2,1,0:T(8,128)(2,1)S(1)}, u32[]{:S(2)}, u32[]{:S(2)}) collective-permute-start(bf16[8,16,128]{2,1,0:T(8,128)(2,1)S(1)} %get-tuple-element.48), channel_id=1, source_target_pairs={{0,8},{8,0},{16,24},{24,16},{1,9},{9,1},{17,25},{25,17},{2,10},{10... | collective-permute-start | bytes 98312 | tf_op jit(solution)/shard_map/ppermute | solution.py:332
  9.3 2.5 %collective-permute-start.4 = (bf16[8,16,128]{2,1,0:T(8,128)(2,1)S(1)}, bf16[8,16,128]{2,1,0:T(8,128)(2,1)S(1)}, u32[]{:S(2)}, u32[]{:S(2)}) collective-permute-start(bf16[8,16,128]{2,1,0:T(8,128)(2,1)S(1)} %get-tuple-element.49), channel_id=1, source_target_pairs={{0,24},{8,16},{16,8},{24,0},{1,25},{9,17},{17,9},{25,1},{2,26},{10... | collective-permute-start | bytes 98312 | tf_op jit(solution)/shard_map/ppermute | solution.py:333
  11.8 0.1 collective-permute-start.5
  11.9 1.5 %collective-permute-start.2 = (bf16[2,9,16,128]{3,2,1,0:T(8,128)(2,1)S(1)}, bf16[2,9,16,128]{3,2,1,0:T(8,128)(2,1)S(1)}, u32[]{:S(2)}, u32[]{:S(2)}) collective-permute-start(bf16[2,9,16,128]{3,2,1,0:T(8,128)(2,1)S(1)} %get-tuple-element.26), channel_id=1, source_target_pairs={{0,4},{4,0},{1,5},{5,1},{2,6},{6,2},{3,7},{7,3},{8,12},{12,8},{9,1... | collective-permute-start | bytes 221192 | tf_op jit(solution)/shard_map/ppermute | solution.py:330
  13.4 0.1 collective-permute-start
  13.5 0.1 fusion.1.flips
  13.6 0.0 collective-permute-done.3
  13.6 1.6 %collective-permute-start.1 = (bf16[17,16,128]{2,1,0:T(8,128)(2,1)S(1)}, bf16[17,16,128]{2,1,0:T(8,128)(2,1)S(1)}, u32[]{:S(2)}, u32[]{:S(2)}) collective-permute-start(bf16[17,16,128]{2,1,0:T(8,128)(2,1)S(1)} %get-tuple-element.45), channel_id=1, source_target_pairs={{0,3},{1,2},{2,1},{3,0},{4,7},{5,6},{6,5},{7,4},{8,11},{9,10},{10,... | collective-permute-start | bytes 208904 | tf_op jit(solution)/shard_map/ppermute | solution.py:333
  15.2 0.3 collective-permute-done.4
  15.5 0.0 collective-permute-done
  15.5 1.9 %collective-permute-done.1 = bf16[17,16,128]{2,1,0:T(8,128)(2,1)S(1)} collective-permute-done((bf16[17,16,128]{2,1,0:T(8,128)(2,1)S(1)}, bf16[17,16,128]{2,1,0:T(8,128)(2,1)S(1)}, u32[]{:S(2)}, u32[]{:S(2)}) %collective-permute-start.1) | collective-permute-done | bytes 69664 | tf_op jit(solution)/shard_map/ppermute | solution.py:333
  17.4 0.2 collective-permute-done.5.came0
  17.7 0.0 collective-permute-done.2.came2
  17.7 0.0 copy-done
  17.7 1.3 %shard_map.51 = (f32[64,8,128]{2,1,0:T(8,128)S(1)}, f32[32,128]{1,0:T(8,128)S(1)}) custom-call(s32[4]{0:T(128)S(1)} %fusion.1.flips, f32[64,8,64]{2,1,0:T(8,128)S(1)} %bitcast.42, f32[64,8,128]{2,1,0:T(8,128)S(1)} %get-tuple-element.23.image, bf16[64,64,256]{2,1,0:T(8,128)(2,1)S(1)} %get-tuple-element.24.links, ...), custom_call_target="tpu_custom_call" | custom-call | tf_op jit(solution)/shard_map/pallas_call | solution.py:297
  19.0 11.1 %all_to_all.22 = f32[32,1,128]{2,1,0:T(1,128)S(1)} all-to-all(f32[32,1,128]{2,1,0:T(1,128)S(1)} %bitcast.51), channel_id=1, replica_groups=mesh['gx'=4,'gz'=2,'ta'=4] {'gx','gz','ta'}, dimensions={0} | all-to-all | bytes 32768 | tf_op jit(solution)/shard_map/all_to_all | solution.py:352
  30.1 3.5 %shard_map.52 = (f32[64,8,128]{2,1,0:T(8,128)S(1)}, f32[64,8,128]{2,1,0:T(8,128)S(1)}, bf16[2,8,16,128]{3,2,1,0:T(8,128)(2,1)S(1)}, bf16[2,8,16,128]{3,2,1,0:T(8...) custom-call(s32[4]{0:T(128)S(1)} %fusion.flips, f32[64,8,64]{2,1,0:T(8,128)S(1)} %bitcast.43, ...), custom_call_target="tpu_custom_call" | custom-call | tf_op jit(solution)/shard_map/pallas_call | solution.py:297
  33.6 0.6 %collective-permute-start.9 = (bf16[8,16,128]{2,1,0:T(8,128)(2,1)S(1)}, bf16[8,16,128]{2,1,0:T(8,128)(2,1)S(1)}, u32[]{:S(2)}, u32[]{:S(2)}) collective-permute-start(bf16[8,16,128]{2,1,0:T(8,128)(2,1)S(1)} %get-tuple-element.46), channel_id=1, source_target_pairs={{0,8},{8,0},{16,24},{24,16},{1,9},{9,1},{17,25},{25,17},{2,10},{10... | collective-permute-start | bytes 98312 | tf_op jit(solution)/shard_map/ppermute | solution.py:332
  34.3 1.5 %collective-permute-start.10 = (bf16[8,16,128]{2,1,0:T(8,128)(2,1)S(1)}, bf16[8,16,128]{2,1,0:T(8,128)(2,1)S(1)}, u32[]{:S(2)}, u32[]{:S(2)}) collective-permute-start(bf16[8,16,128]{2,1,0:T(8,128)(2,1)S(1)} %get-tuple-element.47), channel_id=1, source_target_pairs={{0,24},{8,16},{16,8},{24,0},{1,25},{9,17},{17,9},{25,1},{2,26},{10... | collective-permute-start | bytes 98312 | tf_op jit(solution)/shard_map/ppermute | solution.py:333
  35.8 1.4 %collective-permute-start.11 = (bf16[2,8,16,128]{3,2,1,0:T(8,128)(2,1)S(1)}, bf16[2,8,16,128]{3,2,1,0:T(8,128)(2,1)S(1)}, u32[]{:S(2)}, u32[]{:S(2)}) collective-permute-start(bf16[2,8,16,128]{3,2,1,0:T(8,128)(2,1)S(1)} %get-tuple-element.37), channel_id=1, source_target_pairs={{0,16},{8,24},{16,0},{24,8},{1,17},{9,25},{17,1},{25,9},{2,18},{10... | collective-permute-start | bytes 196616 | tf_op jit(solution)/shard_map/ppermute | solution.py:330
  37.2 0.6 %collective-permute-start.8 = (bf16[2,9,16,128]{3,2,1,0:T(8,128)(2,1)S(1)}, bf16[2,9,16,128]{3,2,1,0:T(8,128)(2,1)S(1)}, u32[]{:S(2)}, u32[]{:S(2)}) collective-permute-start(bf16[2,9,16,128]{3,2,1,0:T(8,128)(2,1)S(1)} %get-tuple-element.35), channel_id=1, source_target_pairs={{0,4},{4,0},{1,5},{5,1},{2,6},{6,2},{3,7},{7,3},{8,12},{12,8},{9,1... | collective-permute-start | bytes 221192 | tf_op jit(solution)/shard_map/ppermute | solution.py:330
  37.8 0.1 collective-permute-start.6
  37.9 0.0 collective-permute-done.9
  37.9 0.7 %collective-permute-start.7 = (bf16[17,16,128]{2,1,0:T(8,128)(2,1)S(1)}, bf16[17,16,128]{2,1,0:T(8,128)(2,1)S(1)}, u32[]{:S(2)}, u32[]{:S(2)}) collective-permute-start(bf16[17,16,128]{2,1,0:T(8,128)(2,1)S(1)} %get-tuple-element.43), channel_id=1, source_target_pairs={{0,3},{1,2},{2,1},{3,0},{4,7},{5,6},{6,5},{7,4},{8,11},{9,10},{10,... | collective-permute-start | bytes 208904 | tf_op jit(solution)/shard_map/ppermute | solution.py:333
  38.6 1.4 %collective-permute-done.10 = bf16[8,16,128]{2,1,0:T(8,128)(2,1)S(1)} collective-permute-done((bf16[8,16,128]{2,1,0:T(8,128)(2,1)S(1)}, bf16[8,16,128]{2,1,0:T(8,128)(2,1)S(1)}, u32[]{:S(2)}, u32[]{:S(2)}) %collective-permute-start.10) | collective-permute-done | bytes 32800 | tf_op jit(solution)/shard_map/ppermute | solution.py:333
  40.0 0.0 collective-permute-done.6
  40.0 1.8 %collective-permute-done.7 = bf16[17,16,128]{2,1,0:T(8,128)(2,1)S(1)} collective-permute-done((bf16[17,16,128]{2,1,0:T(8,128)(2,1)S(1)}, bf16[17,16,128]{2,1,0:T(8,128)(2,1)S(1)}, u32[]{:S(2)}, u32[]{:S(2)}) %collective-permute-start.7) | collective-permute-done | bytes 69664 | tf_op jit(solution)/shard_map/ppermute | solution.py:333
  41.9 0.1 collective-permute-done.11.came0
  42.0 0.0 collective-permute-done.8.came2
  42.0 1.4 %shard_map.53 = (f32[64,8,128]{2,1,0:T(8,128)S(1)}, f32[32,128]{1,0:T(8,128)S(1)}) custom-call(s32[4]{0:T(128)S(1)} %fusion.1.flips, f32[64,8,64]{2,1,0:T(8,128)S(1)} %bitcast.44, f32[64,8,128]{2,1,0:T(8,128)S(1)} %get-tuple-element.29.mapped.first.map_a, f32[32,128]{1,0:T(8,128)S(1)} %bitcast.47, f32[64,8,128]{2,1,0:T(8,128)S(1)} %get-tuple-element.33.image, ...), custom_call_target="tpu_custom_call" | custom-call | tf_op jit(solution)/shard_map/pallas_call | solution.py:297
  43.4 9.6 %all_to_all.23 = f32[32,1,128]{2,1,0:T(1,128)S(1)} all-to-all(f32[32,1,128]{2,1,0:T(1,128)S(1)} %bitcast.50), channel_id=1, replica_groups=mesh['gx'=4,'gz'=2,'ta'=4] {'gx','gz','ta'}, dimensions={0} | all-to-all | bytes 32768 | tf_op jit(solution)/shard_map/all_to_all | solution.py:352
  53.0 1.0 %shard_map.54 = (f32[64,8,64]{2,1,0:T(8,128)}, f32[64,8,64]{2,1,0:T(8,128)}) custom-call(f32[64,8,64]{2,1,0:T(8,128)S(1)} %bitcast.45, f32[64,8,128]{2,1,0:T(8,128)S(1)} %get-tuple-element.22.update_a, f32[64,8,128]{2,1,0:T(8,128)S(1)} %get-tuple-element.29.mapped.first.map_a, f32[64,8,128]{2,1,0:T(8,128)S(1)} %get-tuple-element.32.update_b, ...), custom_call_target="tpu_custom_call" | custom-call | tf_op jit(solution)/shard_map/pallas_call | solution.py:297
  (8 shorter events, 0.1 us)
Async XLA Ops:
  0.6 17.1 %copy-start = (f32[1,2,2,4,4,8,64]{6,5,4,3,2,1,0:T(8,128)S(1)}, f32[1,2,2,4,4,8,64]{6,5,4,3,2,1,0:T(8,128)}, u32[]{:S(2)}) copy-start(f32[1,2,2,4,4,8,64]{6,5,4,3,2,1,0:T(8,128)} %param.3) | copy-start | bytes 393220
  6.2 7.3 %collective-permute-start.3 = (bf16[8,16,128]{2,1,0:T(8,128)(2,1)S(1)}, bf16[8,16,128]{2,1,0:T(8,128)(2,1)S(1)}, u32[]{:S(2)}, u32[]{:S(2)}) collective-permute-start(bf16[8,16,128]{2,1,0:T(8,128)(2,1)S(1)} %get-tuple-element.48), channel_id=1, source_target_pairs={{0,8},{8,0},{16,24},{24,16},{1,9},{9,1},{17,25},{25,17},{2,10},{10... | collective-permute-start | bytes 98312 | tf_op jit(solution)/shard_map/ppermute | solution.py:332
  9.3 6.2 %collective-permute-start.4 = (bf16[8,16,128]{2,1,0:T(8,128)(2,1)S(1)}, bf16[8,16,128]{2,1,0:T(8,128)(2,1)S(1)}, u32[]{:S(2)}, u32[]{:S(2)}) collective-permute-start(bf16[8,16,128]{2,1,0:T(8,128)(2,1)S(1)} %get-tuple-element.49), channel_id=1, source_target_pairs={{0,24},{8,16},{16,8},{24,0},{1,25},{9,17},{17,9},{25,1},{2,26},{10... | collective-permute-start | bytes 98312 | tf_op jit(solution)/shard_map/ppermute | solution.py:333
  11.8 5.9 %collective-permute-start.5 = (bf16[2,8,16,128]{3,2,1,0:T(8,128)(2,1)S(1)}, bf16[2,8,16,128]{3,2,1,0:T(8,128)(2,1)S(1)}, u32[]{:S(2)}, u32[]{:S(2)}) collective-permute-start(bf16[2,8,16,128]{3,2,1,0:T(8,128)(2,1)S(1)} %get-tuple-element.28), channel_id=1, source_target_pairs={{0,16},{8,24},{16,0},{24,8},{1,17},{9,25},{17,1},{25,9},{2,18},{10... | collective-permute-start | bytes 196616 | tf_op jit(solution)/shard_map/ppermute | solution.py:330
  11.9 5.8 %collective-permute-start.2 = (bf16[2,9,16,128]{3,2,1,0:T(8,128)(2,1)S(1)}, bf16[2,9,16,128]{3,2,1,0:T(8,128)(2,1)S(1)}, u32[]{:S(2)}, u32[]{:S(2)}) collective-permute-start(bf16[2,9,16,128]{3,2,1,0:T(8,128)(2,1)S(1)} %get-tuple-element.26), channel_id=1, source_target_pairs={{0,4},{4,0},{1,5},{5,1},{2,6},{6,2},{3,7},{7,3},{8,12},{12,8},{9,1... | collective-permute-start | bytes 221192 | tf_op jit(solution)/shard_map/ppermute | solution.py:330
  13.4 2.1 %collective-permute-start = (bf16[17,16,128]{2,1,0:T(8,128)(2,1)S(1)}, bf16[17,16,128]{2,1,0:T(8,128)(2,1)S(1)}, u32[]{:S(2)}, u32[]{:S(2)}) collective-permute-start(bf16[17,16,128]{2,1,0:T(8,128)(2,1)S(1)} %get-tuple-element.44), channel_id=1, source_target_pairs={{0,1},{1,0},{2,3},{3,2},{4,5},{5,4},{6,7},{7,6},{8,9},{9,8},{10,11... | collective-permute-start | bytes 208904 | tf_op jit(solution)/shard_map/ppermute | solution.py:332
  13.6 3.9 %collective-permute-start.1 = (bf16[17,16,128]{2,1,0:T(8,128)(2,1)S(1)}, bf16[17,16,128]{2,1,0:T(8,128)(2,1)S(1)}, u32[]{:S(2)}, u32[]{:S(2)}) collective-permute-start(bf16[17,16,128]{2,1,0:T(8,128)(2,1)S(1)} %get-tuple-element.45), channel_id=1, source_target_pairs={{0,3},{1,2},{2,1},{3,0},{4,7},{5,6},{6,5},{7,4},{8,11},{9,10},{10,... | collective-permute-start | bytes 208904 | tf_op jit(solution)/shard_map/ppermute | solution.py:333
  33.6 4.2 %collective-permute-start.9 = (bf16[8,16,128]{2,1,0:T(8,128)(2,1)S(1)}, bf16[8,16,128]{2,1,0:T(8,128)(2,1)S(1)}, u32[]{:S(2)}, u32[]{:S(2)}) collective-permute-start(bf16[8,16,128]{2,1,0:T(8,128)(2,1)S(1)} %get-tuple-element.46), channel_id=1, source_target_pairs={{0,8},{8,0},{16,24},{24,16},{1,9},{9,1},{17,25},{25,17},{2,10},{10... | collective-permute-start | bytes 98312 | tf_op jit(solution)/shard_map/ppermute | solution.py:332
  34.3 5.7 %collective-permute-start.10 = (bf16[8,16,128]{2,1,0:T(8,128)(2,1)S(1)}, bf16[8,16,128]{2,1,0:T(8,128)(2,1)S(1)}, u32[]{:S(2)}, u32[]{:S(2)}) collective-permute-start(bf16[8,16,128]{2,1,0:T(8,128)(2,1)S(1)} %get-tuple-element.47), channel_id=1, source_target_pairs={{0,24},{8,16},{16,8},{24,0},{1,25},{9,17},{17,9},{25,1},{2,26},{10... | collective-permute-start | bytes 98312 | tf_op jit(solution)/shard_map/ppermute | solution.py:333
  35.8 6.2 %collective-permute-start.11 = (bf16[2,8,16,128]{3,2,1,0:T(8,128)(2,1)S(1)}, bf16[2,8,16,128]{3,2,1,0:T(8,128)(2,1)S(1)}, u32[]{:S(2)}, u32[]{:S(2)}) collective-permute-start(bf16[2,8,16,128]{3,2,1,0:T(8,128)(2,1)S(1)} %get-tuple-element.37), channel_id=1, source_target_pairs={{0,16},{8,24},{16,0},{24,8},{1,17},{9,25},{17,1},{25,9},{2,18},{10... | collective-permute-start | bytes 196616 | tf_op jit(solution)/shard_map/ppermute | solution.py:330
  37.2 4.8 %collective-permute-start.8 = (bf16[2,9,16,128]{3,2,1,0:T(8,128)(2,1)S(1)}, bf16[2,9,16,128]{3,2,1,0:T(8,128)(2,1)S(1)}, u32[]{:S(2)}, u32[]{:S(2)}) collective-permute-start(bf16[2,9,16,128]{3,2,1,0:T(8,128)(2,1)S(1)} %get-tuple-element.35), channel_id=1, source_target_pairs={{0,4},{4,0},{1,5},{5,1},{2,6},{6,2},{3,7},{7,3},{8,12},{12,8},{9,1... | collective-permute-start | bytes 221192 | tf_op jit(solution)/shard_map/ppermute | solution.py:330
  37.8 2.2 %collective-permute-start.6 = (bf16[17,16,128]{2,1,0:T(8,128)(2,1)S(1)}, bf16[17,16,128]{2,1,0:T(8,128)(2,1)S(1)}, u32[]{:S(2)}, u32[]{:S(2)}) collective-permute-start(bf16[17,16,128]{2,1,0:T(8,128)(2,1)S(1)} %get-tuple-element.42), channel_id=1, source_target_pairs={{0,1},{1,0},{2,3},{3,2},{4,5},{5,4},{6,7},{7,6},{8,9},{9,8},{10,11... | collective-permute-start | bytes 208904 | tf_op jit(solution)/shard_map/ppermute | solution.py:332
  37.9 4.0 %collective-permute-start.7 = (bf16[17,16,128]{2,1,0:T(8,128)(2,1)S(1)}, bf16[17,16,128]{2,1,0:T(8,128)(2,1)S(1)}, u32[]{:S(2)}, u32[]{:S(2)}) collective-permute-start(bf16[17,16,128]{2,1,0:T(8,128)(2,1)S(1)} %get-tuple-element.43), channel_id=1, source_target_pairs={{0,3},{1,2},{2,1},{3,0},{4,7},{5,6},{6,5},{7,4},{8,11},{9,10},{10,... | collective-permute-start | bytes 208904 | tf_op jit(solution)/shard_map/ppermute | solution.py:333

commit v4 on v3

--- a/solution.py
+++ b/solution.py
@@ -13,6 +13,7 @@
 NN = (((1,), (0,)), ((), ()))
 VMEM_BYTES = 24 * 2**20
 GROUP = 4
+LAG = 2
 AXES = ("gx", "gx", "gz", "ta")
 
 
@@ -41,6 +42,65 @@
         return [s for s in range(self.count) if self.coord(s, direction) == wanted]
 
 
+class Tiles:
+    def __init__(self, blocks, first):
+        self.first = first
+        self.tiles = [blocks[k : k + 4] for k in range(0, len(blocks), 4)]
+        self.sites = [list(dict.fromkeys(s for s, _ in tile)) for tile in self.tiles]
+        self.starts = []
+        self.place = {}
+        self.runs = 0
+        for tile, sites in zip(self.tiles, self.sites):
+            self.starts.append(self.runs)
+            for slot, block in enumerate(tile):
+                self.place[block] = (self.runs + sites.index(block[0]), slot)
+            self.runs += len(sites)
+
+
+def split_links(box):
+    blocks = [(s, d) for s in range(box.count) for d in range(4)]
+    inner = Tiles([b for b in blocks if box.ahead(*b) is not None], 0)
+    outer = Tiles([b for b in blocks if box.ahead(*b) is None], len(inner.tiles))
+    return inner, outer
+
+
+def slotted(contents, low, zero):
+    halves = []
+    for left, right in (contents[:2], contents[2:]):
+        if left is None and right is None:
+            halves.append(zero)
+        else:
+            halves.append(jnp.where(low, zero if left is None else left, zero if right is None else right))
+    return jnp.concatenate(halves, axis=1)
+
+
+def ahead_products(tiles, k, value, links, low, zero):
+    rows = zero.shape[0]
+    stack = []
+    for s in tiles.sites[k]:
+        contents = [value(s, d, slot) if t == s else None for slot, (t, d) in enumerate(tiles.tiles[k])]
+        contents += [None] * (4 - len(contents))
+        stack.append(slotted(contents, low, zero))
+    spread = jnp.concatenate(stack, axis=0).astype(BF16)
+    total = lax.dot_general(spread, links[tiles.first + k], NT, preferred_element_type=F32)
+    return {s: total[i * rows : (i + 1) * rows] for i, s in enumerate(tiles.sites[k])}
+
+
+def back_products(tiles, k, field, links, back, chirality):
+    rows, lanes = field.shape[1:]
+    stack = jnp.concatenate([chirality * field[s] for s in tiles.sites[k]], axis=0)
+    product = lax.dot_general(
+        stack[:, : lanes // 2].astype(BF16), links[tiles.first + k], NN, preferred_element_type=F32
+    )
+    for i in range(len(tiles.sites[k])):
+        back[tiles.starts[k] + i] = product[i * rows : (i + 1) * rows]
+
+
+def back_value(tiles, block, back, lanes):
+    run, slot = tiles.place[block]
+    return back[run, :, slot // 2 * lanes : (slot // 2 + 1) * lanes], slot % 2
+
+
 def lane_tools(rows, lanes):
     lane = lax.broadcasted_iota(jnp.int32, (rows, lanes), 1)
     low = lane < lanes // 2
@@ -63,68 +123,105 @@
     return lax.dot_general(blocks, own[group], NT, preferred_element_type=F32)
 
 
-def local_products(box, field, links, own, back, mapped, low, chirality, arrive=None):
+def local_products(box, tiles, field, links, own, back, mapped, low, chirality, prepare=None):
     rows, lanes = field.shape[1:]
     half = lanes // 2
     zero = jnp.zeros((rows, lanes), F32)
-    for g in range(box.count // GROUP):
-        if arrive is not None:
-            arrive(g)
+    top = [zero]
+    bottom = [zero]
+    parts = {}
+
+    def value(s, d, _):
+        return field[box.ahead(s, d)]
+
+    def diagonal(g):
+        if prepare is not None:
+            prepare(group=g)
         sites = range(GROUP * g, GROUP * g + GROUP)
-        here = [field[s] for s in sites]
-        diagonal = own_products(g, here, own, low)
+        total = own_products(g, [field[s] for s in sites], own, low)
         for i, s in enumerate(sites):
-            ahead = [box.ahead(s, d) for d in range(4)]
-            total = diagonal[i * rows : (i + 1) * rows]
-            if any(a is not None for a in ahead):
-                part = [zero if a is None else field[a] for a in ahead]
-                spread = jnp.concatenate(
-                    [jnp.where(low, part[0], part[1]), jnp.where(low, part[2], part[3])], axis=1
-                ).astype(BF16)
-                total = total + lax.dot_general(spread, links[s], NT, preferred_element_type=F32)
-            mapped[s] = jnp.concatenate([total, jnp.zeros((rows, half), F32)], axis=1)
-            back[s] = lax.dot_general(
-                (chirality * here[i])[:, :half].astype(BF16),
-                links[s],
-                NN,
-                preferred_element_type=F32,
-            )
-    top = zero
-    bottom = zero
-    for s in range(box.count):
-        behind = [box.behind(s, d) for d in range(4)]
-        piece = []
+            parts[s] = total[i * rows : (i + 1) * rows]
+
+    def gather(s):
+        sums = [None, None]
         for d in range(4):
-            start = d // 2 * lanes
-            piece.append(zero if behind[d] is None else back[behind[d], :, start : start + lanes])
-        gathered = jnp.where(low, piece[0], piece[1]) + jnp.where(low, piece[2], piece[3])
-        gathered = chirality * gathered + mapped[s]
+            b = box.behind(s, d)
+            if b is not None:
+                piece, side = back_value(tiles, (b, d), back, lanes)
+                sums[side] = piece if sums[side] is None else sums[side] + piece
+        gathered = mapped[s]
+        if sums[0] is not None or sums[1] is not None:
+            sums = [zero if x is None else x for x in sums]
+            gathered = chirality * jnp.where(low, sums[0], sums[1]) + gathered
         here = field[s]
-        value = 4.0 * here + gathered + pltpu.roll(gathered, half, 1)
-        mapped[s] = value
-        top = top + value * here
-        bottom = bottom + value * value
-    return jnp.sum(top, axis=1, keepdims=True) / jnp.sum(bottom, axis=1, keepdims=True)
-
-
-def smooth(box, flips, field, links, own, outs, scratch, arrive=None):
+        result = 4.0 * here + gathered + pltpu.roll(gathered, half, 1)
+        mapped[s] = result
+        top[0] = top[0] + result * here
+        bottom[0] = bottom[0] + result * result
+
+    last = {}
+    for k, sites in enumerate(tiles.sites):
+        for s in sites:
+            last[s] = k
+    ready = 0
+    done = 0
+    for k in range(len(tiles.tiles) + LAG):
+        if k < len(tiles.tiles):
+            for s in tiles.sites[k]:
+                while ready * GROUP <= s:
+                    diagonal(ready)
+                    ready += 1
+            if prepare is not None:
+                prepare(tile=k)
+            for s, part in ahead_products(tiles, k, value, links, low, zero).items():
+                parts[s] = parts[s] + part
+            back_products(tiles, k, field, links, back, chirality)
+            for s in tiles.sites[k]:
+                if last[s] == k:
+                    mapped[s] = jnp.concatenate([parts.pop(s), jnp.zeros((rows, half), F32)], axis=1)
+        if k >= LAG:
+            while done < box.count and last.get(done, -1) <= k - LAG and done // GROUP < ready:
+                if done in parts:
+                    mapped[done] = jnp.concatenate([parts.pop(done), jnp.zeros((rows, half), F32)], axis=1)
+                gather(done)
+                done += 1
+    while ready * GROUP < box.count:
+        diagonal(ready)
+        ready += 1
+    while done < box.count:
+        if done in parts:
+            mapped[done] = jnp.concatenate([parts.pop(done), jnp.zeros((rows, half), F32)], axis=1)
+        gather(done)
+        done += 1
+    return jnp.sum(top[0], axis=1, keepdims=True) / jnp.sum(bottom[0], axis=1, keepdims=True)
+
+
+def smooth(box, flips, field, links, own, outs, scratch, prepare=None):
     update, image, sends = outs
-    back_a, back_b, map_a, map_b, second = scratch
+    back, map_a, map_b, second = scratch
     rows, lanes = field.shape[1:]
     half = lanes // 2
     low, chirality = lane_tools(rows, lanes)
-    weight_a = local_products(box, field, links, own, back_a, map_a, low, chirality, arrive)
+    inner, outer = split_links(box)
+    weight_a = local_products(box, inner, field, links, own, back, map_a, low, chirality, prepare)
     for s in range(box.count):
         second[s] = field[s] - weight_a * map_a[s]
-    weight_b = local_products(box, second, links, own, back_b, map_b, low, chirality)
+    weight_b = local_products(box, inner, second, links, own, back, map_b, low, chirality)
     for s in range(box.count):
         update[s] = weight_a * field[s] + weight_b * second[s]
+    for k in range(len(outer.tiles)):
+        back_products(outer, k, update, links, back, chirality)
+    for s in range(box.count):
         image[s] = weight_a * map_a[s] + weight_b * map_b[s]
+
+    def aligned(s, d, side):
+        piece, found = back_value(outer, (s, d), back, lanes)
+        return piece if found == side else pltpu.roll(piece, half, 1)
+
     for d in range(4):
         flip = flips[d]
         lower = box.rim(d, False)
         upper = box.rim(d, True)
-        start = d // 2 * lanes
         for j in range(len(lower) // 4):
             block = []
             for k in (4 * j, 4 * j + 2):
@@ -132,16 +229,7 @@
             sends[d][flip, j] = jnp.concatenate(block, axis=0).astype(BF16)
             block = []
             for k in (4 * j, 4 * j + 2):
-                pair = []
-                for u in (upper[k], upper[k + 1]):
-                    pair.append(
-                        weight_a * back_a[u, :, start : start + lanes]
-                        + weight_b * back_b[u, :, start : start + lanes]
-                    )
-                if d % 2 == 0:
-                    joined = jnp.where(low, pair[0], pltpu.roll(pair[1], half, 1))
-                else:
-                    joined = jnp.where(low, pltpu.roll(pair[0], half, 1), pair[1])
+                joined = jnp.where(low, aligned(upper[k], d, 0), aligned(upper[k + 1], d, 1))
                 block.append(chirality * joined)
             sends[d][1 - flip, j] = jnp.concatenate(block, axis=0).astype(BF16)
 
@@ -150,7 +238,7 @@
     box, parts, flips, rhs_in, own_in, hop_in, *refs
 ):
     update, image, send0, send1, send2, send3, links, own = refs[:8]
-    field, back_a, back_b, map_a, map_b, second, rhs, own_raw, hop, sems = refs[8:]
+    field, back, map_a, map_b, second, rhs, own_raw, hop, sems = refs[8:]
     each = box.count // parts
     copies = [pltpu.make_async_copy(rhs_in, rhs, sems.at[2 * parts])]
     for c in range(parts):
@@ -162,19 +250,42 @@
     copies[0].wait()
     for s in range(box.count):
         field[s] = twice(rhs[s])
-
-    def arrive(g):
-        if g * GROUP % each == 0:
-            c = g * GROUP // each
+    inner, outer = split_links(box)
+    blank = jnp.zeros(hop.shape[2:], BF16)
+    arrived = [0]
+    packed = [0]
+
+    def await_site(s):
+        while arrived[0] * each <= s:
+            c = arrived[0]
             copies[2 * c + 1].wait()
             copies[2 * c + 2].wait()
-        sites = range(GROUP * g, GROUP * g + GROUP)
-        own[g] = jnp.concatenate([own_raw[s] for s in sites], axis=1)
-        for s in sites:
-            links[s] = jnp.concatenate([hop[d, s] for d in range(4)], axis=1)
-
-    scratch = (back_a, back_b, map_a, map_b, second)
-    smooth(box, flips, field, links, own, (update, image, (send0, send1, send2, send3)), scratch, arrive)
+            arrived[0] += 1
+
+    def pack(tiles, k):
+        matrices = [hop[d, s] for s, d in tiles.tiles[k]]
+        matrices += [blank] * (4 - len(matrices))
+        links[tiles.first + k] = jnp.concatenate(matrices, axis=1)
+
+    def prepare(group=None, tile=None):
+        if group is not None:
+            sites = range(GROUP * group, GROUP * group + GROUP)
+            await_site(sites[-1])
+            own[group] = jnp.concatenate([own_raw[s] for s in sites], axis=1)
+        if tile is not None:
+            await_site(inner.sites[tile][-1])
+            pack(inner, tile)
+            final = tile == len(inner.tiles) - 1
+            if final:
+                await_site(box.count - 1)
+            while packed[0] < len(outer.tiles) and (final or outer.sites[packed[0]][-1] < arrived[0] * each):
+                pack(outer, packed[0])
+                packed[0] += 1
+                if not final and packed[0] * len(inner.tiles) > (tile + 1) * len(outer.tiles):
+                    break
+
+    scratch = (back, map_a, map_b, second)
+    smooth(box, flips, field, links, own, (update, image, (send0, send1, send2, send3)), scratch, prepare)
 
 
 def second_kernel(box, flips, rhs, mapped, sums, links, own, update, image, send0, send1, send2, send3, field, *scratch):
@@ -195,28 +306,42 @@
     def read(d, which, k):
         slot = flips[d] if which == 0 else 1 - flips[d]
         tile = came[d][slot, k // 4].astype(F32)
-        tile = tile[(k // 2 % 2) * rows : (k // 2 % 2 + 1) * rows]
-        if which == 0 and k % 2 != d % 2:
-            tile = pltpu.roll(tile, half, 1)
-        return tile
+        return tile[(k // 2 % 2) * rows : (k // 2 % 2 + 1) * rows]
 
     zero = jnp.zeros((rows, lanes), F32)
-    for s in range(box.count):
-        part = [read(d, 0, places[d][s]) if s in places[d] else None for d in range(4)]
+    _, outer = split_links(box)
+
+    def value(s, d, slot):
+        k = places[d][s]
+        tile = read(d, 0, k)
+        return tile if k % 2 == slot % 2 else pltpu.roll(tile, half, 1)
+
+    parts = {}
+    last = {}
+    for k, sites in enumerate(outer.sites):
+        for s in sites:
+            last[s] = k
+
+    def finish(s):
         extra = zero
-        if any(p is not None for p in part):
-            part = [zero if p is None else p for p in part]
-            spread = jnp.concatenate(
-                [jnp.where(low, part[0], part[1]), jnp.where(low, part[2], part[3])], axis=1
-            ).astype(BF16)
-            total = lax.dot_general(spread, links[s], NT, preferred_element_type=F32)
-            extra = jnp.concatenate([total, jnp.zeros((rows, half), F32)], axis=1)
+        if s in parts:
+            extra = jnp.concatenate([parts.pop(s), jnp.zeros((rows, half), F32)], axis=1)
         for d in range(4):
             if s in lows[d]:
                 k = lows[d][s]
                 tile = read(d, 1, k)
                 extra = extra + (jnp.where(low, tile, 0.0) if k % 2 == 0 else jnp.where(low, 0.0, tile))
         mapped[s] = image[s] + extra + pltpu.roll(extra, half, 1)
+
+    done = 0
+    for k in range(len(outer.tiles)):
+        for s, part in ahead_products(outer, k, value, links, low, zero).items():
+            parts[s] = parts[s] + part if s in parts else part
+        while done < box.count and last.get(done, -1) <= k - LAG:
+            finish(done)
+            done += 1
+    for s in range(done, box.count):
+        finish(s)
 
 
 def sum_places(rows, lanes):
@@ -389,7 +514,9 @@
     full = jax.ShapeDtypeStruct((count, rows, lanes), F32)
     small = jax.ShapeDtypeStruct((sum_rows(), lanes), F32)
     narrow = jax.ShapeDtypeStruct((count, rows, channels), F32)
-    links_shape = jax.ShapeDtypeStruct((count, channels, 4 * channels), BF16)
+    inner, outer = split_links(box)
+    link_tiles = len(inner.tiles) + len(outer.tiles)
+    links_shape = jax.ShapeDtypeStruct((link_tiles, channels, 4 * channels), BF16)
     own_shape = jax.ShapeDtypeStruct((count // GROUP, channels, GROUP * channels), BF16)
     parts = extents[0] * extents[1]
     raw = [
@@ -402,8 +529,8 @@
         jax.ShapeDtypeStruct((2, tiles, 2 * rows, lanes), BF16) for tiles in message_tiles(box)
     ]
     field_scratch = pltpu.VMEM((count, rows, lanes), F32)
-    back_scratch = pltpu.VMEM((count, rows, 4 * channels), F32)
-    scratch = [field_scratch, back_scratch, back_scratch, field_scratch, field_scratch, field_scratch]
+    back_scratch = pltpu.VMEM((max(inner.runs, outer.runs), rows, 4 * channels), F32)
+    scratch = [field_scratch, back_scratch, field_scratch, field_scratch, field_scratch]
 
     update_a, image_a, *sends, links, own = call(
         functools.partial(first_kernel, box, parts),

time: 54.1 us -> 52.8 us (0.976)
  Pallas kernels: 12.6 us -> 11.3 us
    pallas_call x5, Pallas kernels: 12.6 us -> 11.3 us  [call(): pl.pallas_call(body, out_shape=outs, in_specs=specs, out_specs=[vmem] * l...]
where the time goes in v4:
time: 52.8 us; the launch traced here: 52.6 us
  blocking collectives  20.7 us (39%)
  starting transfers between devices  13.8 us (26%)
  Pallas kernels  11.3 us (21%)
  waiting for transfers between devices  5.87 us (11%)
  between operations  0.76 us (1%)
    all_to_all x2, blocking collectives, mesh_sum(): return lax.all_to_all(value, ('gx', 'gz', 'ta'), 0, 0, tiled=True)  20.7 us
    pallas_call x5, Pallas kernels, call(): pl.pallas_call(body, out_shape=outs, in_specs=specs, out_specs=[vmem] * l...  11.3 us
    ppermute x4, starting transfers between devices, exchange(): lax.ppermute(sends[d][1], axis, [(i, (i + 1 if i % 2 else i - 1) % size)...  6.28 us
    ppermute x4, waiting for transfers between devices, exchange(): lax.ppermute(sends[d][1], axis, [(i, (i + 1 if i % 2 else i - 1) % size)...  5.48 us
    ppermute x4, starting transfers between devices, exchange(): even = lax.ppermute(sends[d][0], axis, [(i, i ^ 1) for i in ring])  3.87 us
    ppermute x4, starting transfers between devices, exchange(): lax.ppermute(sends[d], axis, [(i, (i + step) % size) for i in ring])  3.61 us
  transfers between devices with their start and end apart: 12, of which 6 were waited for; matrix products, arithmetic and copies ran while one was open for 0% of the time, Pallas kernels for 0%

profile of v4, /device:TPU:0, one launch (start us, length us, event | category | flops | bytes accessed | tf_op | source)
XLA Modules:
  0.0 52.6 jit_solution(1379600388754692685)
XLA Ops:
  0.6 0.0 copy-start
  0.7 0.1 fusion.flips
  0.7 5.1 %shard_map.50 = (f32[64,8,128]{2,1,0:T(8,128)S(1)}, f32[64,8,128]{2,1,0:T(8,128)S(1)}, bf16[2,8,16,128]{3,2,1,0:T(8,128)(2,1)S(1)}, bf16[2,8,16,128]{3,2,1,0:T(8...) custom-call(s32[4]{0:T(128)S(1)} %fusion.flips, ...), custom_call_target="tpu_custom_call" | custom-call | tf_op jit(solution)/shard_map/pallas_call | solution.py:422
  5.9 3.1 %collective-permute-start.3 = (bf16[8,16,128]{2,1,0:T(8,128)(2,1)S(1)}, bf16[8,16,128]{2,1,0:T(8,128)(2,1)S(1)}, u32[]{:S(2)}, u32[]{:S(2)}) collective-permute-start(bf16[8,16,128]{2,1,0:T(8,128)(2,1)S(1)} %get-tuple-element.48), channel_id=1, source_target_pairs={{0,8},{8,0},{16,24},{24,16},{1,9},{9,1},{17,25},{25,17},{2,10},{10... | collective-permute-start | bytes 98312 | tf_op jit(solution)/shard_map/ppermute | solution.py:457
  9.0 2.5 %collective-permute-start.4 = (bf16[8,16,128]{2,1,0:T(8,128)(2,1)S(1)}, bf16[8,16,128]{2,1,0:T(8,128)(2,1)S(1)}, u32[]{:S(2)}, u32[]{:S(2)}) collective-permute-start(bf16[8,16,128]{2,1,0:T(8,128)(2,1)S(1)} %get-tuple-element.49), channel_id=1, source_target_pairs={{0,24},{8,16},{16,8},{24,0},{1,25},{9,17},{17,9},{25,1},{2,26},{10... | collective-permute-start | bytes 98312 | tf_op jit(solution)/shard_map/ppermute | solution.py:458
  11.4 0.1 collective-permute-start.5
  11.5 1.5 %collective-permute-start.2 = (bf16[2,9,16,128]{3,2,1,0:T(8,128)(2,1)S(1)}, bf16[2,9,16,128]{3,2,1,0:T(8,128)(2,1)S(1)}, u32[]{:S(2)}, u32[]{:S(2)}) collective-permute-start(bf16[2,9,16,128]{3,2,1,0:T(8,128)(2,1)S(1)} %get-tuple-element.26), channel_id=1, source_target_pairs={{0,4},{4,0},{1,5},{5,1},{2,6},{6,2},{3,7},{7,3},{8,12},{12,8},{9,1... | collective-permute-start | bytes 221192 | tf_op jit(solution)/shard_map/ppermute | solution.py:455
  13.0 0.1 collective-permute-start
  13.1 0.1 fusion.1.flips
  13.2 0.0 collective-permute-done.3
  13.2 1.6 %collective-permute-start.1 = (bf16[17,16,128]{2,1,0:T(8,128)(2,1)S(1)}, bf16[17,16,128]{2,1,0:T(8,128)(2,1)S(1)}, u32[]{:S(2)}, u32[]{:S(2)}) collective-permute-start(bf16[17,16,128]{2,1,0:T(8,128)(2,1)S(1)} %get-tuple-element.45), channel_id=1, source_target_pairs={{0,3},{1,2},{2,1},{3,0},{4,7},{5,6},{6,5},{7,4},{8,11},{9,10},{10,... | collective-permute-start | bytes 208904 | tf_op jit(solution)/shard_map/ppermute | solution.py:458
  14.8 0.3 collective-permute-done.4
  15.1 0.0 collective-permute-done
  15.1 1.9 %collective-permute-done.1 = bf16[17,16,128]{2,1,0:T(8,128)(2,1)S(1)} collective-permute-done((bf16[17,16,128]{2,1,0:T(8,128)(2,1)S(1)}, bf16[17,16,128]{2,1,0:T(8,128)(2,1)S(1)}, u32[]{:S(2)}, u32[]{:S(2)}) %collective-permute-start.1) | collective-permute-done | bytes 69664 | tf_op jit(solution)/shard_map/ppermute | solution.py:458
  17.1 0.2 collective-permute-done.5.came0
  17.4 0.0 collective-permute-done.2.came2
  17.4 0.0 copy-done
  17.4 1.1 %shard_map.51 = (f32[64,8,128]{2,1,0:T(8,128)S(1)}, f32[32,128]{1,0:T(8,128)S(1)}) custom-call(s32[4]{0:T(128)S(1)} %fusion.1.flips, f32[64,8,64]{2,1,0:T(8,128)S(1)} %bitcast.42, f32[64,8,128]{2,1,0:T(8,128)S(1)} %get-tuple-element.23.image, bf16[64,64,256]{2,1,0:T(8,128)(2,1)S(1)} %get-tuple-element.24.links, ...), custom_call_target="tpu_custom_call" | custom-call | tf_op jit(solution)/shard_map/pallas_call | solution.py:422
  18.4 11.1 %all_to_all.22 = f32[32,1,128]{2,1,0:T(1,128)S(1)} all-to-all(f32[32,1,128]{2,1,0:T(1,128)S(1)} %bitcast.51), channel_id=1, replica_groups=mesh['gx'=4,'gz'=2,'ta'=4] {'gx','gz','ta'}, dimensions={0} | all-to-all | bytes 32768 | tf_op jit(solution)/shard_map/all_to_all | solution.py:477
  29.5 3.0 %shard_map.52 = (f32[64,8,128]{2,1,0:T(8,128)S(1)}, f32[64,8,128]{2,1,0:T(8,128)S(1)}, bf16[2,8,16,128]{3,2,1,0:T(8,128)(2,1)S(1)}, bf16[2,8,16,128]{3,2,1,0:T(8...) custom-call(s32[4]{0:T(128)S(1)} %fusion.flips, f32[64,8,64]{2,1,0:T(8,128)S(1)} %bitcast.43, ...), custom_call_target="tpu_custom_call" | custom-call | tf_op jit(solution)/shard_map/pallas_call | solution.py:422
  32.5 0.6 %collective-permute-start.9 = (bf16[8,16,128]{2,1,0:T(8,128)(2,1)S(1)}, bf16[8,16,128]{2,1,0:T(8,128)(2,1)S(1)}, u32[]{:S(2)}, u32[]{:S(2)}) collective-permute-start(bf16[8,16,128]{2,1,0:T(8,128)(2,1)S(1)} %get-tuple-element.46), channel_id=1, source_target_pairs={{0,8},{8,0},{16,24},{24,16},{1,9},{9,1},{17,25},{25,17},{2,10},{10... | collective-permute-start | bytes 98312 | tf_op jit(solution)/shard_map/ppermute | solution.py:457
  33.2 1.5 %collective-permute-start.10 = (bf16[8,16,128]{2,1,0:T(8,128)(2,1)S(1)}, bf16[8,16,128]{2,1,0:T(8,128)(2,1)S(1)}, u32[]{:S(2)}, u32[]{:S(2)}) collective-permute-start(bf16[8,16,128]{2,1,0:T(8,128)(2,1)S(1)} %get-tuple-element.47), channel_id=1, source_target_pairs={{0,24},{8,16},{16,8},{24,0},{1,25},{9,17},{17,9},{25,1},{2,26},{10... | collective-permute-start | bytes 98312 | tf_op jit(solution)/shard_map/ppermute | solution.py:458
  34.6 1.4 %collective-permute-start.11 = (bf16[2,8,16,128]{3,2,1,0:T(8,128)(2,1)S(1)}, bf16[2,8,16,128]{3,2,1,0:T(8,128)(2,1)S(1)}, u32[]{:S(2)}, u32[]{:S(2)}) collective-permute-start(bf16[2,8,16,128]{3,2,1,0:T(8,128)(2,1)S(1)} %get-tuple-element.37), channel_id=1, source_target_pairs={{0,16},{8,24},{16,0},{24,8},{1,17},{9,25},{17,1},{25,9},{2,18},{10... | collective-permute-start | bytes 196616 | tf_op jit(solution)/shard_map/ppermute | solution.py:455
  36.1 0.6 %collective-permute-start.8 = (bf16[2,9,16,128]{3,2,1,0:T(8,128)(2,1)S(1)}, bf16[2,9,16,128]{3,2,1,0:T(8,128)(2,1)S(1)}, u32[]{:S(2)}, u32[]{:S(2)}) collective-permute-start(bf16[2,9,16,128]{3,2,1,0:T(8,128)(2,1)S(1)} %get-tuple-element.35), channel_id=1, source_target_pairs={{0,4},{4,0},{1,5},{5,1},{2,6},{6,2},{3,7},{7,3},{8,12},{12,8},{9,1... | collective-permute-start | bytes 221192 | tf_op jit(solution)/shard_map/ppermute | solution.py:455
  36.7 0.1 collective-permute-start.6
  36.7 0.0 collective-permute-done.9
  36.7 0.7 %collective-permute-start.7 = (bf16[17,16,128]{2,1,0:T(8,128)(2,1)S(1)}, bf16[17,16,128]{2,1,0:T(8,128)(2,1)S(1)}, u32[]{:S(2)}, u32[]{:S(2)}) collective-permute-start(bf16[17,16,128]{2,1,0:T(8,128)(2,1)S(1)} %get-tuple-element.43), channel_id=1, source_target_pairs={{0,3},{1,2},{2,1},{3,0},{4,7},{5,6},{6,5},{7,4},{8,11},{9,10},{10,... | collective-permute-start | bytes 208904 | tf_op jit(solution)/shard_map/ppermute | solution.py:458
  37.5 1.4 %collective-permute-done.10 = bf16[8,16,128]{2,1,0:T(8,128)(2,1)S(1)} collective-permute-done((bf16[8,16,128]{2,1,0:T(8,128)(2,1)S(1)}, bf16[8,16,128]{2,1,0:T(8,128)(2,1)S(1)}, u32[]{:S(2)}, u32[]{:S(2)}) %collective-permute-start.10) | collective-permute-done | bytes 32800 | tf_op jit(solution)/shard_map/ppermute | solution.py:458
  38.9 0.0 collective-permute-done.6
  38.9 1.8 %collective-permute-done.7 = bf16[17,16,128]{2,1,0:T(8,128)(2,1)S(1)} collective-permute-done((bf16[17,16,128]{2,1,0:T(8,128)(2,1)S(1)}, bf16[17,16,128]{2,1,0:T(8,128)(2,1)S(1)}, u32[]{:S(2)}, u32[]{:S(2)}) %collective-permute-start.7) | collective-permute-done | bytes 69664 | tf_op jit(solution)/shard_map/ppermute | solution.py:458
  40.7 0.1 collective-permute-done.11.came0
  40.9 0.0 collective-permute-done.8.came2
  40.9 1.1 %shard_map.53 = (f32[64,8,128]{2,1,0:T(8,128)S(1)}, f32[32,128]{1,0:T(8,128)S(1)}) custom-call(s32[4]{0:T(128)S(1)} %fusion.1.flips, f32[64,8,64]{2,1,0:T(8,128)S(1)} %bitcast.44, f32[64,8,128]{2,1,0:T(8,128)S(1)} %get-tuple-element.29.mapped.first.map_a, f32[32,128]{1,0:T(8,128)S(1)} %bitcast.47, f32[64,8,128]{2,1,0:T(8,128)S(1)} %get-tuple-element.33.image, ...), custom_call_target="tpu_custom_call" | custom-call | tf_op jit(solution)/shard_map/pallas_call | solution.py:422
  42.0 9.6 %all_to_all.23 = f32[32,1,128]{2,1,0:T(1,128)S(1)} all-to-all(f32[32,1,128]{2,1,0:T(1,128)S(1)} %bitcast.50), channel_id=1, replica_groups=mesh['gx'=4,'gz'=2,'ta'=4] {'gx','gz','ta'}, dimensions={0} | all-to-all | bytes 32768 | tf_op jit(solution)/shard_map/all_to_all | solution.py:477
  51.6 1.0 %shard_map.54 = (f32[64,8,64]{2,1,0:T(8,128)}, f32[64,8,64]{2,1,0:T(8,128)}) custom-call(f32[64,8,64]{2,1,0:T(8,128)S(1)} %bitcast.45, f32[64,8,128]{2,1,0:T(8,128)S(1)} %get-tuple-element.22.update_a, f32[64,8,128]{2,1,0:T(8,128)S(1)} %get-tuple-element.29.mapped.first.map_a, f32[64,8,128]{2,1,0:T(8,128)S(1)} %get-tuple-element.32.update_b, ...), custom_call_target="tpu_custom_call" | custom-call | tf_op jit(solution)/shard_map/pallas_call | solution.py:422
  (8 shorter events, 0.1 us)
Async XLA Ops:
  0.6 16.7 %copy-start = (f32[1,2,2,4,4,8,64]{6,5,4,3,2,1,0:T(8,128)S(1)}, f32[1,2,2,4,4,8,64]{6,5,4,3,2,1,0:T(8,128)}, u32[]{:S(2)}) copy-start(f32[1,2,2,4,4,8,64]{6,5,4,3,2,1,0:T(8,128)} %param.3) | copy-start | bytes 393220
  5.9 7.4 %collective-permute-start.3 = (bf16[8,16,128]{2,1,0:T(8,128)(2,1)S(1)}, bf16[8,16,128]{2,1,0:T(8,128)(2,1)S(1)}, u32[]{:S(2)}, u32[]{:S(2)}) collective-permute-start(bf16[8,16,128]{2,1,0:T(8,128)(2,1)S(1)} %get-tuple-element.48), channel_id=1, source_target_pairs={{0,8},{8,0},{16,24},{24,16},{1,9},{9,1},{17,25},{25,17},{2,10},{10... | collective-permute-start | bytes 98312 | tf_op jit(solution)/shard_map/ppermute | solution.py:457
  9.0 6.2 %collective-permute-start.4 = (bf16[8,16,128]{2,1,0:T(8,128)(2,1)S(1)}, bf16[8,16,128]{2,1,0:T(8,128)(2,1)S(1)}, u32[]{:S(2)}, u32[]{:S(2)}) collective-permute-start(bf16[8,16,128]{2,1,0:T(8,128)(2,1)S(1)} %get-tuple-element.49), channel_id=1, source_target_pairs={{0,24},{8,16},{16,8},{24,0},{1,25},{9,17},{17,9},{25,1},{2,26},{10... | collective-permute-start | bytes 98312 | tf_op jit(solution)/shard_map/ppermute | solution.py:458
  11.4 5.9 %collective-permute-start.5 = (bf16[2,8,16,128]{3,2,1,0:T(8,128)(2,1)S(1)}, bf16[2,8,16,128]{3,2,1,0:T(8,128)(2,1)S(1)}, u32[]{:S(2)}, u32[]{:S(2)}) collective-permute-start(bf16[2,8,16,128]{3,2,1,0:T(8,128)(2,1)S(1)} %get-tuple-element.28), channel_id=1, source_target_pairs={{0,16},{8,24},{16,0},{24,8},{1,17},{9,25},{17,1},{25,9},{2,18},{10... | collective-permute-start | bytes 196616 | tf_op jit(solution)/shard_map/ppermute | solution.py:455
  11.5 5.8 %collective-permute-start.2 = (bf16[2,9,16,128]{3,2,1,0:T(8,128)(2,1)S(1)}, bf16[2,9,16,128]{3,2,1,0:T(8,128)(2,1)S(1)}, u32[]{:S(2)}, u32[]{:S(2)}) collective-permute-start(bf16[2,9,16,128]{3,2,1,0:T(8,128)(2,1)S(1)} %get-tuple-element.26), channel_id=1, source_target_pairs={{0,4},{4,0},{1,5},{5,1},{2,6},{6,2},{3,7},{7,3},{8,12},{12,8},{9,1... | collective-permute-start | bytes 221192 | tf_op jit(solution)/shard_map/ppermute | solution.py:455
  13.0 2.1 %collective-permute-start = (bf16[17,16,128]{2,1,0:T(8,128)(2,1)S(1)}, bf16[17,16,128]{2,1,0:T(8,128)(2,1)S(1)}, u32[]{:S(2)}, u32[]{:S(2)}) collective-permute-start(bf16[17,16,128]{2,1,0:T(8,128)(2,1)S(1)} %get-tuple-element.44), channel_id=1, source_target_pairs={{0,1},{1,0},{2,3},{3,2},{4,5},{5,4},{6,7},{7,6},{8,9},{9,8},{10,11... | collective-permute-start | bytes 208904 | tf_op jit(solution)/shard_map/ppermute | solution.py:457
  13.2 3.9 %collective-permute-start.1 = (bf16[17,16,128]{2,1,0:T(8,128)(2,1)S(1)}, bf16[17,16,128]{2,1,0:T(8,128)(2,1)S(1)}, u32[]{:S(2)}, u32[]{:S(2)}) collective-permute-start(bf16[17,16,128]{2,1,0:T(8,128)(2,1)S(1)} %get-tuple-element.45), channel_id=1, source_target_pairs={{0,3},{1,2},{2,1},{3,0},{4,7},{5,6},{6,5},{7,4},{8,11},{9,10},{10,... | collective-permute-start | bytes 208904 | tf_op jit(solution)/shard_map/ppermute | solution.py:458
  32.5 4.2 %collective-permute-start.9 = (bf16[8,16,128]{2,1,0:T(8,128)(2,1)S(1)}, bf16[8,16,128]{2,1,0:T(8,128)(2,1)S(1)}, u32[]{:S(2)}, u32[]{:S(2)}) collective-permute-start(bf16[8,16,128]{2,1,0:T(8,128)(2,1)S(1)} %get-tuple-element.46), channel_id=1, source_target_pairs={{0,8},{8,0},{16,24},{24,16},{1,9},{9,1},{17,25},{25,17},{2,10},{10... | collective-permute-start | bytes 98312 | tf_op jit(solution)/shard_map/ppermute | solution.py:457
  33.2 5.7 %collective-permute-start.10 = (bf16[8,16,128]{2,1,0:T(8,128)(2,1)S(1)}, bf16[8,16,128]{2,1,0:T(8,128)(2,1)S(1)}, u32[]{:S(2)}, u32[]{:S(2)}) collective-permute-start(bf16[8,16,128]{2,1,0:T(8,128)(2,1)S(1)} %get-tuple-element.47), channel_id=1, source_target_pairs={{0,24},{8,16},{16,8},{24,0},{1,25},{9,17},{17,9},{25,1},{2,26},{10... | collective-permute-start | bytes 98312 | tf_op jit(solution)/shard_map/ppermute | solution.py:458
  34.6 6.2 %collective-permute-start.11 = (bf16[2,8,16,128]{3,2,1,0:T(8,128)(2,1)S(1)}, bf16[2,8,16,128]{3,2,1,0:T(8,128)(2,1)S(1)}, u32[]{:S(2)}, u32[]{:S(2)}) collective-permute-start(bf16[2,8,16,128]{3,2,1,0:T(8,128)(2,1)S(1)} %get-tuple-element.37), channel_id=1, source_target_pairs={{0,16},{8,24},{16,0},{24,8},{1,17},{9,25},{17,1},{25,9},{2,18},{10... | collective-permute-start | bytes 196616 | tf_op jit(solution)/shard_map/ppermute | solution.py:455
  36.1 4.8 %collective-permute-start.8 = (bf16[2,9,16,128]{3,2,1,0:T(8,128)(2,1)S(1)}, bf16[2,9,16,128]{3,2,1,0:T(8,128)(2,1)S(1)}, u32[]{:S(2)}, u32[]{:S(2)}) collective-permute-start(bf16[2,9,16,128]{3,2,1,0:T(8,128)(2,1)S(1)} %get-tuple-element.35), channel_id=1, source_target_pairs={{0,4},{4,0},{1,5},{5,1},{2,6},{6,2},{3,7},{7,3},{8,12},{12,8},{9,1... | collective-permute-start | bytes 221192 | tf_op jit(solution)/shard_map/ppermute | solution.py:455
  36.7 2.2 %collective-permute-start.6 = (bf16[17,16,128]{2,1,0:T(8,128)(2,1)S(1)}, bf16[17,16,128]{2,1,0:T(8,128)(2,1)S(1)}, u32[]{:S(2)}, u32[]{:S(2)}) collective-permute-start(bf16[17,16,128]{2,1,0:T(8,128)(2,1)S(1)} %get-tuple-element.42), channel_id=1, source_target_pairs={{0,1},{1,0},{2,3},{3,2},{4,5},{5,4},{6,7},{7,6},{8,9},{9,8},{10,11... | collective-permute-start | bytes 208904 | tf_op jit(solution)/shard_map/ppermute | solution.py:457
  36.7 4.0 %collective-permute-start.7 = (bf16[17,16,128]{2,1,0:T(8,128)(2,1)S(1)}, bf16[17,16,128]{2,1,0:T(8,128)(2,1)S(1)}, u32[]{:S(2)}, u32[]{:S(2)}) collective-permute-start(bf16[17,16,128]{2,1,0:T(8,128)(2,1)S(1)} %get-tuple-element.43), channel_id=1, source_target_pairs={{0,3},{1,2},{2,1},{3,0},{4,7},{5,6},{6,5},{7,4},{8,11},{9,10},{10,... | collective-permute-start | bytes 208904 | tf_op jit(solution)/shard_map/ppermute | solution.py:458

commit v5 on v4

--- a/solution.py
+++ b/solution.py
@@ -196,6 +196,14 @@
     return jnp.sum(top[0], axis=1, keepdims=True) / jnp.sum(bottom[0], axis=1, keepdims=True)
 
 
+def came_slots(kinds):
+    return [lax.axis_index(AXES[d]) % 2 if kinds[d] == "pairs" else 0 for d in range(4)]
+
+
+def sent_slots(kinds):
+    return [1 - slot if kind == "pairs" else 0 for kind, slot in zip(kinds, came_slots(kinds))]
+
+
 def smooth(box, flips, field, links, own, outs, scratch, prepare=None):
     update, image, sends = outs
     back, map_a, map_b, second = scratch
@@ -234,9 +242,8 @@
             sends[d][1 - flip, j] = jnp.concatenate(block, axis=0).astype(BF16)
 
 
-def first_kernel(
-    box, parts, flips, rhs_in, own_in, hop_in, *refs
-):
+def first_kernel(box, parts, kinds, rhs_in, own_in, hop_in, *refs):
+    flips = sent_slots(kinds)
     update, image, send0, send1, send2, send3, links, own = refs[:8]
     field, back, map_a, map_b, second, rhs, own_raw, hop, sems = refs[8:]
     each = box.count // parts
@@ -288,7 +295,8 @@
     smooth(box, flips, field, links, own, (update, image, (send0, send1, send2, send3)), scratch, prepare)
 
 
-def second_kernel(box, flips, rhs, mapped, sums, links, own, update, image, send0, send1, send2, send3, field, *scratch):
+def second_kernel(box, kinds, rhs, mapped, sums, links, own, update, image, send0, send1, send2, send3, field, *scratch):
+    flips = sent_slots(kinds)
     top, square = unpacked_sums(sums, 2, mapped.shape[1])
     alpha = top / square
     for s in range(box.count):
@@ -368,10 +376,10 @@
     ]
 
 
-def third_kernel(box, flips, rhs, image, links, came3, came2, came1, came0, mapped, sums):
+def third_kernel(box, kinds, rhs, image, links, came3, came2, came1, came0, mapped, sums):
     rows, lanes = image.shape[1:]
     low, _ = lane_tools(rows, lanes)
-    joined_halo(box, flips, image, links, (came0, came1, came2, came3), mapped, low)
+    joined_halo(box, came_slots(kinds), image, links, (came0, came1, came2, came3), mapped, low)
     zero = jnp.zeros((rows, lanes), F32)
     top = zero
     bottom = zero
@@ -382,10 +390,10 @@
     packed_sums((top, bottom), sums)
 
 
-def fourth_kernel(box, flips, rhs, first, before, image, links, came3, came2, came1, came0, mapped, sums):
+def fourth_kernel(box, kinds, rhs, first, before, image, links, came3, came2, came1, came0, mapped, sums):
     rows, lanes = image.shape[1:]
     low, _ = lane_tools(rows, lanes)
-    joined_halo(box, flips, image, links, (came0, came1, came2, came3), mapped, low)
+    joined_halo(box, came_slots(kinds), image, links, (came0, came1, came2, came3), mapped, low)
     top, square = unpacked_sums(before, 2, rows)
     alpha = top / square
     total = [jnp.zeros((rows, lanes), F32) for _ in range(4)]
@@ -413,16 +421,12 @@
         residual_out[s] = rhs[s] - alpha * old - step * (map_b[s][:, :half] - beta * old)
 
 
-def call(body, outs, scratch, ins, flips=None, space=pltpu.VMEM):
+def call(body, outs, scratch, ins, space=pltpu.VMEM):
     vmem = pl.BlockSpec(memory_space=pltpu.VMEM)
-    specs = [pl.BlockSpec(memory_space=space)] * len(ins)
-    if flips is not None:
-        specs.insert(0, pl.BlockSpec(memory_space=pltpu.SMEM))
-        ins = (flips, *ins)
     return pl.pallas_call(
         body,
         out_shape=outs,
-        in_specs=specs,
+        in_specs=[pl.BlockSpec(memory_space=space)] * len(ins),
         out_specs=[vmem] * len(outs),
         scratch_shapes=scratch,
         compiler_params=pltpu.CompilerParams(vmem_limit_bytes=VMEM_BYTES),
@@ -497,20 +501,7 @@
     own = self_coupling.reshape(count, channels, channels)
     hop = hopping.reshape(4, count, channels, channels)
 
-    flips_out = []
-    flips_in = []
-    for d in range(4):
-        axis, _, _, kind = plan(d)
-        if kind == "pairs":
-            odd = lax.axis_index(axis) % 2
-            flips_out.append(1 - odd)
-            flips_in.append(odd)
-        else:
-            flips_out.append(jnp.int32(0))
-            flips_in.append(jnp.int32(0))
-    flips_out = jnp.stack(flips_out).astype(jnp.int32)
-    flips_in = jnp.stack(flips_in).astype(jnp.int32)
-
+    kinds = [plan(d)[3] for d in range(4)]
     full = jax.ShapeDtypeStruct((count, rows, lanes), F32)
     small = jax.ShapeDtypeStruct((sum_rows(), lanes), F32)
     narrow = jax.ShapeDtypeStruct((count, rows, channels), F32)
@@ -533,32 +524,29 @@
     scratch = [field_scratch, back_scratch, field_scratch, field_scratch, field_scratch]
 
     update_a, image_a, *sends, links, own = call(
-        functools.partial(first_kernel, box, parts),
+        functools.partial(first_kernel, box, parts, kinds),
         [full, full, *send_shapes, links_shape, own_shape],
         scratch + raw,
         [pltpu.with_memory_space_constraint(a, pltpu.HBM) for a in (source, own, hop)],
-        flips_out,
         pltpu.HBM,
     )
     came = exchange(sends)
     map_a, sums_a = call(
-        functools.partial(third_kernel, box), [full, small], [], (source, image_a, links, *came[::-1]), flips_in
+        functools.partial(third_kernel, box, kinds), [full, small], [], (source, image_a, links, *came[::-1])
     )
     sums_a = mesh_sum(sums_a)
     update_b, image_b, *sends = call(
-        functools.partial(second_kernel, box),
+        functools.partial(second_kernel, box, kinds),
         [full, full, *send_shapes],
         scratch,
         (source, map_a, sums_a, links, own),
-        flips_out,
     )
     came = exchange(sends)
     map_b, sums_b = call(
-        functools.partial(fourth_kernel, box),
+        functools.partial(fourth_kernel, box, kinds),
         [full, small],
         [],
         (source, map_a, sums_a, image_b, links, *came[::-1]),
-        flips_in,
     )
     sums_b = mesh_sum(sums_b)
     found, left = call(

time: 52.8 us -> 50.5 us (0.956)
  Pallas kernels: 11.3 us -> 9.08 us
    pallas_call x5, Pallas kernels: 11.3 us -> 9.08 us  [call(): pl.pallas_call(body, out_shape=outs, in_specs=[pl.BlockSpec(memory_space=...]
where the time goes in v5:
time: 50.5 us; the launch traced here: 50.3 us
  blocking collectives  20.7 us (41%)
  starting transfers between devices  13.8 us (27%)
  Pallas kernels  9.08 us (18%)
  waiting for transfers between devices  5.94 us (12%)
  between operations  0.75 us (1%)
    all_to_all x2, blocking collectives, mesh_sum(): return lax.all_to_all(value, ('gx', 'gz', 'ta'), 0, 0, tiled=True)  20.7 us
    pallas_call x5, Pallas kernels, call(): pl.pallas_call(body, out_shape=outs, in_specs=[pl.BlockSpec(memory_space=...  9.08 us
    ppermute x4, starting transfers between devices, exchange(): lax.ppermute(sends[d][1], axis, [(i, (i + 1 if i % 2 else i - 1) % size)...  6.29 us
    ppermute x4, waiting for transfers between devices, exchange(): lax.ppermute(sends[d][1], axis, [(i, (i + 1 if i % 2 else i - 1) % size)...  5.58 us
    ppermute x4, starting transfers between devices, exchange(): even = lax.ppermute(sends[d][0], axis, [(i, i ^ 1) for i in ring])  3.88 us
    ppermute x4, starting transfers between devices, exchange(): lax.ppermute(sends[d], axis, [(i, (i + step) % size) for i in ring])  3.6 us
  transfers between devices with their start and end apart: 12, of which 6 were waited for; matrix products, arithmetic and copies ran while one was open for 0% of the time, Pallas kernels for 0%

profile of v5, /device:TPU:0, one launch (start us, length us, event | category | flops | bytes accessed | tf_op | source)
XLA Modules:
  0.0 50.3 jit_solution(2179015112580774774)
XLA Ops:
  0.6 0.0 copy-start
  0.6 4.6 %shard_map.50 = (f32[64,8,128]{2,1,0:T(8,128)S(1)}, f32[64,8,128]{2,1,0:T(8,128)S(1)}, bf16[2,8,16,128]{3,2,1,0:T(8,128)(2,1)S(1)}, bf16[2,8,16,128]{3,2,1,0:T(8...) custom-call(f32[64,8,64]{2,1,0:T(8,128)} %bitcast.37, ...), custom_call_target="tpu_custom_call" | custom-call | tf_op jit(solution)/shard_map/pallas_call | solution.py:426
  5.3 3.1 %collective-permute-start.3 = (bf16[8,16,128]{2,1,0:T(8,128)(2,1)S(1)}, bf16[8,16,128]{2,1,0:T(8,128)(2,1)S(1)}, u32[]{:S(2)}, u32[]{:S(2)}) collective-permute-start(bf16[8,16,128]{2,1,0:T(8,128)(2,1)S(1)} %get-tuple-element.48), channel_id=1, source_target_pairs={{0,8},{8,0},{16,24},{24,16},{1,9},{9,1},{17,25},{25,17},{2,10},{10... | collective-permute-start | bytes 98312 | tf_op jit(solution)/shard_map/ppermute | solution.py:461
  8.3 2.5 %collective-permute-start.4 = (bf16[8,16,128]{2,1,0:T(8,128)(2,1)S(1)}, bf16[8,16,128]{2,1,0:T(8,128)(2,1)S(1)}, u32[]{:S(2)}, u32[]{:S(2)}) collective-permute-start(bf16[8,16,128]{2,1,0:T(8,128)(2,1)S(1)} %get-tuple-element.49), channel_id=1, source_target_pairs={{0,24},{8,16},{16,8},{24,0},{1,25},{9,17},{17,9},{25,1},{2,26},{10... | collective-permute-start | bytes 98312 | tf_op jit(solution)/shard_map/ppermute | solution.py:462
  10.8 0.1 collective-permute-start.5
  10.9 1.5 %collective-permute-start.2 = (bf16[2,9,16,128]{3,2,1,0:T(8,128)(2,1)S(1)}, bf16[2,9,16,128]{3,2,1,0:T(8,128)(2,1)S(1)}, u32[]{:S(2)}, u32[]{:S(2)}) collective-permute-start(bf16[2,9,16,128]{3,2,1,0:T(8,128)(2,1)S(1)} %get-tuple-element.26), channel_id=1, source_target_pairs={{0,4},{4,0},{1,5},{5,1},{2,6},{6,2},{3,7},{7,3},{8,12},{12,8},{9,1... | collective-permute-start | bytes 221192 | tf_op jit(solution)/shard_map/ppermute | solution.py:459
  12.4 0.1 collective-permute-start
  12.5 0.0 collective-permute-done.3
  12.5 1.6 %collective-permute-start.1 = (bf16[17,16,128]{2,1,0:T(8,128)(2,1)S(1)}, bf16[17,16,128]{2,1,0:T(8,128)(2,1)S(1)}, u32[]{:S(2)}, u32[]{:S(2)}) collective-permute-start(bf16[17,16,128]{2,1,0:T(8,128)(2,1)S(1)} %get-tuple-element.45), channel_id=1, source_target_pairs={{0,3},{1,2},{2,1},{3,0},{4,7},{5,6},{6,5},{7,4},{8,11},{9,10},{10,... | collective-permute-start | bytes 208904 | tf_op jit(solution)/shard_map/ppermute | solution.py:462
  14.2 0.4 collective-permute-done.4
  14.5 0.0 collective-permute-done
  14.5 2.0 %collective-permute-done.1 = bf16[17,16,128]{2,1,0:T(8,128)(2,1)S(1)} collective-permute-done((bf16[17,16,128]{2,1,0:T(8,128)(2,1)S(1)}, bf16[17,16,128]{2,1,0:T(8,128)(2,1)S(1)}, u32[]{:S(2)}, u32[]{:S(2)}) %collective-permute-start.1) | collective-permute-done | bytes 69664 | tf_op jit(solution)/shard_map/ppermute | solution.py:462
  16.5 0.2 collective-permute-done.5.came0
  16.7 0.0 collective-permute-done.2.came2
  16.8 0.0 copy-done
  16.8 0.5 %shard_map.51 = (f32[64,8,128]{2,1,0:T(8,128)S(1)}, f32[32,128]{1,0:T(8,128)S(1)}) custom-call(f32[64,8,64]{2,1,0:T(8,128)S(1)} %bitcast.38, f32[64,8,128]{2,1,0:T(8,128)S(1)} %get-tuple-element.23.image, bf16[64,64,256]{2,1,0:T(8,128)(2,1)S(1)} %get-tuple-element.24.links, bf16[2,17,16,128]{3,2,1,0:T(8,128)(2,1)S(1)} %pad_maximum_fusion.came3, ...), custom_call_target="tpu_custom_call" | custom-call | tf_op jit(solution)/shard_map/pallas_call | solution.py:426
  17.3 11.1 %all_to_all.22 = f32[32,1,128]{2,1,0:T(1,128)S(1)} all-to-all(f32[32,1,128]{2,1,0:T(1,128)S(1)} %bitcast.47), channel_id=1, replica_groups=mesh['gx'=4,'gz'=2,'ta'=4] {'gx','gz','ta'}, dimensions={0} | all-to-all | bytes 32768 | tf_op jit(solution)/shard_map/all_to_all | solution.py:481
  28.4 2.4 %shard_map.52 = (f32[64,8,128]{2,1,0:T(8,128)S(1)}, f32[64,8,128]{2,1,0:T(8,128)S(1)}, bf16[2,8,16,128]{3,2,1,0:T(8,128)(2,1)S(1)}, bf16[2,8,16,128]{3,2,1,0:T(8...) custom-call(f32[64,8,64]{2,1,0:T(8,128)S(1)} %bitcast.39, ...), custom_call_target="tpu_custom_call" | custom-call | tf_op jit(solution)/shard_map/pallas_call | solution.py:426
  30.8 0.6 %collective-permute-start.9 = (bf16[8,16,128]{2,1,0:T(8,128)(2,1)S(1)}, bf16[8,16,128]{2,1,0:T(8,128)(2,1)S(1)}, u32[]{:S(2)}, u32[]{:S(2)}) collective-permute-start(bf16[8,16,128]{2,1,0:T(8,128)(2,1)S(1)} %get-tuple-element.46), channel_id=1, source_target_pairs={{0,8},{8,0},{16,24},{24,16},{1,9},{9,1},{17,25},{25,17},{2,10},{10... | collective-permute-start | bytes 98312 | tf_op jit(solution)/shard_map/ppermute | solution.py:461
  31.5 1.5 %collective-permute-start.10 = (bf16[8,16,128]{2,1,0:T(8,128)(2,1)S(1)}, bf16[8,16,128]{2,1,0:T(8,128)(2,1)S(1)}, u32[]{:S(2)}, u32[]{:S(2)}) collective-permute-start(bf16[8,16,128]{2,1,0:T(8,128)(2,1)S(1)} %get-tuple-element.47), channel_id=1, source_target_pairs={{0,24},{8,16},{16,8},{24,0},{1,25},{9,17},{17,9},{25,1},{2,26},{10... | collective-permute-start | bytes 98312 | tf_op jit(solution)/shard_map/ppermute | solution.py:462
  32.9 1.4 %collective-permute-start.11 = (bf16[2,8,16,128]{3,2,1,0:T(8,128)(2,1)S(1)}, bf16[2,8,16,128]{3,2,1,0:T(8,128)(2,1)S(1)}, u32[]{:S(2)}, u32[]{:S(2)}) collective-permute-start(bf16[2,8,16,128]{3,2,1,0:T(8,128)(2,1)S(1)} %get-tuple-element.37), channel_id=1, source_target_pairs={{0,16},{8,24},{16,0},{24,8},{1,17},{9,25},{17,1},{25,9},{2,18},{10... | collective-permute-start | bytes 196616 | tf_op jit(solution)/shard_map/ppermute | solution.py:459
  34.4 0.6 %collective-permute-start.8 = (bf16[2,9,16,128]{3,2,1,0:T(8,128)(2,1)S(1)}, bf16[2,9,16,128]{3,2,1,0:T(8,128)(2,1)S(1)}, u32[]{:S(2)}, u32[]{:S(2)}) collective-permute-start(bf16[2,9,16,128]{3,2,1,0:T(8,128)(2,1)S(1)} %get-tuple-element.35), channel_id=1, source_target_pairs={{0,4},{4,0},{1,5},{5,1},{2,6},{6,2},{3,7},{7,3},{8,12},{12,8},{9,1... | collective-permute-start | bytes 221192 | tf_op jit(solution)/shard_map/ppermute | solution.py:459
  35.0 0.1 collective-permute-start.6
  35.0 0.0 collective-permute-done.9
  35.0 0.7 %collective-permute-start.7 = (bf16[17,16,128]{2,1,0:T(8,128)(2,1)S(1)}, bf16[17,16,128]{2,1,0:T(8,128)(2,1)S(1)}, u32[]{:S(2)}, u32[]{:S(2)}) collective-permute-start(bf16[17,16,128]{2,1,0:T(8,128)(2,1)S(1)} %get-tuple-element.43), channel_id=1, source_target_pairs={{0,3},{1,2},{2,1},{3,0},{4,7},{5,6},{6,5},{7,4},{8,11},{9,10},{10,... | collective-permute-start | bytes 208904 | tf_op jit(solution)/shard_map/ppermute | solution.py:462
  35.8 1.4 %collective-permute-done.10 = bf16[8,16,128]{2,1,0:T(8,128)(2,1)S(1)} collective-permute-done((bf16[8,16,128]{2,1,0:T(8,128)(2,1)S(1)}, bf16[8,16,128]{2,1,0:T(8,128)(2,1)S(1)}, u32[]{:S(2)}, u32[]{:S(2)}) %collective-permute-start.10) | collective-permute-done | bytes 32800 | tf_op jit(solution)/shard_map/ppermute | solution.py:462
  37.2 0.0 collective-permute-done.6
  37.2 1.8 %collective-permute-done.7 = bf16[17,16,128]{2,1,0:T(8,128)(2,1)S(1)} collective-permute-done((bf16[17,16,128]{2,1,0:T(8,128)(2,1)S(1)}, bf16[17,16,128]{2,1,0:T(8,128)(2,1)S(1)}, u32[]{:S(2)}, u32[]{:S(2)}) %collective-permute-start.7) | collective-permute-done | bytes 69664 | tf_op jit(solution)/shard_map/ppermute | solution.py:462
  39.0 0.1 collective-permute-done.11.came0
  39.2 0.0 collective-permute-done.8.came2
  39.2 0.5 %shard_map.53 = (f32[64,8,128]{2,1,0:T(8,128)S(1)}, f32[32,128]{1,0:T(8,128)S(1)}) custom-call(f32[64,8,64]{2,1,0:T(8,128)S(1)} %bitcast.40, f32[64,8,128]{2,1,0:T(8,128)S(1)} %get-tuple-element.29.mapped.first.map_a, f32[32,128]{1,0:T(8,128)S(1)} %bitcast.43, f32[64,8,128]{2,1,0:T(8,128)S(1)} %get-tuple-element.33.image, ...), custom_call_target="tpu_custom_call" | custom-call | tf_op jit(solution)/shard_map/pallas_call | solution.py:426
  39.7 9.6 %all_to_all.23 = f32[32,1,128]{2,1,0:T(1,128)S(1)} all-to-all(f32[32,1,128]{2,1,0:T(1,128)S(1)} %bitcast.46), channel_id=1, replica_groups=mesh['gx'=4,'gz'=2,'ta'=4] {'gx','gz','ta'}, dimensions={0} | all-to-all | bytes 32768 | tf_op jit(solution)/shard_map/all_to_all | solution.py:481
  49.4 1.0 %shard_map.54 = (f32[64,8,64]{2,1,0:T(8,128)}, f32[64,8,64]{2,1,0:T(8,128)}) custom-call(f32[64,8,64]{2,1,0:T(8,128)S(1)} %bitcast.41, f32[64,8,128]{2,1,0:T(8,128)S(1)} %get-tuple-element.22.update_a, f32[64,8,128]{2,1,0:T(8,128)S(1)} %get-tuple-element.29.mapped.first.map_a, f32[64,8,128]{2,1,0:T(8,128)S(1)} %get-tuple-element.32.update_b, ...), custom_call_target="tpu_custom_call" | custom-call | tf_op jit(solution)/shard_map/pallas_call | solution.py:426
  (8 shorter events, 0.1 us)
Async XLA Ops:
  0.6 16.1 %copy-start = (f32[1,2,2,4,4,8,64]{6,5,4,3,2,1,0:T(8,128)S(1)}, f32[1,2,2,4,4,8,64]{6,5,4,3,2,1,0:T(8,128)}, u32[]{:S(2)}) copy-start(f32[1,2,2,4,4,8,64]{6,5,4,3,2,1,0:T(8,128)} %param.3) | copy-start | bytes 393220
  5.3 7.3 %collective-permute-start.3 = (bf16[8,16,128]{2,1,0:T(8,128)(2,1)S(1)}, bf16[8,16,128]{2,1,0:T(8,128)(2,1)S(1)}, u32[]{:S(2)}, u32[]{:S(2)}) collective-permute-start(bf16[8,16,128]{2,1,0:T(8,128)(2,1)S(1)} %get-tuple-element.48), channel_id=1, source_target_pairs={{0,8},{8,0},{16,24},{24,16},{1,9},{9,1},{17,25},{25,17},{2,10},{10... | collective-permute-start | bytes 98312 | tf_op jit(solution)/shard_map/ppermute | solution.py:461
  8.3 6.2 %collective-permute-start.4 = (bf16[8,16,128]{2,1,0:T(8,128)(2,1)S(1)}, bf16[8,16,128]{2,1,0:T(8,128)(2,1)S(1)}, u32[]{:S(2)}, u32[]{:S(2)}) collective-permute-start(bf16[8,16,128]{2,1,0:T(8,128)(2,1)S(1)} %get-tuple-element.49), channel_id=1, source_target_pairs={{0,24},{8,16},{16,8},{24,0},{1,25},{9,17},{17,9},{25,1},{2,26},{10... | collective-permute-start | bytes 98312 | tf_op jit(solution)/shard_map/ppermute | solution.py:462
  10.8 5.9 %collective-permute-start.5 = (bf16[2,8,16,128]{3,2,1,0:T(8,128)(2,1)S(1)}, bf16[2,8,16,128]{3,2,1,0:T(8,128)(2,1)S(1)}, u32[]{:S(2)}, u32[]{:S(2)}) collective-permute-start(bf16[2,8,16,128]{3,2,1,0:T(8,128)(2,1)S(1)} %get-tuple-element.28), channel_id=1, source_target_pairs={{0,16},{8,24},{16,0},{24,8},{1,17},{9,25},{17,1},{25,9},{2,18},{10... | collective-permute-start | bytes 196616 | tf_op jit(solution)/shard_map/ppermute | solution.py:459
  10.9 5.8 %collective-permute-start.2 = (bf16[2,9,16,128]{3,2,1,0:T(8,128)(2,1)S(1)}, bf16[2,9,16,128]{3,2,1,0:T(8,128)(2,1)S(1)}, u32[]{:S(2)}, u32[]{:S(2)}) collective-permute-start(bf16[2,9,16,128]{3,2,1,0:T(8,128)(2,1)S(1)} %get-tuple-element.26), channel_id=1, source_target_pairs={{0,4},{4,0},{1,5},{5,1},{2,6},{6,2},{3,7},{7,3},{8,12},{12,8},{9,1... | collective-permute-start | bytes 221192 | tf_op jit(solution)/shard_map/ppermute | solution.py:459
  12.4 2.1 %collective-permute-start = (bf16[17,16,128]{2,1,0:T(8,128)(2,1)S(1)}, bf16[17,16,128]{2,1,0:T(8,128)(2,1)S(1)}, u32[]{:S(2)}, u32[]{:S(2)}) collective-permute-start(bf16[17,16,128]{2,1,0:T(8,128)(2,1)S(1)} %get-tuple-element.44), channel_id=1, source_target_pairs={{0,1},{1,0},{2,3},{3,2},{4,5},{5,4},{6,7},{7,6},{8,9},{9,8},{10,11... | collective-permute-start | bytes 208904 | tf_op jit(solution)/shard_map/ppermute | solution.py:461
  12.5 4.0 %collective-permute-start.1 = (bf16[17,16,128]{2,1,0:T(8,128)(2,1)S(1)}, bf16[17,16,128]{2,1,0:T(8,128)(2,1)S(1)}, u32[]{:S(2)}, u32[]{:S(2)}) collective-permute-start(bf16[17,16,128]{2,1,0:T(8,128)(2,1)S(1)} %get-tuple-element.45), channel_id=1, source_target_pairs={{0,3},{1,2},{2,1},{3,0},{4,7},{5,6},{6,5},{7,4},{8,11},{9,10},{10,... | collective-permute-start | bytes 208904 | tf_op jit(solution)/shard_map/ppermute | solution.py:462
  30.8 4.2 %collective-permute-start.9 = (bf16[8,16,128]{2,1,0:T(8,128)(2,1)S(1)}, bf16[8,16,128]{2,1,0:T(8,128)(2,1)S(1)}, u32[]{:S(2)}, u32[]{:S(2)}) collective-permute-start(bf16[8,16,128]{2,1,0:T(8,128)(2,1)S(1)} %get-tuple-element.46), channel_id=1, source_target_pairs={{0,8},{8,0},{16,24},{24,16},{1,9},{9,1},{17,25},{25,17},{2,10},{10... | collective-permute-start | bytes 98312 | tf_op jit(solution)/shard_map/ppermute | solution.py:461
  31.5 5.7 %collective-permute-start.10 = (bf16[8,16,128]{2,1,0:T(8,128)(2,1)S(1)}, bf16[8,16,128]{2,1,0:T(8,128)(2,1)S(1)}, u32[]{:S(2)}, u32[]{:S(2)}) collective-permute-start(bf16[8,16,128]{2,1,0:T(8,128)(2,1)S(1)} %get-tuple-element.47), channel_id=1, source_target_pairs={{0,24},{8,16},{16,8},{24,0},{1,25},{9,17},{17,9},{25,1},{2,26},{10... | collective-permute-start | bytes 98312 | tf_op jit(solution)/shard_map/ppermute | solution.py:462
  32.9 6.2 %collective-permute-start.11 = (bf16[2,8,16,128]{3,2,1,0:T(8,128)(2,1)S(1)}, bf16[2,8,16,128]{3,2,1,0:T(8,128)(2,1)S(1)}, u32[]{:S(2)}, u32[]{:S(2)}) collective-permute-start(bf16[2,8,16,128]{3,2,1,0:T(8,128)(2,1)S(1)} %get-tuple-element.37), channel_id=1, source_target_pairs={{0,16},{8,24},{16,0},{24,8},{1,17},{9,25},{17,1},{25,9},{2,18},{10... | collective-permute-start | bytes 196616 | tf_op jit(solution)/shard_map/ppermute | solution.py:459
  34.4 4.8 %collective-permute-start.8 = (bf16[2,9,16,128]{3,2,1,0:T(8,128)(2,1)S(1)}, bf16[2,9,16,128]{3,2,1,0:T(8,128)(2,1)S(1)}, u32[]{:S(2)}, u32[]{:S(2)}) collective-permute-start(bf16[2,9,16,128]{3,2,1,0:T(8,128)(2,1)S(1)} %get-tuple-element.35), channel_id=1, source_target_pairs={{0,4},{4,0},{1,5},{5,1},{2,6},{6,2},{3,7},{7,3},{8,12},{12,8},{9,1... | collective-permute-start | bytes 221192 | tf_op jit(solution)/shard_map/ppermute | solution.py:459
  35.0 2.2 %collective-permute-start.6 = (bf16[17,16,128]{2,1,0:T(8,128)(2,1)S(1)}, bf16[17,16,128]{2,1,0:T(8,128)(2,1)S(1)}, u32[]{:S(2)}, u32[]{:S(2)}) collective-permute-start(bf16[17,16,128]{2,1,0:T(8,128)(2,1)S(1)} %get-tuple-element.42), channel_id=1, source_target_pairs={{0,1},{1,0},{2,3},{3,2},{4,5},{5,4},{6,7},{7,6},{8,9},{9,8},{10,11... | collective-permute-start | bytes 208904 | tf_op jit(solution)/shard_map/ppermute | solution.py:461
  35.0 4.0 %collective-permute-start.7 = (bf16[17,16,128]{2,1,0:T(8,128)(2,1)S(1)}, bf16[17,16,128]{2,1,0:T(8,128)(2,1)S(1)}, u32[]{:S(2)}, u32[]{:S(2)}) collective-permute-start(bf16[17,16,128]{2,1,0:T(8,128)(2,1)S(1)} %get-tuple-element.43), channel_id=1, source_target_pairs={{0,3},{1,2},{2,1},{3,0},{4,7},{5,6},{6,5},{7,4},{8,11},{9,10},{10,... | collective-permute-start | bytes 208904 | tf_op jit(solution)/shard_map/ppermute | solution.py:462

commit v6 on v5

--- a/solution.py
+++ b/solution.py
@@ -13,7 +13,7 @@
 NN = (((1,), (0,)), ((), ()))
 VMEM_BYTES = 24 * 2**20
 GROUP = 4
-LAG = 2
+LAG = 4
 AXES = ("gx", "gx", "gz", "ta")
 
 
@@ -246,10 +246,11 @@
     flips = sent_slots(kinds)
     update, image, send0, send1, send2, send3, links, own = refs[:8]
     field, back, map_a, map_b, second, rhs, own_raw, hop, sems = refs[8:]
-    each = box.count // parts
+    groups = box.count // GROUP
+    bounds = [0, GROUP * (groups // 4), GROUP * (groups * 5 // 8), box.count]
     copies = [pltpu.make_async_copy(rhs_in, rhs, sems.at[2 * parts])]
     for c in range(parts):
-        run = pl.ds(c * each, each)
+        run = pl.ds(bounds[c], bounds[c + 1] - bounds[c])
         copies.append(pltpu.make_async_copy(hop_in.at[:, run], hop.at[:, run], sems.at[2 * c]))
         copies.append(pltpu.make_async_copy(own_in.at[run], own_raw.at[run], sems.at[2 * c + 1]))
     for copy in copies:
@@ -263,7 +264,7 @@
     packed = [0]
 
     def await_site(s):
-        while arrived[0] * each <= s:
+        while bounds[arrived[0]] <= s:
             c = arrived[0]
             copies[2 * c + 1].wait()
             copies[2 * c + 2].wait()
@@ -285,7 +286,7 @@
             final = tile == len(inner.tiles) - 1
             if final:
                 await_site(box.count - 1)
-            while packed[0] < len(outer.tiles) and (final or outer.sites[packed[0]][-1] < arrived[0] * each):
+            while packed[0] < len(outer.tiles) and (final or outer.sites[packed[0]][-1] < bounds[arrived[0]]):
                 pack(outer, packed[0])
                 packed[0] += 1
                 if not final and packed[0] * len(inner.tiles) > (tile + 1) * len(outer.tiles):
@@ -509,7 +510,7 @@
     link_tiles = len(inner.tiles) + len(outer.tiles)
     links_shape = jax.ShapeDtypeStruct((link_tiles, channels, 4 * channels), BF16)
     own_shape = jax.ShapeDtypeStruct((count // GROUP, channels, GROUP * channels), BF16)
-    parts = extents[0] * extents[1]
+    parts = 3
     raw = [
         pltpu.VMEM(source.shape, F32),
         pltpu.VMEM(own.shape, BF16),

time: 50.5 us -> 50.5 us (level)
  no operation moved by 1% of the time
where the time goes in v6:
time: 50.5 us; the launch traced here: 50.3 us
  blocking collectives  20.7 us (41%)
  starting transfers between devices  13.8 us (27%)
  Pallas kernels  9.07 us (18%)
  waiting for transfers between devices  5.94 us (12%)
  between operations  0.75 us (1%)
    all_to_all x2, blocking collectives, mesh_sum(): return lax.all_to_all(value, ('gx', 'gz', 'ta'), 0, 0, tiled=True)  20.7 us
    pallas_call x5, Pallas kernels, call(): pl.pallas_call(body, out_shape=outs, in_specs=[pl.BlockSpec(memory_space=...  9.07 us
    ppermute x4, starting transfers between devices, exchange(): lax.ppermute(sends[d][1], axis, [(i, (i + 1 if i % 2 else i - 1) % size)...  6.3 us
    ppermute x4, waiting for transfers between devices, exchange(): lax.ppermute(sends[d][1], axis, [(i, (i + 1 if i % 2 else i - 1) % size)...  5.57 us
    ppermute x4, starting transfers between devices, exchange(): even = lax.ppermute(sends[d][0], axis, [(i, i ^ 1) for i in ring])  3.86 us
    ppermute x4, starting transfers between devices, exchange(): lax.ppermute(sends[d], axis, [(i, (i + step) % size) for i in ring])  3.6 us
  transfers between devices with their start and end apart: 12, of which 6 were waited for; matrix products, arithmetic and copies ran while one was open for 0% of the time, Pallas kernels for 0%

profile of v6, /device:TPU:0, one launch (start us, length us, event | category | flops | bytes accessed | tf_op | source)
XLA Modules:
  0.0 50.3 jit_solution(9069790062377400567)
XLA Ops:
  0.6 0.0 copy-start
  0.6 4.6 %shard_map.50 = (f32[64,8,128]{2,1,0:T(8,128)S(1)}, f32[64,8,128]{2,1,0:T(8,128)S(1)}, bf16[2,8,16,128]{3,2,1,0:T(8,128)(2,1)S(1)}, bf16[2,8,16,128]{3,2,1,0:T(8...) custom-call(f32[64,8,64]{2,1,0:T(8,128)} %bitcast.37, ...), custom_call_target="tpu_custom_call" | custom-call | tf_op jit(solution)/shard_map/pallas_call | solution.py:427
  5.2 3.1 %collective-permute-start.3 = (bf16[8,16,128]{2,1,0:T(8,128)(2,1)S(1)}, bf16[8,16,128]{2,1,0:T(8,128)(2,1)S(1)}, u32[]{:S(2)}, u32[]{:S(2)}) collective-permute-start(bf16[8,16,128]{2,1,0:T(8,128)(2,1)S(1)} %get-tuple-element.48), channel_id=1, source_target_pairs={{0,8},{8,0},{16,24},{24,16},{1,9},{9,1},{17,25},{25,17},{2,10},{10... | collective-permute-start | bytes 98312 | tf_op jit(solution)/shard_map/ppermute | solution.py:462
  8.3 2.5 %collective-permute-start.4 = (bf16[8,16,128]{2,1,0:T(8,128)(2,1)S(1)}, bf16[8,16,128]{2,1,0:T(8,128)(2,1)S(1)}, u32[]{:S(2)}, u32[]{:S(2)}) collective-permute-start(bf16[8,16,128]{2,1,0:T(8,128)(2,1)S(1)} %get-tuple-element.49), channel_id=1, source_target_pairs={{0,24},{8,16},{16,8},{24,0},{1,25},{9,17},{17,9},{25,1},{2,26},{10... | collective-permute-start | bytes 98312 | tf_op jit(solution)/shard_map/ppermute | solution.py:463
  10.8 0.1 collective-permute-start.5
  10.9 1.5 %collective-permute-start.2 = (bf16[2,9,16,128]{3,2,1,0:T(8,128)(2,1)S(1)}, bf16[2,9,16,128]{3,2,1,0:T(8,128)(2,1)S(1)}, u32[]{:S(2)}, u32[]{:S(2)}) collective-permute-start(bf16[2,9,16,128]{3,2,1,0:T(8,128)(2,1)S(1)} %get-tuple-element.26), channel_id=1, source_target_pairs={{0,4},{4,0},{1,5},{5,1},{2,6},{6,2},{3,7},{7,3},{8,12},{12,8},{9,1... | collective-permute-start | bytes 221192 | tf_op jit(solution)/shard_map/ppermute | solution.py:460
  12.4 0.1 collective-permute-start
  12.5 0.0 collective-permute-done.3
  12.5 1.6 %collective-permute-start.1 = (bf16[17,16,128]{2,1,0:T(8,128)(2,1)S(1)}, bf16[17,16,128]{2,1,0:T(8,128)(2,1)S(1)}, u32[]{:S(2)}, u32[]{:S(2)}) collective-permute-start(bf16[17,16,128]{2,1,0:T(8,128)(2,1)S(1)} %get-tuple-element.45), channel_id=1, source_target_pairs={{0,3},{1,2},{2,1},{3,0},{4,7},{5,6},{6,5},{7,4},{8,11},{9,10},{10,... | collective-permute-start | bytes 208904 | tf_op jit(solution)/shard_map/ppermute | solution.py:463
  14.1 0.3 collective-permute-done.4
  14.5 0.0 collective-permute-done
  14.5 2.0 %collective-permute-done.1 = bf16[17,16,128]{2,1,0:T(8,128)(2,1)S(1)} collective-permute-done((bf16[17,16,128]{2,1,0:T(8,128)(2,1)S(1)}, bf16[17,16,128]{2,1,0:T(8,128)(2,1)S(1)}, u32[]{:S(2)}, u32[]{:S(2)}) %collective-permute-start.1) | collective-permute-done | bytes 69664 | tf_op jit(solution)/shard_map/ppermute | solution.py:463
  16.5 0.2 collective-permute-done.5.came0
  16.7 0.0 collective-permute-done.2.came2
  16.7 0.0 copy-done
  16.7 0.5 %shard_map.51 = (f32[64,8,128]{2,1,0:T(8,128)S(1)}, f32[32,128]{1,0:T(8,128)S(1)}) custom-call(f32[64,8,64]{2,1,0:T(8,128)S(1)} %bitcast.38, f32[64,8,128]{2,1,0:T(8,128)S(1)} %get-tuple-element.23.image, bf16[64,64,256]{2,1,0:T(8,128)(2,1)S(1)} %get-tuple-element.24.links, bf16[2,17,16,128]{3,2,1,0:T(8,128)(2,1)S(1)} %pad_maximum_fusion.came3, ...), custom_call_target="tpu_custom_call" | custom-call | tf_op jit(solution)/shard_map/pallas_call | solution.py:427
  17.3 11.1 %all_to_all.22 = f32[32,1,128]{2,1,0:T(1,128)S(1)} all-to-all(f32[32,1,128]{2,1,0:T(1,128)S(1)} %bitcast.47), channel_id=1, replica_groups=mesh['gx'=4,'gz'=2,'ta'=4] {'gx','gz','ta'}, dimensions={0} | all-to-all | bytes 32768 | tf_op jit(solution)/shard_map/all_to_all | solution.py:482
  28.4 2.4 %shard_map.52 = (f32[64,8,128]{2,1,0:T(8,128)S(1)}, f32[64,8,128]{2,1,0:T(8,128)S(1)}, bf16[2,8,16,128]{3,2,1,0:T(8,128)(2,1)S(1)}, bf16[2,8,16,128]{3,2,1,0:T(8...) custom-call(f32[64,8,64]{2,1,0:T(8,128)S(1)} %bitcast.39, ...), custom_call_target="tpu_custom_call" | custom-call | tf_op jit(solution)/shard_map/pallas_call | solution.py:427
  30.8 0.6 %collective-permute-start.9 = (bf16[8,16,128]{2,1,0:T(8,128)(2,1)S(1)}, bf16[8,16,128]{2,1,0:T(8,128)(2,1)S(1)}, u32[]{:S(2)}, u32[]{:S(2)}) collective-permute-start(bf16[8,16,128]{2,1,0:T(8,128)(2,1)S(1)} %get-tuple-element.46), channel_id=1, source_target_pairs={{0,8},{8,0},{16,24},{24,16},{1,9},{9,1},{17,25},{25,17},{2,10},{10... | collective-permute-start | bytes 98312 | tf_op jit(solution)/shard_map/ppermute | solution.py:462
  31.4 1.5 %collective-permute-start.10 = (bf16[8,16,128]{2,1,0:T(8,128)(2,1)S(1)}, bf16[8,16,128]{2,1,0:T(8,128)(2,1)S(1)}, u32[]{:S(2)}, u32[]{:S(2)}) collective-permute-start(bf16[8,16,128]{2,1,0:T(8,128)(2,1)S(1)} %get-tuple-element.47), channel_id=1, source_target_pairs={{0,24},{8,16},{16,8},{24,0},{1,25},{9,17},{17,9},{25,1},{2,26},{10... | collective-permute-start | bytes 98312 | tf_op jit(solution)/shard_map/ppermute | solution.py:463
  32.9 1.4 %collective-permute-start.11 = (bf16[2,8,16,128]{3,2,1,0:T(8,128)(2,1)S(1)}, bf16[2,8,16,128]{3,2,1,0:T(8,128)(2,1)S(1)}, u32[]{:S(2)}, u32[]{:S(2)}) collective-permute-start(bf16[2,8,16,128]{3,2,1,0:T(8,128)(2,1)S(1)} %get-tuple-element.37), channel_id=1, source_target_pairs={{0,16},{8,24},{16,0},{24,8},{1,17},{9,25},{17,1},{25,9},{2,18},{10... | collective-permute-start | bytes 196616 | tf_op jit(solution)/shard_map/ppermute | solution.py:460
  34.4 0.6 %collective-permute-start.8 = (bf16[2,9,16,128]{3,2,1,0:T(8,128)(2,1)S(1)}, bf16[2,9,16,128]{3,2,1,0:T(8,128)(2,1)S(1)}, u32[]{:S(2)}, u32[]{:S(2)}) collective-permute-start(bf16[2,9,16,128]{3,2,1,0:T(8,128)(2,1)S(1)} %get-tuple-element.35), channel_id=1, source_target_pairs={{0,4},{4,0},{1,5},{5,1},{2,6},{6,2},{3,7},{7,3},{8,12},{12,8},{9,1... | collective-permute-start | bytes 221192 | tf_op jit(solution)/shard_map/ppermute | solution.py:460
  34.9 0.1 collective-permute-start.6
  35.0 0.0 collective-permute-done.9
  35.0 0.7 %collective-permute-start.7 = (bf16[17,16,128]{2,1,0:T(8,128)(2,1)S(1)}, bf16[17,16,128]{2,1,0:T(8,128)(2,1)S(1)}, u32[]{:S(2)}, u32[]{:S(2)}) collective-permute-start(bf16[17,16,128]{2,1,0:T(8,128)(2,1)S(1)} %get-tuple-element.43), channel_id=1, source_target_pairs={{0,3},{1,2},{2,1},{3,0},{4,7},{5,6},{6,5},{7,4},{8,11},{9,10},{10,... | collective-permute-start | bytes 208904 | tf_op jit(solution)/shard_map/ppermute | solution.py:463
  35.7 1.4 %collective-permute-done.10 = bf16[8,16,128]{2,1,0:T(8,128)(2,1)S(1)} collective-permute-done((bf16[8,16,128]{2,1,0:T(8,128)(2,1)S(1)}, bf16[8,16,128]{2,1,0:T(8,128)(2,1)S(1)}, u32[]{:S(2)}, u32[]{:S(2)}) %collective-permute-start.10) | collective-permute-done | bytes 32800 | tf_op jit(solution)/shard_map/ppermute | solution.py:463
  37.2 0.0 collective-permute-done.6
  37.2 1.8 %collective-permute-done.7 = bf16[17,16,128]{2,1,0:T(8,128)(2,1)S(1)} collective-permute-done((bf16[17,16,128]{2,1,0:T(8,128)(2,1)S(1)}, bf16[17,16,128]{2,1,0:T(8,128)(2,1)S(1)}, u32[]{:S(2)}, u32[]{:S(2)}) %collective-permute-start.7) | collective-permute-done | bytes 69664 | tf_op jit(solution)/shard_map/ppermute | solution.py:463
  39.0 0.1 collective-permute-done.11.came0
  39.2 0.0 collective-permute-done.8.came2
  39.2 0.5 %shard_map.53 = (f32[64,8,128]{2,1,0:T(8,128)S(1)}, f32[32,128]{1,0:T(8,128)S(1)}) custom-call(f32[64,8,64]{2,1,0:T(8,128)S(1)} %bitcast.40, f32[64,8,128]{2,1,0:T(8,128)S(1)} %get-tuple-element.29.mapped.first.map_a, f32[32,128]{1,0:T(8,128)S(1)} %bitcast.43, f32[64,8,128]{2,1,0:T(8,128)S(1)} %get-tuple-element.33.image, ...), custom_call_target="tpu_custom_call" | custom-call | tf_op jit(solution)/shard_map/pallas_call | solution.py:427
  39.7 9.6 %all_to_all.23 = f32[32,1,128]{2,1,0:T(1,128)S(1)} all-to-all(f32[32,1,128]{2,1,0:T(1,128)S(1)} %bitcast.46), channel_id=1, replica_groups=mesh['gx'=4,'gz'=2,'ta'=4] {'gx','gz','ta'}, dimensions={0} | all-to-all | bytes 32768 | tf_op jit(solution)/shard_map/all_to_all | solution.py:482
  49.3 1.0 %shard_map.54 = (f32[64,8,64]{2,1,0:T(8,128)}, f32[64,8,64]{2,1,0:T(8,128)}) custom-call(f32[64,8,64]{2,1,0:T(8,128)S(1)} %bitcast.41, f32[64,8,128]{2,1,0:T(8,128)S(1)} %get-tuple-element.22.update_a, f32[64,8,128]{2,1,0:T(8,128)S(1)} %get-tuple-element.29.mapped.first.map_a, f32[64,8,128]{2,1,0:T(8,128)S(1)} %get-tuple-element.32.update_b, ...), custom_call_target="tpu_custom_call" | custom-call | tf_op jit(solution)/shard_map/pallas_call | solution.py:427
  (8 shorter events, 0.1 us)
Async XLA Ops:
  0.6 16.1 %copy-start = (f32[1,2,2,4,4,8,64]{6,5,4,3,2,1,0:T(8,128)S(1)}, f32[1,2,2,4,4,8,64]{6,5,4,3,2,1,0:T(8,128)}, u32[]{:S(2)}) copy-start(f32[1,2,2,4,4,8,64]{6,5,4,3,2,1,0:T(8,128)} %param.3) | copy-start | bytes 393220
  5.2 7.3 %collective-permute-start.3 = (bf16[8,16,128]{2,1,0:T(8,128)(2,1)S(1)}, bf16[8,16,128]{2,1,0:T(8,128)(2,1)S(1)}, u32[]{:S(2)}, u32[]{:S(2)}) collective-permute-start(bf16[8,16,128]{2,1,0:T(8,128)(2,1)S(1)} %get-tuple-element.48), channel_id=1, source_target_pairs={{0,8},{8,0},{16,24},{24,16},{1,9},{9,1},{17,25},{25,17},{2,10},{10... | collective-permute-start | bytes 98312 | tf_op jit(solution)/shard_map/ppermute | solution.py:462
  8.3 6.2 %collective-permute-start.4 = (bf16[8,16,128]{2,1,0:T(8,128)(2,1)S(1)}, bf16[8,16,128]{2,1,0:T(8,128)(2,1)S(1)}, u32[]{:S(2)}, u32[]{:S(2)}) collective-permute-start(bf16[8,16,128]{2,1,0:T(8,128)(2,1)S(1)} %get-tuple-element.49), channel_id=1, source_target_pairs={{0,24},{8,16},{16,8},{24,0},{1,25},{9,17},{17,9},{25,1},{2,26},{10... | collective-permute-start | bytes 98312 | tf_op jit(solution)/shard_map/ppermute | solution.py:463
  10.8 5.9 %collective-permute-start.5 = (bf16[2,8,16,128]{3,2,1,0:T(8,128)(2,1)S(1)}, bf16[2,8,16,128]{3,2,1,0:T(8,128)(2,1)S(1)}, u32[]{:S(2)}, u32[]{:S(2)}) collective-permute-start(bf16[2,8,16,128]{3,2,1,0:T(8,128)(2,1)S(1)} %get-tuple-element.28), channel_id=1, source_target_pairs={{0,16},{8,24},{16,0},{24,8},{1,17},{9,25},{17,1},{25,9},{2,18},{10... | collective-permute-start | bytes 196616 | tf_op jit(solution)/shard_map/ppermute | solution.py:460
  10.9 5.8 %collective-permute-start.2 = (bf16[2,9,16,128]{3,2,1,0:T(8,128)(2,1)S(1)}, bf16[2,9,16,128]{3,2,1,0:T(8,128)(2,1)S(1)}, u32[]{:S(2)}, u32[]{:S(2)}) collective-permute-start(bf16[2,9,16,128]{3,2,1,0:T(8,128)(2,1)S(1)} %get-tuple-element.26), channel_id=1, source_target_pairs={{0,4},{4,0},{1,5},{5,1},{2,6},{6,2},{3,7},{7,3},{8,12},{12,8},{9,1... | collective-permute-start | bytes 221192 | tf_op jit(solution)/shard_map/ppermute | solution.py:460
  12.4 2.1 %collective-permute-start = (bf16[17,16,128]{2,1,0:T(8,128)(2,1)S(1)}, bf16[17,16,128]{2,1,0:T(8,128)(2,1)S(1)}, u32[]{:S(2)}, u32[]{:S(2)}) collective-permute-start(bf16[17,16,128]{2,1,0:T(8,128)(2,1)S(1)} %get-tuple-element.44), channel_id=1, source_target_pairs={{0,1},{1,0},{2,3},{3,2},{4,5},{5,4},{6,7},{7,6},{8,9},{9,8},{10,11... | collective-permute-start | bytes 208904 | tf_op jit(solution)/shard_map/ppermute | solution.py:462
  12.5 4.0 %collective-permute-start.1 = (bf16[17,16,128]{2,1,0:T(8,128)(2,1)S(1)}, bf16[17,16,128]{2,1,0:T(8,128)(2,1)S(1)}, u32[]{:S(2)}, u32[]{:S(2)}) collective-permute-start(bf16[17,16,128]{2,1,0:T(8,128)(2,1)S(1)} %get-tuple-element.45), channel_id=1, source_target_pairs={{0,3},{1,2},{2,1},{3,0},{4,7},{5,6},{6,5},{7,4},{8,11},{9,10},{10,... | collective-permute-start | bytes 208904 | tf_op jit(solution)/shard_map/ppermute | solution.py:463
  30.8 4.2 %collective-permute-start.9 = (bf16[8,16,128]{2,1,0:T(8,128)(2,1)S(1)}, bf16[8,16,128]{2,1,0:T(8,128)(2,1)S(1)}, u32[]{:S(2)}, u32[]{:S(2)}) collective-permute-start(bf16[8,16,128]{2,1,0:T(8,128)(2,1)S(1)} %get-tuple-element.46), channel_id=1, source_target_pairs={{0,8},{8,0},{16,24},{24,16},{1,9},{9,1},{17,25},{25,17},{2,10},{10... | collective-permute-start | bytes 98312 | tf_op jit(solution)/shard_map/ppermute | solution.py:462
  31.4 5.7 %collective-permute-start.10 = (bf16[8,16,128]{2,1,0:T(8,128)(2,1)S(1)}, bf16[8,16,128]{2,1,0:T(8,128)(2,1)S(1)}, u32[]{:S(2)}, u32[]{:S(2)}) collective-permute-start(bf16[8,16,128]{2,1,0:T(8,128)(2,1)S(1)} %get-tuple-element.47), channel_id=1, source_target_pairs={{0,24},{8,16},{16,8},{24,0},{1,25},{9,17},{17,9},{25,1},{2,26},{10... | collective-permute-start | bytes 98312 | tf_op jit(solution)/shard_map/ppermute | solution.py:463
  32.9 6.2 %collective-permute-start.11 = (bf16[2,8,16,128]{3,2,1,0:T(8,128)(2,1)S(1)}, bf16[2,8,16,128]{3,2,1,0:T(8,128)(2,1)S(1)}, u32[]{:S(2)}, u32[]{:S(2)}) collective-permute-start(bf16[2,8,16,128]{3,2,1,0:T(8,128)(2,1)S(1)} %get-tuple-element.37), channel_id=1, source_target_pairs={{0,16},{8,24},{16,0},{24,8},{1,17},{9,25},{17,1},{25,9},{2,18},{10... | collective-permute-start | bytes 196616 | tf_op jit(solution)/shard_map/ppermute | solution.py:460
  34.4 4.8 %collective-permute-start.8 = (bf16[2,9,16,128]{3,2,1,0:T(8,128)(2,1)S(1)}, bf16[2,9,16,128]{3,2,1,0:T(8,128)(2,1)S(1)}, u32[]{:S(2)}, u32[]{:S(2)}) collective-permute-start(bf16[2,9,16,128]{3,2,1,0:T(8,128)(2,1)S(1)} %get-tuple-element.35), channel_id=1, source_target_pairs={{0,4},{4,0},{1,5},{5,1},{2,6},{6,2},{3,7},{7,3},{8,12},{12,8},{9,1... | collective-permute-start | bytes 221192 | tf_op jit(solution)/shard_map/ppermute | solution.py:460
  34.9 2.2 %collective-permute-start.6 = (bf16[17,16,128]{2,1,0:T(8,128)(2,1)S(1)}, bf16[17,16,128]{2,1,0:T(8,128)(2,1)S(1)}, u32[]{:S(2)}, u32[]{:S(2)}) collective-permute-start(bf16[17,16,128]{2,1,0:T(8,128)(2,1)S(1)} %get-tuple-element.42), channel_id=1, source_target_pairs={{0,1},{1,0},{2,3},{3,2},{4,5},{5,4},{6,7},{7,6},{8,9},{9,8},{10,11... | collective-permute-start | bytes 208904 | tf_op jit(solution)/shard_map/ppermute | solution.py:462
  35.0 4.0 %collective-permute-start.7 = (bf16[17,16,128]{2,1,0:T(8,128)(2,1)S(1)}, bf16[17,16,128]{2,1,0:T(8,128)(2,1)S(1)}, u32[]{:S(2)}, u32[]{:S(2)}) collective-permute-start(bf16[17,16,128]{2,1,0:T(8,128)(2,1)S(1)} %get-tuple-element.43), channel_id=1, source_target_pairs={{0,3},{1,2},{2,1},{3,0},{4,7},{5,6},{6,5},{7,4},{8,11},{9,10},{10,... | collective-permute-start | bytes 208904 | tf_op jit(solution)/shard_map/ppermute | solution.py:463
